TPU v7x, 32 devices: a whole 2x2x4 slice. The times are simulated.
32 devices in a mesh: dp: 16 (over z, y, x), mp: 2 (over core).
Axes of the slice: x: 2, y: 2, z: 4, core: 2. Of those that a mesh axis runs over, the one named last changes fastest.
Arguments:
- tokens: bfloat16 [2, 16, 1024, 768], P(None, 'dp', 'mp'), may hold values from -6 to 6
- segment: int32 [2, 16, 1024], P(None, 'dp'), may hold values from 0 to 7, never falling along the last dimension, each value on 1 to 768 neighbouring positions
- ln1_gain: float32 [768], replicated, may hold values from 0.25 to 1.75
- ln1_bias: float32 [768], replicated, may hold values from -3 to 3
- w_qkv: bfloat16 [768, 3, 768], P('dp', None, 'mp'), may hold values from -0.21875 to 0.21875
- w_out: bfloat16 [768, 768], P('mp', 'dp'), may hold values from -1.25 to 1.25
- ln2_gain: float32 [768], replicated, may hold values from 0.25 to 1.75
- ln2_bias: float32 [768], replicated, may hold values from -3 to 3
- w_up: bfloat16 [768, 3072], P('dp', 'mp'), may hold values from -0.21875 to 0.21875
- w_down: bfloat16 [3072, 768], P('mp', 'dp'), may hold values from -0.109375 to 0.109375
- cotangent: bfloat16 [2, 16, 1024, 768], P(None, 'dp', 'mp'), may hold values from -6 to 6
Outputs:
- mixed: bfloat16 [2, 16, 1024, 768], P(None, 'dp', 'mp')
- grad_tokens: float32 [2, 16, 1024, 768], P(None, 'dp', 'mp')
- grad_ln1_gain: float32 [768], replicated
- grad_ln1_bias: float32 [768], replicated
- grad_w_qkv: float32 [768, 3, 768], P('dp', None, 'mp')
- grad_w_out: float32 [768, 768], P('mp', 'dp')
- grad_ln2_gain: float32 [768], replicated
- grad_ln2_bias: float32 [768], replicated
- grad_w_up: float32 [768, 3072], P('dp', 'mp')
- grad_w_down: float32 [3072, 768], P('mp', 'dp')
Inputs may be any that keep to these rules, and one draw needn't show every extreme that they name: `segment`: episode numbers never fall along a sequence; an episode has 1 to 768 positions, and one episode of each sequence has exactly 768.
All inputs are finite; a program needn't handle non-finite values.
Results may differ from a plain program's by a relative error of at most 0.014.
Values may be sent and summed in bfloat16 or wider, within the bound.
No kernel may reach another device: no remote copies, remote signals or barrier semaphores. Data moves between devices by JAX's collectives and lax.ppermute only.
A program may use at most 384 MiB of HBM per device.

v0:
```python
import functools
import math

import jax
import jax.numpy as jnp
from jax import lax
from jax.experimental import pallas as pl
from jax.experimental.pallas import tpu as pltpu
from jax.sharding import PartitionSpec as P

HD = 32
QB = 256
EPS = 1e-05
BF = jnp.bfloat16
F32 = jnp.float32
NEG = -1e30
SCALE = 1.0 / math.sqrt(HD)
LOG2E = math.log2(math.e)
C2 = SCALE * LOG2E
MIB = 1024 * 1024
SDS = jax.ShapeDtypeStruct


def nn(a, b):
    return lax.dot_general(a, b, (((1,), (0,)), ((), ())), preferred_element_type=F32)


def nt(a, b):
    return lax.dot_general(a, b, (((1,), (1,)), ((), ())), preferred_element_type=F32)


def params(mib):
    return pltpu.CompilerParams(vmem_limit_bytes=mib * MIB)


def in_hbm(values):
    return [pltpu.with_memory_space_constraint(v, pltpu.HBM) for v in values]


def in_vmem(values):
    return [pltpu.with_memory_space_constraint(v, pltpu.VMEM) for v in values]


def cost(gflop, mbytes):
    return pl.CostEstimate(flops=int(gflop * 1e9), bytes_accessed=int(mbytes * 1e6), transcendentals=0)


def any_spec():
    return pl.BlockSpec(memory_space=pl.ANY)


def smem_spec():
    return pl.BlockSpec(memory_space=pltpu.SMEM)


def vmem_spec():
    return pl.BlockSpec(memory_space=pltpu.VMEM)


def row_spec(width, rows=512):
    return pl.BlockSpec((rows, width), lambda r: (r, 0))


def column_spec(height, rows=512):
    return pl.BlockSpec((height, rows), lambda r: (0, r))


def whole_spec(shape):
    return pl.BlockSpec(shape, lambda r: tuple(0 for _ in shape))


MASKS = (0, 1, 2, 3)


class Rows:
    def __init__(self, dp_count, depth):
        self.dp_count = dp_count
        self.depth = depth
        self.split = (depth // dp_count) % 16 == 0 and dp_count == 16
        self.near = 4 if self.split else 1
        self.far = dp_count // 4 if self.split else 1
        self.block = depth // (self.near * self.far)
        self.shape = (self.far, self.near, self.block)


class Piece:
    def __init__(self, rows, kind, start=0, width=0, masks=MASKS):
        self.rows = rows
        self.masks = masks
        self.kind = kind if rows.split else "whole"
        self.start = start
        self.count = 2 * len(MASKS) if self.kind == "slabs" else 2
        if self.kind == "stack":
            self.shape = (len(MASKS), rows.far, rows.block, width)
        else:
            self.shape = rows.shape + (width,)


def piece_copies(piece, me, refs, moves, sem, outward):
    copies = []
    each = piece.count // 2
    for half, column, width, view in moves:
        cols = pl.ds(piece.start + column, width)
        if piece.kind == "whole":
            pairs = [(refs[half].at[:, :, :, cols], view)]
        else:
            pairs = []
            for k, mask in enumerate(piece.masks):
                ref = refs[half].at[k] if piece.kind == "stack" else refs[half * each + k]
                near = lax.bitwise_xor(lax.rem(me, 4), mask)
                pairs.append((ref.at[:, :, cols], view.at[:, near]))
        for outside, inside in pairs:
            if outward:
                copies.append(pltpu.make_async_copy(inside, outside, sem))
            else:
                copies.append(pltpu.make_async_copy(outside, inside, sem))
    return copies


def start_all(copies):
    for copy in copies:
        copy.start()


def wait_bytes(ref, sem):
    pltpu.make_async_copy(ref, ref, sem).wait()


def flat(value):
    return value.reshape(-1, value.shape[-1])


def head_row(h):
    return lax.broadcasted_iota(jnp.int32, (1, 128), 1) // HD == h


def fill_bias(bias, seg_col, seg_row):
    key = lax.broadcasted_iota(jnp.int32, (QB, QB), 0)
    query = lax.broadcasted_iota(jnp.int32, (QB, QB), 1)
    bias[0] = jnp.where(query >= key, 0.0, NEG)
    bias[1] = jnp.where((query >= key) & (seg_col[...] == seg_row[...]), 0.0, NEG)


def fill_double(double, halves):
    here = halves[0].shape[0]
    for k in range(4):
        double[k * here : (k + 1) * here, :] = halves[k % 2][...]


def turned(doubles, start, r):
    coarse = pl.multiple_of(start // 16 * 16 + r * QB, 16)
    fine = start % 16
    row = lax.broadcasted_iota(jnp.int32, (QB, QB + 16), 0)
    col = lax.broadcasted_iota(jnp.int32, (QB, QB + 16), 1)
    pick = jnp.where(col - row == fine, 1.0, 0.0).astype(BF)
    total = None
    for double in doubles:
        part = nn(pick, double[pl.ds(coarse, QB + 16), :])
        total = part if total is None else total + part
    return total


def norm_parts(values):
    centered = values - jnp.mean(values, axis=-1, keepdims=True)
    spread = jnp.mean(centered * centered, axis=-1, keepdims=True)
    root = lax.rsqrt(spread + EPS)
    return centered * root, root


def prepare_body(
    start,
    own,
    other,
    cot_own,
    cot_other,
    gain,
    offset,
    x_out,
    normed,
    normed_t_out,
    cot,
    cot_t,
    double,
    x,
    normed_t,
    sems,
):
    fill_double(double, [own, other])

    def step(r, carry):
        at = pl.ds(pl.multiple_of(r * QB, QB), QB)
        value = turned([double], start[0], r)
        x[at, :] = value.astype(BF)
        hat, _ = norm_parts(value)
        low = (hat * gain[...] + offset[...]).astype(BF)
        normed[at, :] = low
        normed_t[:, at] = low.T
        return carry

    count = x.shape[0] // QB
    lax.fori_loop(0, count, step, 0)
    copies = [
        pltpu.make_async_copy(x, x_out, sems.at[0]),
        pltpu.make_async_copy(normed_t, normed_t_out, sems.at[1]),
    ]
    start_all(copies)
    fill_double(double, [cot_own, cot_other])

    def second(r, carry):
        at = pl.ds(pl.multiple_of(r * QB, QB), QB)
        low = turned([double], start[0], r).astype(BF)
        cot[at, :] = low
        cot_t[:, at] = low.T
        return carry

    lax.fori_loop(0, count, second, 0)
    for copy in copies:
        copy.wait()


def prepare(start, own, other, cot_own, cot_other, gain, offset):
    here, depth = own.shape
    shape, shape_t = (2 * here, depth), (depth, 2 * here)
    return pl.pallas_call(
        prepare_body,
        in_specs=[smem_spec()] + [vmem_spec()] * 6,
        out_specs=[any_spec(), vmem_spec(), any_spec(), vmem_spec(), vmem_spec()],
        out_shape=[
            pltpu.HBM(shape, BF),
            pltpu.VMEM(shape, BF),
            pltpu.HBM(shape_t, BF),
            pltpu.VMEM(shape, BF),
            pltpu.VMEM(shape_t, BF),
        ],
        scratch_shapes=[
            pltpu.VMEM((4 * here, depth), BF),
            pltpu.VMEM(shape, BF),
            pltpu.VMEM(shape_t, BF),
            pltpu.SemaphoreType.DMA((2,)),
        ],
        compiler_params=params(20),
        cost_estimate=cost(4, 8),
        name="prepare",
    )(start, own, other, cot_own, cot_other, gain, offset)


def turn_back_body(start, core, values, held, other, double, own, sem):
    here = other.shape[0]
    double[: 2 * here, :] = values[...]
    double[2 * here :, :] = values[...]
    count = here // QB

    def step(r, carry):
        at = pl.ds(pl.multiple_of(r * QB, QB), QB)
        own[at, :] = turned([double], start[0], r).astype(BF)
        other[at, :] = turned([double], start[0], r + count).astype(BF)
        return carry

    lax.fori_loop(0, count, step, 0)
    copy = pltpu.make_async_copy(own, held.at[core[0]], sem)
    copy.start()
    copy.wait()


def turn_back(start, core, values):
    length, depth = values.shape
    half = (length // 2, depth)
    return pl.pallas_call(
        turn_back_body,
        in_specs=[smem_spec()] * 2 + [vmem_spec()],
        out_specs=[any_spec(), vmem_spec()],
        out_shape=[pltpu.HBM((2,) + half, BF), SDS(half, BF)],
        scratch_shapes=[
            pltpu.VMEM((2 * length, depth), BF),
            pltpu.VMEM(half, BF),
            pltpu.SemaphoreType.DMA,
        ],
        compiler_params=params(16),
        cost_estimate=cost(2, 4),
        name="turn_back",
    )(start, core, values)


def arrange_body(widths, me, *refs):
    pieces, outs = refs[:4], refs[4:]
    far = me[0] // 4
    for m, piece in enumerate(pieces):
        begin = 0
        for out, width in zip(outs, widths):
            out[lax.bitwise_xor(far, m)] = piece[:, begin : begin + width]
            begin += width


def arrange(rows, me, pieces, widths):
    return pl.pallas_call(
        functools.partial(arrange_body, widths),
        in_specs=[smem_spec()] + [vmem_spec()] * 4,
        out_specs=[vmem_spec()] * len(widths),
        out_shape=[SDS((rows.far, rows.block, w), BF) for w in widths],
        compiler_params=params(8),
        cost_estimate=cost(1, 1),
        name="arrange",
    )(me, *pieces)


def project_attend_body(piece, me, normed, seg_col, seg_row, *refs):
    slabs = refs[: piece.count]
    proj_out, att, lse, weight, proj, bias, keys_m, values_t, att_t, sem, out_sem = refs[piece.count :]
    moves = [(half, 0, 384, weight.at[:, :, :, pl.ds(384 * half, 384)]) for half in range(2)]
    start_all(piece_copies(piece, me[0], slabs, moves, sem, False))
    fill_bias(bias, seg_col, seg_row)
    values_t[...] = jnp.ones_like(values_t)
    wait_bytes(weight, sem)
    length = normed.shape[0]

    def project(r, carry):
        at = pl.ds(pl.multiple_of(r * 512, 512), 512)
        proj[at, :] = nn(normed[at, :], flat(weight[...])).astype(BF)
        return carry

    lax.fori_loop(0, length // 512, project, 0)
    proj_copy = pltpu.make_async_copy(proj, proj_out, out_sem)
    proj_copy.start()
    for half in range(2):
        flipped = proj[:, half * 384 + 256 : half * 384 + 384].T
        for h in range(4):
            values_t[half * 4 + h, 0:HD, :] = flipped[h * HD : (h + 1) * HD]

    units = [(h, i) for i in (2, 1, 0, 3) for h in range(4)]

    def step(half, carry):
        col = pl.multiple_of(half * 384, 128)
        for h in range(4):
            keys_m[h] = jnp.where(head_row(h), proj[:, pl.ds(col + 128, 128)], 0)

        def score(h, i):
            first = 768 if i == 3 else 0
            scores = nt(keys_m[h, first : (i + 1) * QB, :], proj[i * QB : (i + 1) * QB, pl.ds(col, 128)])
            edge = scores[-QB:] + bias[1 if i == 3 else 0]
            return jnp.concatenate([scores[:-QB], edge], 0) if scores.shape[0] > QB else edge

        ahead = score(*units[0])
        for k, (h, i) in enumerate(units):
            scores = ahead
            if k + 1 < len(units):
                ahead = score(*units[k + 1])
            first = 768 if i == 3 else 0
            last = (i + 1) * QB
            at = slice(i * QB, last)
            peak = jnp.max(scores, axis=0, keepdims=True) * C2
            probs = jnp.exp2(scores * C2 - peak).astype(BF)
            summed = nn(values_t[half * 4 + h, :, first:last], probs)
            total = summed[HD : HD + 1]
            att_t[pl.ds(pl.multiple_of(half * 128 + h * HD, HD), HD), at] = summed[:HD] / total
            lse[pl.ds(half * 4 + h, 1), at] = peak + jnp.log2(total)
        return carry

    lax.fori_loop(0, 2, step, 0)
    for half in range(2):
        cols = slice(half * 128, half * 128 + 128)
        att[:, cols] = att_t[cols, :].T.astype(BF)
    proj_copy.wait()


def project_attend(piece, me, normed, seg_col, seg_row, slabs):
    length, depth = normed.shape
    rows = piece.rows
    return pl.pallas_call(
        functools.partial(project_attend_body, piece),
        in_specs=[smem_spec()] + [vmem_spec()] * 3 + [any_spec()] * len(slabs),
        out_specs=[any_spec()] + [vmem_spec()] * 2,
        out_shape=[
            pltpu.HBM((length, 768), BF),
            pltpu.HBM((length, 256), BF),
            pltpu.HBM((8, length), F32),
        ],
        scratch_shapes=[
            pltpu.VMEM(rows.shape + (768,), BF),
            pltpu.VMEM((length, 768), BF),
            pltpu.VMEM((2, QB, QB), F32),
            pltpu.VMEM((4, length, 128), BF),
            pltpu.VMEM((8, HD + 16, length), BF),
            pltpu.VMEM((256, length), F32),
            pltpu.SemaphoreType.DMA,
            pltpu.SemaphoreType.DMA,
        ],
        compiler_params=params(20),
        cost_estimate=cost(8, 8),
        name="project_attend",
    )(me, *in_vmem([normed]), seg_col, seg_row, *in_hbm(slabs))


def join_heads(attended):
    return jnp.concatenate([a[:, :128] for a in attended] + [a[:, 128:] for a in attended], 1)


def out_norm_body(piece, groups, me, tokens, gain, offset, *refs):
    attended = refs[:groups]
    slabs = refs[groups : groups + piece.count]
    middle, normed, normed_t, weight, sem = refs[groups + piece.count :]
    width = weight.shape[3] // 2

    @pl.when(pl.program_id(0) == 0)
    def _():
        moves = [(half, 0, width, weight.at[:, :, :, pl.ds(width * half, width)]) for half in range(2)]
        start_all(piece_copies(piece, me[0], slabs, moves, sem, False))
        wait_bytes(weight, sem)

    value = tokens[...].astype(F32) + nt(join_heads([a[...] for a in attended]), flat(weight[...]))
    middle[...] = value
    hat, _ = norm_parts(value)
    low = (hat * gain[...] + offset[...]).astype(BF)
    normed[...] = low
    normed_t[...] = low.T


def out_norm(piece, me, tokens, gain, offset, attended, slabs):
    length, depth = tokens.shape
    return pl.pallas_call(
        functools.partial(out_norm_body, piece, len(attended)),
        grid=(length // 512,),
        in_specs=[smem_spec(), row_spec(depth), whole_spec((1, depth)), whole_spec((1, depth))]
        + [row_spec(256)] * len(attended)
        + [any_spec()] * len(slabs),
        out_specs=[row_spec(depth)] * 2 + [column_spec(depth)],
        out_shape=[
            pltpu.HBM((length, depth), F32),
            pltpu.VMEM((length, depth), BF),
            pltpu.VMEM((depth, length), BF),
        ],
        scratch_shapes=[pltpu.VMEM(piece.rows.shape + (depth,), BF), pltpu.SemaphoreType.DMA],
        compiler_params=params(28),
        cost_estimate=cost(3, 8),
        name="out_norm",
    )(me, *in_hbm([tokens]), gain, offset, *in_hbm(attended), *in_hbm(slabs))


def gelu_parts(values):
    size = jnp.abs(values)
    density = jnp.exp2(values * values * (-0.5 * LOG2E) + math.log2(1.0 / math.sqrt(2 * math.pi)))
    t = 1.0 / (1.0 + 0.2316419 * size)
    poly = t * (
        0.319381530
        + t * (-0.356563782 + t * (1.781477937 + t * (-1.821255978 + t * 1.330274429)))
    )
    tail = density * poly
    below = jnp.where(values >= 0, 1.0 - tail, tail)
    return values * below, below + values * density


def feed_forward_body(piece, out_piece, first, final, aliased, me, normed, normed_t, cot, cot_t, *refs):
    refs = list(refs)
    held = [] if first else [refs.pop(0), refs.pop(0)]
    middle = refs.pop(0) if final else None
    slabs, refs = refs[: piece.count], refs[piece.count + aliased :]
    mixed, grad_in = refs[:2]
    outs, refs = refs[2:4], refs[4:]
    weight, staged, act, grad_hidden, mixed_acc, grad_acc, sems = refs[:7]
    mixed_low, middle_here = refs[7:] if final else (None, None)
    length, depth = normed.shape
    moves = []
    for half in range(2):
        for which in range(2):
            at = pl.ds(which * 768 + half * 384, 384)
            moves.append((half, which * 384, 384, at))
    into = [(h, c, w, weight.at[:, :, :, at]) for h, c, w, at in moves]
    outof = [(h, c, w, staged.at[:, :, :, at]) for h, c, w, at in moves]
    start_all(piece_copies(piece, me[0], slabs, into, sems.at[0], False))
    held_copies = []
    if not first:
        held_copies.append(pltpu.make_async_copy(held[0], mixed_acc, sems.at[1]))
        held_copies.append(pltpu.make_async_copy(held[1], grad_acc, sems.at[2]))
    if final:
        held_copies.append(pltpu.make_async_copy(middle, middle_here, sems.at[4]))
    start_all(held_copies)
    wait_bytes(weight, sems.at[0])
    chunks = [slice(c * 256, c * 256 + 256) for c in range(3)]

    def products(c):
        hidden = nn(normed[...], flat(weight[:, :, :, c * 256 : c * 256 + 256]))
        return hidden, nn(cot[...], flat(weight[:, :, :, 768 + c * 256 : 1024 + c * 256]))

    ahead = products(0)
    for c in range(3):
        hidden, grad_act = ahead
        if c < 2:
            ahead = products(c + 1)
        value, slope = gelu_parts(hidden)
        act[:, chunks[c]] = value.astype(BF)
        grad_hidden[:, chunks[c]] = (grad_act * slope).astype(BF)
    for copy in held_copies:
        copy.wait()
    for cols in chunks:
        mixed_part = nt(act[...], flat(weight[:, :, :, 768:1536])[cols])
        grad_part = nt(grad_hidden[...], flat(weight[:, :, :, 0:768])[cols])
        if not first:
            mixed_part = mixed_part + mixed_acc[:, cols]
            grad_part = grad_part + grad_acc[:, cols]
        if final:
            mixed_low[:, cols] = (middle_here[:, cols] + mixed_part).astype(BF)
        else:
            mixed_acc[:, cols] = mixed_part
        grad_acc[:, cols] = grad_part
    out_copies = [
        pltpu.make_async_copy(mixed_low if final else mixed_acc, mixed, sems.at[1]),
        pltpu.make_async_copy(grad_acc, grad_in, sems.at[2]),
    ]
    start_all(out_copies)
    for c in range(3):
        cols = slice(c * 256, c * 256 + 256)
        up = nn(normed_t[...], grad_hidden[:, cols]).astype(BF)
        staged[:, :, :, cols] = up.reshape(staged.shape[:3] + (256,))
        down = nn(cot_t[...], act[:, cols]).astype(BF)
        staged[:, :, :, 768 + c * 256 : 1024 + c * 256] = down.reshape(staged.shape[:3] + (256,))
    start_all(piece_copies(out_piece, me[0], outs, outof, sems.at[3], True))
    for copy in out_copies:
        copy.wait()
    wait_bytes(staged, sems.at[3])


def feed_forward(piece, out_piece, me, normed, normed_t, cot, cot_t, held, middle, slabs, onto):
    length, depth = normed.shape
    rows = piece.rows
    first, final = held is None, middle is not None
    ins = [me] + in_vmem([normed, normed_t, cot, cot_t]) + ([] if first else in_hbm(held))
    specs = [smem_spec()] + [vmem_spec()] * 4 + [any_spec()] * (0 if first else 2)
    if final:
        ins += in_hbm([middle])
        specs.append(any_spec())
    scratch = [
        pltpu.VMEM(rows.shape + (1536,), BF),
        pltpu.VMEM(rows.shape + (1536,), BF),
        pltpu.VMEM((length, 768), BF),
        pltpu.VMEM((length, 768), BF),
        pltpu.VMEM((length, depth), F32),
        pltpu.VMEM((length, depth), F32),
        pltpu.SemaphoreType.DMA((5,)),
    ]
    if final:
        scratch += [pltpu.VMEM((length, depth), BF), pltpu.VMEM((length, depth), F32)]
    got = pl.pallas_call(
        functools.partial(feed_forward_body, piece, out_piece, first, final, len(onto)),
        in_specs=specs + [any_spec()] * (piece.count + len(onto)),
        out_specs=[any_spec()] * 4,
        out_shape=[pltpu.HBM((length, depth), BF if final else F32), pltpu.HBM((length, depth), F32)]
        + [pltpu.HBM(out_piece.shape, BF)] * 2,
        input_output_aliases={len(ins) + piece.count + k: 2 + k for k in range(len(onto))},
        scratch_shapes=scratch,
        compiler_params=params(40),
        cost_estimate=cost(11, 20),
        name="feed_forward",
    )(*ins, *in_hbm(slabs), *in_hbm(onto))
    return got[0], got[1], got[2:]


def norm_pull(grad, hat, root, gain):
    scaled = grad * gain
    first = jnp.mean(scaled, axis=-1, keepdims=True)
    second = jnp.mean(scaled * hat, axis=-1, keepdims=True)
    return root * (scaled - first - hat * second)


def add_sums(sums, grad, hat):
    @pl.when(pl.program_id(0) == 0)
    def _():
        sums[...] = jnp.zeros_like(sums)

    sums[0:1, :] += jnp.sum(grad * hat, axis=0, keepdims=True)
    sums[1:2, :] += jnp.sum(grad, axis=0, keepdims=True)


def out_back_body(piece, groups, me, middle, grad_in, cot, gain, *refs):
    slabs, refs = refs[: piece.count], refs[piece.count :]
    grad_middle, branch_t, sums = refs[:3]
    grad_att = refs[3 : 3 + groups]
    weight, sem = refs[3 + groups :]
    width = weight.shape[3] // 2

    @pl.when(pl.program_id(0) == 0)
    def _():
        moves = [(half, 0, width, weight.at[:, :, :, pl.ds(width * half, width)]) for half in range(2)]
        start_all(piece_copies(piece, me[0], slabs, moves, sem, False))
        wait_bytes(weight, sem)

    hat, root = norm_parts(middle[...])
    grad = grad_in[...]
    value = cot[...].astype(F32) + norm_pull(grad, hat, root, gain[...])
    grad_middle[...] = value
    low = value.astype(BF)
    branch_t[...] = low.T
    add_sums(sums, grad, hat)
    back = nn(low, flat(weight[...])).astype(BF)
    for g in range(groups):
        grad_att[g][:, 0:128] = back[:, g * 128 : g * 128 + 128]
        grad_att[g][:, 128:256] = back[:, width + g * 128 : width + g * 128 + 128]


def out_back(piece, groups, me, middle, grad_in, cot, gain, slabs):
    length, depth = middle.shape
    got = pl.pallas_call(
        functools.partial(out_back_body, piece, groups),
        grid=(length // 512,),
        in_specs=[smem_spec()] + [row_spec(depth)] * 3 + [whole_spec((1, depth))] + [any_spec()] * len(slabs),
        out_specs=[row_spec(depth), column_spec(depth), whole_spec((8, depth))] + [row_spec(256)] * groups,
        out_shape=[pltpu.HBM((length, depth), F32), pltpu.VMEM((depth, length), BF), SDS((8, depth), F32)]
        + [pltpu.HBM((length, 256), BF)] * groups,
        scratch_shapes=[pltpu.VMEM(piece.rows.shape + (depth,), BF), pltpu.SemaphoreType.DMA],
        compiler_params=params(28),
        cost_estimate=cost(4, 16),
        name="out_back",
    )(me, *in_hbm([middle, grad_in]), *in_vmem([cot]), gain, *in_hbm(slabs))
    return got[0], got[1], got[2], got[3:]


def attend_back_body(piece, out_piece, extra, aliased, final, me, normed_t_in, proj, att, grad_att, lse, seg_col, seg_row, *refs):
    refs = list(refs)
    slabs, refs = refs[: piece.count], refs[piece.count :]
    if extra:
        branch_t = refs.pop(0)
        attended, refs = refs[:extra], refs[extra:]
    else:
        held = refs.pop(0)
    if final:
        tokens_in = refs.pop(0)
    refs = refs[aliased:]
    grad_normed, outs, refs = refs[0], refs[1:3], refs[3:]
    if final:
        sums = refs.pop(0)
    grad_proj, key_sum, value_sum = refs[:3]
    refs = refs[3:]
    bias, delta, keys_t, query_t, query_m, grad_m, staged, normed_t, total, weight, sems = refs[:11]
    copies = [pltpu.make_async_copy(normed_t_in, normed_t, sems.at[1])]
    if not extra:
        copies.append(pltpu.make_async_copy(held, total, sems.at[2]))
    if final:
        copies.append(pltpu.make_async_copy(tokens_in, refs[11], sems.at[3]))
    moves = [(half, 0, 384, weight.at[:, :, :, pl.ds(384 * half, 384)]) for half in range(2)]
    start_all(copies + piece_copies(piece, me[0], slabs, moves, sems.at[4], False))
    length = proj.shape[0]
    fill_bias(bias, seg_col, seg_row)
    if extra:
        joined = join_heads([a[...] for a in attended])
        out_grad = nn(branch_t[...], joined).astype(BF)
        staged[:, :, :, 768:] = out_grad.reshape(staged.shape[:3] + (768,))
    for half in range(2):
        cols = slice(half * 128, half * 128 + 128)
        product = (grad_att[:, cols].astype(F32) * att[:, cols].astype(F32)).T
        for h in range(4):
            delta[half * 4 + h : half * 4 + h + 1, :] = jnp.sum(
                product[h * HD : (h + 1) * HD], axis=0, keepdims=True
            )
        keys_t[cols, :] = proj[:, half * 384 + 128 : half * 384 + 256].T

    def step(half, carry):
        col = pl.multiple_of(half * 384, 128)
        out = pl.multiple_of(half * 128, 128)
        for h in range(4):
            mine = head_row(h)
            query_m[h] = jnp.where(mine, proj[:, pl.ds(col, 128)], 0)
            grad_m[h] = jnp.where(mine, grad_att[:, pl.ds(out, 128)], 0)
        key_sum[...] = jnp.zeros_like(key_sum)
        value_sum[...] = jnp.zeros_like(value_sum)
        for i in (2, 1, 0, 3):
            first = 768 if i == 3 else 0
            last = (i + 1) * QB
            here = slice(first, last)
            there = slice(i * QB, last)
            keys = proj[here, pl.ds(col + 128, 128)]
            values = proj[here, pl.ds(col + 256, 128)]

            def products(h):
                scores = nt(keys, query_m[h, there, :])
                edge = scores[-QB:] + bias[1 if i == 3 else 0]
                if last - first > QB:
                    scores = jnp.concatenate([scores[:-QB], edge], 0)
                else:
                    scores = edge
                return scores, nt(values, grad_m[h, there, :])

            all_probs, all_grads = [], []
            ahead = products(0)
            for h in range(4):
                scores, grad_probs = ahead
                if h < 3:
                    ahead = products(h + 1)
                stat = pl.ds(half * 4 + h, 1)
                lanes = pl.ds(pl.multiple_of(half * 128 + h * HD, HD), HD)
                probs = jnp.exp2(scores * C2 - lse[stat, there])
                grad_scores = (probs * (grad_probs - delta[stat, there])).astype(BF)
                all_probs.append(probs.astype(BF))
                all_grads.append(grad_scores)
                query_t[lanes, there] = nn(keys_t[lanes, here], grad_scores)
            stacked = jnp.concatenate([grad_m[h, there, :] for h in range(4)], 0)
            value_sum[here, :] += nn(jnp.concatenate(all_probs, 1), stacked)
            stacked = jnp.concatenate([query_m[h, there, :] for h in range(4)], 0)
            key_sum[here, :] += nn(jnp.concatenate(all_grads, 1), stacked)
        grad_proj[:, pl.ds(col + 128, 128)] = (key_sum[...] * SCALE).astype(BF)
        grad_proj[:, pl.ds(col + 256, 128)] = value_sum[...].astype(BF)
        return carry

    lax.fori_loop(0, 2, step, 0)
    for half in range(2):
        grad_proj[:, half * 384 : half * 384 + 128] = (
            query_t[half * 128 : half * 128 + 128, :].T * SCALE
        ).astype(BF)
    for copy in copies:
        copy.wait()
    wait_bytes(weight, sems.at[4])
    for c in range(3):
        cols = slice(c * 256, c * 256 + 256)
        part = nn(normed_t[...], grad_proj[:, cols]).astype(BF)
        staged[:, :, :, cols] = part.reshape(staged.shape[:3] + (256,))
    moves = [(half, 0, 384, staged.at[:, :, :, pl.ds(384 * half, 384)]) for half in range(2)]
    if extra:
        moves += [
            (half, -384, 384, staged.at[:, :, :, pl.ds(768 + 384 * half, 384)]) for half in range(2)
        ]
    start_all(piece_copies(out_piece, me[0], outs, moves, sems.at[0], True))
    if final:
        sums[...] = jnp.zeros_like(sums)

    total_copies = []
    for c in range(3):
        cols = slice(c * 256, c * 256 + 256)
        value = nt(grad_proj[...], flat(weight[...])[cols])
        if not extra:
            value = value + total[:, cols]
        total[:, cols] = value
        total_copies.append(
            pltpu.make_async_copy(
                total.at[:, pl.ds(c * 256, 256)], grad_normed.at[:, pl.ds(c * 256, 256)], sems.at[2]
            )
        )
        total_copies[-1].start()
    if final:

        def sum_step(r, carry):
            at = pl.ds(pl.multiple_of(r * QB, QB), QB)
            value = total[at, :]
            hat, _ = norm_parts(refs[11][at, :].astype(F32))
            sums[0:1, :] += jnp.sum(value * hat, axis=0, keepdims=True)
            sums[1:2, :] += jnp.sum(value, axis=0, keepdims=True)
            return carry

        lax.fori_loop(0, length // QB, sum_step, 0)
    wait_bytes(staged, sems.at[0])
    wait_bytes(total, sems.at[2])


def attend_back(
    piece,
    out_piece,
    me,
    normed_t,
    proj,
    att,
    grad_att,
    lse,
    seg_col,
    seg_row,
    slabs,
    branch_t,
    attended,
    held,
    tokens,
    onto,
):
    depth, length = normed_t.shape
    extra = len(attended)
    final = tokens is not None
    columns = 1536 if extra else 768
    ins = [me] + in_hbm([normed_t, proj, att, grad_att, lse]) + [seg_col, seg_row] + in_hbm(slabs)
    specs = [smem_spec(), any_spec()] + [vmem_spec()] * 6 + [any_spec()] * len(slabs)
    if extra:
        ins += in_vmem([branch_t]) + in_hbm(attended)
        specs += [vmem_spec()] * (1 + extra)
    else:
        ins += in_hbm([held])
        specs += [any_spec()]
    if final:
        ins += in_hbm([tokens])
        specs += [any_spec()]
    outs = [pltpu.HBM((length, depth), F32)] + [pltpu.HBM(out_piece.shape, BF)] * 2
    scratch = [
        pltpu.VMEM((2, QB, QB), F32),
        pltpu.VMEM((8, length), F32),
        pltpu.VMEM((256, length), BF),
        pltpu.VMEM((256, length), F32),
        pltpu.VMEM((4, length, 128), BF),
        pltpu.VMEM((4, length, 128), BF),
        pltpu.VMEM(out_piece.rows.shape + (columns,), BF),
        pltpu.VMEM((depth, length), BF),
        pltpu.VMEM((length, depth), F32),
        pltpu.VMEM(piece.rows.shape + (768,), BF),
        pltpu.SemaphoreType.DMA((5,)),
    ]
    if final:
        outs.append(SDS((8, depth), F32))
        scratch.append(pltpu.VMEM((length, depth), BF))
    got = pl.pallas_call(
        functools.partial(attend_back_body, piece, out_piece, extra, len(onto), final),
        in_specs=specs + [any_spec()] * len(onto),
        out_specs=[any_spec()] * 3 + ([vmem_spec()] if final else []),
        out_shape=outs,
        input_output_aliases={len(ins) + k: 1 + k for k in range(len(onto))},
        scratch_shapes=[
            pltpu.VMEM((length, 768), BF),
            pltpu.VMEM((length, 128), F32),
            pltpu.VMEM((length, 128), F32),
        ]
        + scratch,
        compiler_params=params(40),
        cost_estimate=cost(12, 8),
        name="attend_back",
    )(*ins, *in_hbm(onto))
    return got[0], got[1:3], got[3] if final else None


def norm_back_body(
    start, core, tokens, grad_normed, grad_middle, gain, held, other, high, low, own, sem
):
    length = high.shape[0] // 2
    r = pl.program_id(0)
    hat, root = norm_parts(tokens[...].astype(F32))
    value = grad_middle[...] + norm_pull(grad_normed[...], hat, root, gain[...])
    top = value.astype(BF)
    rest = (value - top.astype(F32)).astype(BF)
    for base in (0, length):
        at = pl.ds(pl.multiple_of(base + r * QB, QB), QB)
        high[at, :] = top
        low[at, :] = rest

    @pl.when(r == pl.num_programs(0) - 1)
    def _():
        count = own.shape[0] // QB
        for k in range(count):
            own[k * QB : k * QB + QB, :] = turned([high, low], start[0], k)
        copy = pltpu.make_async_copy(own, held.at[core[0]], sem)
        copy.start()
        for k in range(count):
            other[k * QB : k * QB + QB, :] = turned([high, low], start[0], k + count)
        copy.wait()


def norm_back(start, core, tokens, grad_normed, grad_middle, gain):
    length, depth = tokens.shape
    half = (length // 2, depth)
    return pl.pallas_call(
        norm_back_body,
        grid=(length // QB,),
        in_specs=[smem_spec()] * 2 + [row_spec(depth, QB)] * 3 + [whole_spec((1, depth))],
        out_specs=[any_spec(), whole_spec(half)],
        out_shape=[pltpu.HBM((2,) + half, F32), SDS(half, F32)],
        scratch_shapes=[
            pltpu.VMEM((2 * length, depth), BF),
            pltpu.VMEM((2 * length, depth), BF),
            pltpu.VMEM(half, F32),
            pltpu.SemaphoreType.DMA,
        ],
        compiler_params=params(24),
        cost_estimate=cost(4, 16),
        name="norm_back",
    )(start, core, *in_hbm([tokens, grad_normed, grad_middle]), gain)


def split_far_body(counts, me, *refs):
    keep, send = refs[-2:]
    far = me[0] // 4
    begin = 0
    for count in counts:
        pieces, refs = refs[:count], refs[count:]
        cols = pl.ds(begin, pieces[0].shape[-1])
        begin += pieces[0].shape[-1]
        for k, out in enumerate((keep, send)):
            for slot in range(2):
                at = lax.bitwise_xor(far, k + 2 * slot)
                total = pieces[0][at].astype(F32)
                for piece in pieces[1:]:
                    total = total + piece[at].astype(F32)
                out[slot, :, cols] = total.astype(BF)


def split_far(me, groups):
    width, specs = 0, []
    for pieces in groups:
        far, block, columns = pieces[0].shape[-3:]
        width += columns
        for piece in pieces:
            if piece.ndim == 4:
                specs.append(pl.BlockSpec((None, far, block, columns), lambda i: (0, 0, 0, 0)))
            else:
                specs.append(whole_spec(piece.shape))
    return pl.pallas_call(
        functools.partial(split_far_body, [len(pieces) for pieces in groups]),
        grid=(1,),
        in_specs=[smem_spec()] + specs,
        out_specs=[whole_spec((2, block, width))] * 2,
        out_shape=[SDS((2, block, width), BF)] * 2,
        compiler_params=params(16),
        cost_estimate=cost(1, 2),
        name="split_far",
    )(me, *[piece for pieces in groups for piece in pieces])


def put_sums(ref, base, total):
    high = total.astype(BF)
    ref[base : base + 4, :] = high
    ref[base + 4 : base + 8, :] = (total - high.astype(F32)).astype(BF)
    ref[base + 8 : base + 16, :] = jnp.zeros((8, total.shape[1]), BF)


def get_sums(ref, base):
    return ref[base : base + 4, :].astype(F32) + ref[base + 4 : base + 8, :].astype(F32)


def last_join_body(own, other, sums, sums_away, *outs):
    total = sums[...] + sums_away[...]
    rows = outs[0].shape[0] - 16
    for k, out in enumerate(outs):
        value = own[k].astype(F32) + other[k].astype(F32)
        out[:rows, :] = value.astype(BF).reshape(rows, -1)
        put_sums(out, rows, total)


def last_split_body(me, m0, m1, m2, m3, keep, send):
    far = me[0] // 4
    rows = m0.shape[0] - 16
    block = rows // 4
    for k, out in enumerate((keep, send)):
        for slot in range(2):
            at = pl.ds(pl.multiple_of(lax.bitwise_xor(far, k + 2 * slot) * block, 16), block)
            total = (m0[at, :].astype(F32) + m1[at, :].astype(F32)) + (
                m2[at, :].astype(F32) + m3[at, :].astype(F32)
            )
            out[slot * block : (slot + 1) * block, :] = total.astype(BF)
    total = (get_sums(m0, rows) + get_sums(m1, rows)) + (get_sums(m2, rows) + get_sums(m3, rows))
    put_sums(keep, 2 * block, total)
    put_sums(send, 2 * block, total)


def last_middle_body(keep, near, rest, send):
    block = (keep.shape[0] - 16) // 2
    value = keep[:block, :].astype(F32) + near[:block, :].astype(F32)
    rest[:block, :] = value.astype(BF)
    value = keep[block : 2 * block, :].astype(F32) + near[block : 2 * block, :].astype(F32)
    send[:block, :] = value.astype(BF)
    total = get_sums(keep, 2 * block) + get_sums(near, 2 * block)
    put_sums(rest, block, total)
    put_sums(send, block, total)


def last_sum_body(rest, away, first, grad_qkv, sums):
    block = rest.shape[0] - 16
    value = rest[:block, :].astype(F32) + away[:block, :].astype(F32)
    parts = [first[:, 384:], value[:, :384], value[:, 384:]]
    for which in range(3):
        cols = slice(which * 128, which * 128 + 128)
        grad_qkv[which] = jnp.concatenate([part[:, cols] for part in parts], 1)
    sums[...] = get_sums(rest, block) + get_sums(away, block)


def pack_body(part, out, up, down, packed):
    width = out.shape[1]
    packed[:, :width] = out[...]
    for s in range(up.shape[1] // part):
        cols = slice(s * part, (s + 1) * part)
        packed[:, width + 2 * s * part : width + (2 * s + 1) * part] = up[:, cols]
        packed[:, width + (2 * s + 1) * part : width + (2 * s + 2) * part] = down[:, cols]


def small_call(body, name, outs, scalars, values):
    return pl.pallas_call(
        body,
        in_specs=[smem_spec()] * len(scalars) + [vmem_spec()] * len(values),
        out_specs=[vmem_spec()] * len(outs),
        out_shape=outs,
        compiler_params=params(16),
        cost_estimate=cost(1, 3),
        name=name,
    )(*scalars, *values)


def swap(value):
    return lax.ppermute(value, "mp", [(0, 1), (1, 0)])


def tie(*values):
    return lax.optimization_barrier(values)


def hop(value, mask, count):
    return lax.ppermute(value, "dp", [(i, i ^ mask) for i in range(count)])


def hops(value, masks, count):
    return [(value, functools.partial(hop, mask=m, count=count)) for m in masks]


def far_hops(rows, values):
    return [
        (v, functools.partial(hop, mask=rows.near * m, count=rows.dp_count))
        for m, v in zip(range(1, rows.far), values)
    ]


def swaps(values):
    return [(v, swap) for v in values]


def send_all(requests):
    return [send(value) for value, send in requests]


def low_sum(values):
    total = values[0].astype(F32)
    for value in values[1:]:
        total = total + value.astype(F32)
    return total


class Flow:
    def __init__(self, me):
        self.me = me
        self.active = []

    def add(self, transfer, name, results, seeds=()):
        self.active.append([transfer, list(seeds), name, results])

    def step(self, *pivots):
        values = [v for item in self.active for v in item[1]]
        tied = list(tie(self.me, *pivots, *values))
        self.me = tied.pop(0)
        pivots, tied = tied[: len(pivots)], tied[len(pivots) :]
        going, self.active, requests = self.active, [], []
        for item in going:
            transfer, values, name, results = item
            got, tied = tied[: len(values)], tied[len(values) :]
            try:
                if callable(transfer):
                    item[0] = transfer(*got)
                    asked = next(item[0])
                else:
                    asked = transfer.send(got)
                self.active.append(item)
                requests.append(asked)
            except StopIteration as stop:
                results[name] = stop.value
        tied = list(tie(self.me, *(operand for asked in requests for operand, _ in asked)))
        self.me = tied.pop(0)
        for item, asked in zip(self.active, requests):
            item[1] = [send(operand) for (_, send), operand in zip(asked, tied)]
            tied = tied[len(asked) :]
        return pivots


def add_low(a, b):
    return (a.astype(F32) + b.astype(F32)).astype(BF)


def on_device(
    tokens, segment, ln1_gain, ln1_bias, w_qkv, w_out, ln2_gain, ln2_bias, w_up, w_down, cotangent
):
    dp_count = lax.axis_size("dp")
    core = lax.axis_index("mp")
    me = lax.axis_index("dp").astype(jnp.int32).reshape(1)
    here, depth = tokens.shape[2], tokens.shape[3]
    length = 2 * here
    rows = Rows(dp_count, depth)

    groups = w_qkv.shape[2] // 128
    part = 384
    subs = w_up.shape[1] // part
    cut = subs // 2
    qkv = [w_qkv[:, :, g * 128 : (g + 1) * 128].reshape(-1, part) for g in range(groups)]
    shards = {"q": jnp.concatenate(qkv, 1)}

    shard_a = small_call(
        functools.partial(pack_body, part),
        "pack",
        [SDS((w_up.shape[0], w_out.shape[0] + 2 * w_up.shape[1]), BF)],
        [],
        [w_out.T, w_up, w_down.T],
    )[0]

    def halves(values):
        own = lax.dynamic_index_in_dim(values[:, 0], core, 0, keepdims=False)
        away = lax.dynamic_index_in_dim(values[:, 0], 1 - core, 0, keepdims=False)
        return own, swap(away)

    seg = lax.dynamic_index_in_dim(segment[:, 0], core, 0, keepdims=False)
    run = length * 3 // 4
    begin = jnp.argmax(seg[: length - run + 1] == seg[run - 1 :]).astype(jnp.int32)
    start = ((begin - here * core) % length).reshape(1)
    back = (length - start) % length
    seg_tail = lax.dynamic_slice_in_dim(jnp.concatenate([seg, seg]), begin + run, length - run)
    seg_col = seg_tail.reshape(-1, 1)
    seg_row = seg_tail.reshape(1, -1)
    gain1, bias1, gain2, bias2 = (
        v.reshape(1, -1) for v in (ln1_gain, ln1_bias, ln2_gain, ln2_bias)
    )

    flow = Flow(me)
    token_halves = halves(tokens)
    cot_halves = halves(cotangent)
    wide = 2 * part
    qkv_pieces = [Piece(rows, "slabs")] + [Piece(rows, "slabs", part * g) for g in range(groups - 1)]
    out_piece = Piece(rows, "slabs")
    feed_pieces = [Piece(rows, "slabs", part + wide * s) for s in range(cut)]
    feed_pieces += [Piece(rows, "slabs", wide * s) for s in range(subs - cut)]
    turns = [(0, 2, 1, 3), MASKS]
    feed_outs = [
        Piece(rows, "stack", wide * (s % cut), wide * cut, turns[s % cut]) for s in range(subs)
    ]
    qkv_outs = [Piece(rows, "stack", part, wide)]
    qkv_outs += [Piece(rows, "stack", part * g, part * (groups - 1)) for g in range(groups - 1)]
    far = lax.axis_index("dp") // rows.near

    def gather_whole(shard):
        return lax.all_gather(shard, "dp", axis=0, tiled=True).reshape(rows.shape + (-1,))

    def fetch_near(near):
        got = yield hops(near, MASKS[1:], dp_count)
        own = [near] + got
        return own + [swap(x) for x in own]

    def via(mask):
        return functools.partial(hop, mask=mask, count=dp_count)

    def fetch_wide(widths, shard, near, away):
        (both_ways,) = yield [(away, via(4))]
        a0, c0 = arrange(rows, flow.me, [shard, near, away, both_ways], widths)
        a1, a2, b0 = yield [(a0, via(1)), (a0, via(2))] + swaps([a0])
        a3, c1, b1, b2, d0 = yield [(a1, via(2)), (c0, via(1))] + swaps([a1, a2, c0])
        slabs["a"] = [a0, a1, a2, a3, b0, b1, b2, swap(a3)]
        c2, d1 = yield [(c0, via(2))] + swaps([c1])
        c3, d2 = yield [(c2, via(1))] + swaps([c2])
        return [c0, c1, c2, c3, d0, d1, d2, swap(c3)]

    def whole(shard):
        own = gather_whole(shard)
        return [own, swap(own)]

    def halve(own, other):
        (other,) = yield swaps([other])
        middle_col = own.shape[-1] // 2
        keep, send = [], []
        for cols in (slice(0, middle_col), slice(middle_col, None)):
            keep.append(low_sum([own[:2, ..., cols], other[:2, ..., cols]]).astype(BF))
            send.append(low_sum([own[2:, ..., cols], other[2:, ..., cols]]).astype(BF))
        near = yield [(v, via(m)) for v, m in zip(send, (1, 2))]
        send = [low_sum([k[1], n[1]]).astype(BF) for k, n in zip(keep, near)]
        away = yield [(v, via(m)) for v, m in zip(send, (2, 1))]
        return [list(group) for group in zip(keep, near, away)]

    def direct(mine):
        got = yield hops_of(mine, (1, 2, 3))
        return [mine[0]] + got

    def hops_of(values, masks):
        return [(values[m], via(m)) for m in masks]

    def reduce_far(groups):
        keep, send = split_far(flow.me, groups)
        (near,) = yield [(send, via(4))]
        (away,) = yield [(low_sum([keep[1], near[1]]).astype(BF), via(8))]
        return low_sum([keep[0], near[0], away])

    def reduce_all(own, other):
        groups_here = yield from halve(own, other)
        return (yield from reduce_far(sums_of["early"] + groups_here))

    def reduce_last(own, other, sums):
        other, sums_away = swap(other), swap(sums)
        mine = small_call(
            last_join_body,
            "last_join",
            [SDS((rows.far * rows.block + 16, wide), BF)] * 4,
            [],
            [own, other, sums, sums_away],
        )
        return (yield from direct(mine))

    def exchange(value):
        (got,) = yield swaps([value])
        return got

    def reduce_direct(own, other):
        (other,) = yield swaps([other])
        mine = [low_sum([own[k], other[k]]).astype(BF) for k in range(4)]
        pieces = yield from direct(mine)
        return (yield from reduce_far([pieces]))

    def plain(own, other):
        value = low_sum([own, swap(other)]).astype(BF).reshape(depth, -1)
        return lax.psum_scatter(value, "dp", scatter_dimension=0, tiled=True).astype(F32)

    def run(transfer):
        requests = next(transfer)
        while True:
            try:
                requests = transfer.send(send_all(requests))
            except StopIteration as stop:
                return stop.value

    slabs, forward = {}, []

    def project(g):
        name = "q0" if g == 0 else "q1"
        forward.append(
            project_attend(qkv_pieces[g], flow.me, normed, seg_col, seg_row, slabs[name])
        )

    if rows.split:
        tied = tie(shards["q"], *token_halves, *cot_halves)
        shard_q, token_halves, cot_halves = tied[0], tied[1:3], tied[3:]
        got = send_all(far_hops(rows, [shard_q] * (rows.far - 1)))
        prepared = prepare(start, *token_halves, *cot_halves, gain1, bias1)
        tied = tie(*got, *prepared, shard_a)
        got, prepared, shard_a = tied[:3], tied[3:8], tied[8]
        near_q0, near_q1 = arrange(rows, me, [shard_q] + list(got), [part, wide])
        own = [near_q0] + [hop(near_q0, m, dp_count) for m in MASKS[1:]]
        away_a = [hop(shard_a, m, dp_count) for m in (4, 8)]
        slabs["q0"] = own + [swap(v) for v in own]
        flow.add(fetch_near, "q1", slabs, [near_q1])
        flow.add(
            functools.partial(fetch_wide, [part + wide * cut, wide * (subs - cut)]),
            "c",
            slabs,
            [shard_a] + away_a,
        )
        flow.step(own[3])
    else:
        for name, shard in (
            ("q0", shards["q"][:, :part]),
            ("q1", shards["q"][:, part:]),
            ("a", shard_a[:, : part + wide * cut]),
            ("c", shard_a[:, part + wide * cut :]),
        ):
            slabs[name] = whole(shard)
        prepared = prepare(start, *token_halves, *cot_halves, gain1, bias1)
    x, normed, normed_t, cot, cot_t = prepared
    for g in range(groups):
        project(g)
        flow.step(forward[g][2])
    atts = [f[1] for f in forward]
    middle, normed_ffn, normed_ffn_t = out_norm(
        out_piece, flow.me, x, gain2, bias2, atts, slabs["a"]
    )
    flow.step(normed_ffn)

    held = None
    sums_of = {}
    onto = []
    feed_names = ["a"] * cut + ["c"] * (subs - cut)
    for s in range(subs):
        mixed, grad_in, grads = feed_forward(
            feed_pieces[s],
            feed_outs[s],
            flow.me,
            normed_ffn,
            normed_ffn_t,
            cot,
            cot_t,
            held,
            middle if s == subs - 1 else None,
            slabs[feed_names[s]],
            onto,
        )
        held = (mixed, grad_in)
        onto = grads
        if s % cut == cut - 1:
            k = s // cut
            if rows.split and k == 0:
                flow.add(halve, "early", sums_of, grads)
            elif rows.split:
                flow.add(reduce_all, "feed", sums_of, grads)
            else:
                sums_of[k] = plain(*grads)
            onto = []
        flow.step(grad_in)
    grad_middle, branch_t, sums2, grad_atts = out_back(
        out_piece, groups, flow.me, middle, grad_in, cot, gain2, slabs["a"]
    )
    mixed, core_place, _ = flow.step(mixed, core.astype(jnp.int32).reshape(1), sums2)
    mixed_held, mixed_other = turn_back(back, core_place, mixed)
    flow.add(exchange, "mixed", sums_of, [mixed_other])
    grad_projs = []
    onto = []

    held = None
    qkv_slabs = [slabs["q0"]] + [slabs["q1"]] * (groups - 1)
    for g in range(groups):
        proj, att, lse = forward[g]
        held, grads, sums1 = attend_back(
            qkv_pieces[g],
            qkv_outs[g],
            flow.me,
            normed_t,
            proj,
            att,
            grad_atts[g],
            lse,
            seg_col,
            seg_row,
            qkv_slabs[g],
            branch_t,
            atts if g == 0 else [],
            held,
            x if g == groups - 1 else None,
            onto,
        )
        onto = grads
        if g == 0:
            if rows.split:
                flow.add(reduce_direct, "first", sums_of, grads)
            else:
                sums_of["first"] = plain(*grads)
            onto = []
        if g < groups - 1:
            flow.step(held)
    sums = jnp.concatenate([sums1[:2], sums2[:2]], 0)
    if rows.split:
        flow.add(reduce_last, "last", sums_of, [*grads, sums])
        (held,) = flow.step(held)
    else:
        sums_of["last"] = plain(*grads)
    start_late, _ = tie(back, flow.me)
    tokens_held, tokens_other = norm_back(start_late, core_place, x, held, grad_middle, gain1)
    tokens_held, tokens_other = flow.step(tokens_held, tokens_other)
    if rows.split:
        block = rows.block
        keep, send = small_call(
            last_split_body,
            "last_split",
            [SDS((2 * block + 16, wide), BF)] * 2,
            [flow.me],
            sums_of["last"],
        )
        near = hop(send, 4, dp_count)
        rest, send = small_call(
            last_middle_body, "last_middle", [SDS((block + 16, wide), BF)] * 2, [], [keep, near]
        )
        away = hop(send, 8, dp_count)
        while flow.active:
            flow.step()
        grad_qkv, norm_sums = small_call(
            last_sum_body,
            "last_sum",
            [SDS((3, block, part), F32), SDS((4, depth), F32)],
            [],
            [rest, away, sums_of["first"]],
        )
        grad_qkv = grad_qkv.transpose(1, 0, 2)
        grad_out = sums_of["first"][:, :part].T
        feed_sums = [sums_of["feed"]]
    else:
        early, last = sums_of["first"], sums_of["last"]
        parts = [early[:, part:], last[:, :part], last[:, part:]]
        grad_qkv = jnp.concatenate([r.reshape(-1, 3, 128) for r in parts], 2)
        grad_out = early[:, :part].T
        feed_sums = [sums_of[0], sums_of[1]]
        norm_sums = jnp.sum(lax.all_gather(sums + swap(sums), "dp", axis=0), 0)
    feed_sum = jnp.concatenate(feed_sums, 1) if len(feed_sums) > 1 else feed_sums[0]
    feed_list = [feed_sum[:, wide * s : wide * (s + 1)] for s in range(subs)]

    def place(values, other):
        return lax.dynamic_update_index_in_dim(values, other, 1 - core, 0)[:, None]

    return (
        place(mixed_held, sums_of["mixed"]),
        place(tokens_held, swap(tokens_other)),
        norm_sums[0],
        norm_sums[1],
        grad_qkv,
        grad_out,
        norm_sums[2],
        norm_sums[3],
        jnp.concatenate([r[:, :part] for r in feed_list], 1),
        jnp.concatenate([r[:, part:] for r in feed_list], 1).T,
    )


def solution(mesh):
    in_specs = (
        P(None, "dp", "mp", None),
        P(None, "dp", None),
        P(),
        P(),
        P("dp", None, "mp"),
        P("mp", "dp"),
        P(),
        P(),
        P("dp", "mp"),
        P("mp", "dp"),
        P(None, "dp", "mp", None),
    )
    out_specs = (
        P(None, "dp", "mp", None),
        P(None, "dp", "mp", None),
        P(),
        P(),
        P("dp", None, "mp"),
        P("mp", "dp"),
        P(),
        P(),
        P("dp", "mp"),
        P("mp", "dp"),
    )
    return jax.shard_map(
        on_device, mesh=mesh, in_specs=in_specs, out_specs=out_specs, check_vma=False
    )
```

profile of v0, /device:TPU:0, one launch (start us, length us, event | category | flops | bytes accessed | tf_op | source)
XLA Modules:
  0.0 317.2 jit_solution(4283761145671434087)
XLA Ops:
  0.7 2.5 dynamic-slice_bitcast_fusion.2
  8.8 5.1 %collective-permute-start.4 = (bf16[48,1152]{1,0:T(8,128)(2,1)S(1)}, bf16[48,1152]{1,0:T(8,128)(2,1)S(1)}, u32[]{:S(2)}, u32[]{:S(2)}) collective-permute-start(bf16[48,1152]{1,0:T(8,128)(2,1)S(1)} %pad_maximum_fusion.1.refs_0_), channel_id=1, source_target_pairs={{0,24},{2,26},{4,28},{6,30},{8,16},{10,18},{12,20},{14,22},{16,8},... | collective-permute-start | bytes 331784 | tf_op jit(solution)/shard_map/ppermute | solution.py:992
  14.6 4.9 %prepare.1 = (bf16[1024,768]{1,0:T(8,128)(2,1)}, bf16[1024,768]{1,0:T(8,128)(2,1)S(1)}, bf16[768,1024]{1,0:T(8,128)(2,1)}, bf16[1024,768]{1,0:T(8,128)(2,1)S(1)}, bf16[768,1024]{1,0:T(8,128)(2,1)S(1)}) custom-call(s32[1]{0:T(128)} %bitcast.start, bf16[512,768]{1,0:T(8,128)(2,1)S(1)} %get-tuple-element.221.own, ...), custom_call_target="tpu_custom_call" | custom-call | flops 4000000000 | bytes 8000000 | tf_op jit(solution)/shard_map/prepare/pallas_call | solution.py:224
  30.4 2.0 collective-permute-start.6
  32.5 2.2 collective-permute-done.8.refs_1_
  34.7 2.0 collective-permute-done.5.refs_3_
  36.7 4.6 %collective-permute-done.7.refs_2_ = bf16[48,3456]{1,0:T(8,128)(2,1)S(1)} collective-permute-done((bf16[48,3456]{1,0:T(8,128)(2,1)}, bf16[48,3456]{1,0:T(8,128)(2,1)S(1)}, u32[]{:S(2)}, u32[]{:S(2)}) %collective-permute-start.7) | collective-permute-done | bytes 331808 | tf_op jit(solution)/shard_map/ppermute | solution.py:992
  42.8 2.2 collective-permute-done.6.refs_1_
  50.7 11.0 %project_attend.3 = (bf16[1024,768]{1,0:T(8,128)(2,1)}, bf16[1024,256]{1,0:T(8,128)(2,1)}, f32[8,1024]{1,0:T(8,128)}) custom-call(s32[1]{0:T(128)} %bitcast.1.me, bf16[1024,768]{1,0:T(8,128)(2,1)S(1)} %copy-done.16, s32[256,1]{1,0:T(8,128)S(1)} %copy.37.seg_col, s32[1,256]{1,0:T(1,128)S(1)} %bitcast.71, bf16[4,48,384]{2,1,0:T(8,128)(2,1)} %copy-done.5, ...), custom_call_target="tpu_custom_call" | custom-call | flops 8000000000 | bytes 8000000 | tf_op jit(solution)/shard_map/project_attend/pallas_call | solution.py:368
  68.2 23.8 %project_attend.4 = (bf16[1024,768]{1,0:T(8,128)(2,1)}, bf16[1024,256]{1,0:T(8,128)(2,1)}, f32[8,1024]{1,0:T(8,128)}) custom-call(s32[1]{0:T(128)} %bitcast.1.me, bf16[1024,768]{1,0:T(8,128)(2,1)S(1)} %copy-done.16, s32[256,1]{1,0:T(8,128)S(1)} %copy.37.seg_col, s32[1,256]{1,0:T(1,128)S(1)} %bitcast.72, bf16[4,48,768]{2,1,0:T(8,128)(2,1)} %copy-done.2, ...), custom_call_target="tpu_custom_call" | custom-call | flops 8000000000 | bytes 8000000 | tf_op jit(solution)/shard_map/project_attend/pallas_call | solution.py:368
  94.1 11.0 %project_attend.5 = (bf16[1024,768]{1,0:T(8,128)(2,1)}, bf16[1024,256]{1,0:T(8,128)(2,1)}, f32[8,1024]{1,0:T(8,128)}) custom-call(s32[1]{0:T(128)} %bitcast.1.me, bf16[1024,768]{1,0:T(8,128)(2,1)S(1)} %copy-done.16, s32[256,1]{1,0:T(8,128)S(1)} %copy.37.seg_col, s32[1,256]{1,0:T(1,128)S(1)} %bitcast.73, bf16[4,48,768]{2,1,0:T(8,128)(2,1)} %copy-done.2, ...), custom_call_target="tpu_custom_call" | custom-call | flops 8000000000 | bytes 8000000 | tf_op jit(solution)/shard_map/project_attend/pallas_call | solution.py:368
  105.2 2.7 collective-permute-done.26.refs_3_.refs_4_
  107.9 4.0 %collective-permute-done.25.refs_6_.refs_3_.refs_5_ = bf16[4,48,1920]{2,1,0:T(8,128)(2,1)S(1)} collective-permute-done((bf16[4,48,1920]{2,1,0:T(8,128)(2,1)S(1)}, bf16[4,48,1920]{2,1,0:T(8,128)(2,1)S(1)}, u32[]{:S(2)}, u32[]{:S(2)}) %collective-permute-start.25) | collective-permute-done | bytes 737312 | tf_op jit(solution)/shard_map/ppermute | solution.py:992
  115.1 6.7 %out_norm.1 = (f32[1024,768]{1,0:T(8,128)}, bf16[1024,768]{1,0:T(8,128)(2,1)S(1)}, bf16[768,1024]{1,0:T(8,128)(2,1)S(1)}) custom-call(s32[1]{0:T(128)} %bitcast.1.me, bf16[1024,768]{1,0:T(8,128)(2,1)} %get-tuple-element.273.tokens.refs_9_, f32[1,768]{1,0:T(1,128)S(1)} %reshape.132.gain, f32[1,768]{1,0:T(1,128)S(1)} %reshape.133.offset, ...), custom_call_target="tpu_custom_call" | custom-call | flops 3000000000 | bytes 8000000 | tf_op jit(solution)/shard_map/out_norm/pallas_call | solution.py:419
  121.8 5.9 %collective-permute-done.31.refs_4_.refs_5_ = bf16[4,48,1536]{2,1,0:T(8,128)(2,1)S(1)} collective-permute-done((bf16[4,48,1536]{2,1,0:T(8,128)(2,1)S(1)}, bf16[4,48,1536]{2,1,0:T(8,128)(2,1)S(1)}, u32[]{:S(2)}, u32[]{:S(2)}) %collective-permute-start.31) | collective-permute-done | bytes 589856 | tf_op jit(solution)/shard_map/ppermute | solution.py:992
  129.1 14.2 %feed_forward.4 = (f32[1024,768]{1,0:T(8,128)}, f32[1024,768]{1,0:T(8,128)}, bf16[4,4,48,1536]{3,2,1,0:T(8,128)(2,1)}, bf16[4,4,48,1536]{3,2,1,0:T(8,128)(2,1)}) custom-call(s32[1]{0:T(128)} %bitcast.1.me, bf16[1024,768]{1,0:T(8,128)(2,1)S(1)} %get-tuple-element.281.normed, bf16[768,1024]{1,0:T(8,128)(2,1)S(1)} %get-tuple-element.287.normed_t, ...), custom_call_target="tpu_custom_call" | custom-call | flops 11000000512 | bytes 20000000 | tf_op jit(solution)/shard_map/feed_forward/pallas_call | solution.py:541
  143.4 13.4 %feed_forward.5 = (f32[1024,768]{1,0:T(8,128)}, f32[1024,768]{1,0:T(8,128)}, bf16[4,4,48,1536]{3,2,1,0:T(8,128)(2,1)}, bf16[4,4,48,1536]{3,2,1,0:T(8,128)(2,1)}) custom-call(s32[1]{0:T(128)} %bitcast.1.me, bf16[1024,768]{1,0:T(8,128)(2,1)S(1)} %get-tuple-element.281.normed, ...), custom_call_target="tpu_custom_call", output_to_operand_aliasing={{2}: (15, {}), {3}: (16, {})} | custom-call | flops 11000000512 | bytes 20000000 | tf_op jit(solution)/shard_map/feed_forward/pallas_call | solution.py:541
  157.4 4.8 %collective-permute-done.35.refs_9_.refs_10_ = bf16[4,48,1536]{2,1,0:T(8,128)(2,1)S(1)} collective-permute-done((bf16[4,48,1536]{2,1,0:T(8,128)(2,1)S(1)}, bf16[4,48,1536]{2,1,0:T(8,128)(2,1)S(1)}, u32[]{:S(2)}, u32[]{:S(2)}) %collective-permute-start.35) | collective-permute-done | bytes 589856 | tf_op jit(solution)/shard_map/ppermute | solution.py:984
  163.0 12.6 %feed_forward.6 = (f32[1024,768]{1,0:T(8,128)}, f32[1024,768]{1,0:T(8,128)}, bf16[4,4,48,1536]{3,2,1,0:T(8,128)(2,1)}, bf16[4,4,48,1536]{3,2,1,0:T(8,128)(2,1)}) custom-call(s32[1]{0:T(128)} %bitcast.1.me, bf16[1024,768]{1,0:T(8,128)(2,1)S(1)} %get-tuple-element.281.normed, bf16[768,1024]{1,0:T(8,128)(2,1)S(1)} %get-tuple-element.287.normed_t, ...), custom_call_target="tpu_custom_call" | custom-call | flops 11000000512 | bytes 20000000 | tf_op jit(solution)/shard_map/feed_forward/pallas_call | solution.py:541
  177.7 14.1 %feed_forward.7 = (bf16[1024,768]{1,0:T(8,128)(2,1)}, f32[1024,768]{1,0:T(8,128)}, bf16[4,4,48,1536]{3,2,1,0:T(8,128)(2,1)}, bf16[4,4,48,1536]{3,2,1,0:T(8,128)(2,1)}) custom-call(s32[1]{0:T(128)} %bitcast.1.me, bf16[1024,768]{1,0:T(8,128)(2,1)S(1)} %get-tuple-element.281.normed, ...), custom_call_target="tpu_custom_call", output_to_operand_aliasing={{2}: (16, {}), {3}: (17, {})} | custom-call | flops 11000000512 | bytes 20000000 | tf_op jit(solution)/shard_map/feed_forward/pallas_call | solution.py:541
  194.9 8.9 %out_back.1 = (f32[1024,768]{1,0:T(8,128)}, bf16[768,1024]{1,0:T(8,128)(2,1)S(1)}, f32[8,768]{1,0:T(8,128)S(1)}, bf16[1024,256]{1,0:T(8,128)(2,1)}, bf16[1024,25...) custom-call(s32[1]{0:T(128)} %bitcast.1.me, f32[1024,768]{1,0:T(8,128)} %get-tuple-element.315.refs_2_.middle, ...), custom_call_target="tpu_custom_call" | custom-call | flops 4000000000 | bytes 16000000 | tf_op jit(solution)/shard_map/out_back/pallas_call | solution.py:600
  206.2 19.5 %attend_back.3 = (f32[1024,768]{1,0:T(8,128)}, bf16[4,4,48,768]{3,2,1,0:T(8,128)(2,1)}, bf16[4,4,48,768]{3,2,1,0:T(8,128)(2,1)}) custom-call(s32[1]{0:T(128)} %bitcast.1.me, bf16[768,1024]{1,0:T(8,128)(2,1)} %get-tuple-element.340.normed_t_in, bf16[1024,768]{1,0:T(8,128)(2,1)} %get-tuple-element.341.proj, ...), custom_call_target="tpu_custom_call" | custom-call | flops 12000000000 | bytes 8000000 | tf_op jit(solution)/shard_map/attend_back/pallas_call | solution.py:800
  225.7 2.1 turn_back.1
  231.5 18.5 %attend_back.4 = (f32[1024,768]{1,0:T(8,128)}, bf16[4,4,48,768]{3,2,1,0:T(8,128)(2,1)}, bf16[4,4,48,768]{3,2,1,0:T(8,128)(2,1)}) custom-call(s32[1]{0:T(128)} %bitcast.1.me, bf16[768,1024]{1,0:T(8,128)(2,1)} %get-tuple-element.340.normed_t_in, bf16[1024,768]{1,0:T(8,128)(2,1)} %get-tuple-element.356.proj, ...), custom_call_target="tpu_custom_call" | custom-call | flops 12000000000 | bytes 8000000 | tf_op jit(solution)/shard_map/attend_back/pallas_call | solution.py:800
  255.8 18.4 %attend_back.5 = (f32[1024,768]{1,0:T(8,128)}, bf16[4,4,48,768]{3,2,1,0:T(8,128)(2,1)}, bf16[4,4,48,768]{3,2,1,0:T(8,128)(2,1)}, f32[8,768]{1,0:T(8,128)S(1)}) custom-call(s32[1]{0:T(128)} %bitcast.1.me, bf16[768,1024]{1,0:T(8,128)(2,1)} %get-tuple-element.340.normed_t_in, ...), custom_call_target="tpu_custom_call", output_to_operand_aliasing={{1}: (18, {}), {2}: (19, {})} | custom-call | flops 12000000000 | bytes 8000000 | tf_op jit(solution)/shard_map/attend_back/pallas_call | solution.py:800
  278.4 2.1 collective-permute-start.54
  283.9 7.8 %norm_back.1 = (f32[2,512,768]{2,1,0:T(8,128)}, f32[512,768]{1,0:T(8,128)S(1)}) custom-call(s32[1]{0:T(128)S(6)} %select_n.37.start, s32[1]{0:T(128)} %bitcast.13.core, bf16[1024,768]{1,0:T(8,128)(2,1)} %get-tuple-element.273.tokens.refs_9_, f32[1024,768]{1,0:T(8,128)} %get-tuple-element.400.grad_normed, f32[1024,768]{1,0:T(8,128)} %get-tuple-element.401.grad_middle, ...), custom_call_target="tpu_custom_call" | custom-call | flops 4000000000 | bytes 16000000 | tf_op jit(solution)/shard_map/norm_back/pallas_call | solution.py:848
  291.7 2.7 collective-permute-done.54
  294.4 2.3 collective-permute-done.58.m3
  301.0 3.2 %collective-permute-done.62 = bf16[48,768]{1,0:T(8,128)(2,1)S(1)} collective-permute-done((bf16[48,768]{1,0:T(8,128)(2,1)S(1)}, bf16[48,768]{1,0:T(8,128)(2,1)S(1)}, u32[]{:S(2)}, u32[]{:S(2)}) %collective-permute-start.62) | collective-permute-done | bytes 73760 | tf_op jit(solution)/shard_map/ppermute | solution.py:992
  304.2 2.0 collective-permute-done.60.near
  307.7 5.5 %collective-permute-done.61.away = bf16[64,768]{1,0:T(8,128)(2,1)S(1)} collective-permute-done((bf16[64,768]{1,0:T(8,128)(2,1)S(1)}, bf16[64,768]{1,0:T(8,128)(2,1)S(1)}, u32[]{:S(2)}, u32[]{:S(2)}) %collective-permute-start.61) | collective-permute-done | bytes 98336 | tf_op jit(solution)/shard_map/ppermute | solution.py:992
  (272 shorter events, 70.6 us)
Async XLA Ops:
  24.1 17.2 %collective-permute-start.7 = (bf16[48,3456]{1,0:T(8,128)(2,1)}, bf16[48,3456]{1,0:T(8,128)(2,1)S(1)}, u32[]{:S(2)}, u32[]{:S(2)}) collective-permute-start(bf16[48,3456]{1,0:T(8,128)(2,1)} %pack.1.refs_0_), channel_id=1, source_target_pairs={{0,16},{2,18},{4,20},{6,22},{8,24},{10,26},{12,28},{14,30},{16,0},... | collective-permute-start | bytes 995336 | tf_op jit(solution)/shard_map/ppermute | solution.py:992
  30.4 14.6 %collective-permute-start.6 = (bf16[48,3456]{1,0:T(8,128)(2,1)}, bf16[48,3456]{1,0:T(8,128)(2,1)S(1)}, u32[]{:S(2)}, u32[]{:S(2)}) collective-permute-start(bf16[48,3456]{1,0:T(8,128)(2,1)} %pack.1.refs_0_), channel_id=1, source_target_pairs={{0,8},{2,10},{4,12},{6,14},{8,0},{10,2},{12,4},{14,6},{16,24},{18,... | collective-permute-start | bytes 995336 | tf_op jit(solution)/shard_map/ppermute | solution.py:992
  45.1 20.1 %collective-permute-start.18 = (bf16[4,48,768]{2,1,0:T(8,128)(2,1)S(1)}, bf16[4,48,768]{2,1,0:T(8,128)(2,1)S(1)}, u32[]{:S(2)}, u32[]{:S(2)}) collective-permute-start(bf16[4,48,768]{2,1,0:T(8,128)(2,1)S(1)} %get-tuple-element.244.refs_0_), channel_id=1, source_target_pairs={{0,1},{1,0},{2,3},{3,2},{4,5},{5,4},{6,7},{7,6},{8,9},{9,8},{10,11... | collective-permute-start | bytes 884744 | tf_op jit(solution)/shard_map/ppermute | solution.py:984
  45.1 16.7 %collective-permute-start.14 = (bf16[4,48,768]{2,1,0:T(8,128)(2,1)S(1)}, bf16[4,48,768]{2,1,0:T(8,128)(2,1)S(1)}, u32[]{:S(2)}, u32[]{:S(2)}) collective-permute-start(bf16[4,48,768]{2,1,0:T(8,128)(2,1)S(1)} %get-tuple-element.244.refs_0_), channel_id=1, source_target_pairs={{0,2},{2,0},{4,6},{6,4},{8,10},{10,8},{12,14},{14,12},{16,18},{18,... | collective-permute-start | bytes 884744 | tf_op jit(solution)/shard_map/ppermute | solution.py:992
  46.6 15.4 %collective-permute-start.15 = (bf16[4,48,768]{2,1,0:T(8,128)(2,1)S(1)}, bf16[4,48,768]{2,1,0:T(8,128)(2,1)S(1)}, u32[]{:S(2)}, u32[]{:S(2)}) collective-permute-start(bf16[4,48,768]{2,1,0:T(8,128)(2,1)S(1)} %get-tuple-element.244.refs_0_), channel_id=1, source_target_pairs={{0,4},{2,6},{4,0},{6,2},{8,12},{10,14},{12,8},{14,10},{16,20},{18,... | collective-permute-start | bytes 884744 | tf_op jit(solution)/shard_map/ppermute | solution.py:992
  63.8 28.3 %collective-permute-start.22 = (bf16[4,48,1920]{2,1,0:T(8,128)(2,1)S(1)}, bf16[4,48,1920]{2,1,0:T(8,128)(2,1)S(1)}, u32[]{:S(2)}, u32[]{:S(2)}) collective-permute-start(bf16[4,48,1920]{2,1,0:T(8,128)(2,1)S(1)} %get-tuple-element.258.refs_3_.refs_0_.refs_2_), channel_id=1, source_target_pairs={{0,2},{2,0},{4,6},{6,4},{8,10},{10,8},{12,14},{14,12},{16,18},{18,... | collective-permute-start | bytes 2211848 | tf_op jit(solution)/shard_map/ppermute | solution.py:992
  65.2 27.0 %collective-permute-start.23 = (bf16[4,48,1920]{2,1,0:T(8,128)(2,1)S(1)}, bf16[4,48,1920]{2,1,0:T(8,128)(2,1)S(1)}, u32[]{:S(2)}, u32[]{:S(2)}) collective-permute-start(bf16[4,48,1920]{2,1,0:T(8,128)(2,1)S(1)} %get-tuple-element.258.refs_3_.refs_0_.refs_2_), channel_id=1, source_target_pairs={{0,4},{2,6},{4,0},{6,2},{8,12},{10,14},{12,8},{14,10},{16,20},{18,... | collective-permute-start | bytes 2211848 | tf_op jit(solution)/shard_map/ppermute | solution.py:992
  66.7 25.4 %collective-permute-start.24 = (bf16[4,48,1920]{2,1,0:T(8,128)(2,1)S(1)}, bf16[4,48,1920]{2,1,0:T(8,128)(2,1)S(1)}, u32[]{:S(2)}, u32[]{:S(2)}) collective-permute-start(bf16[4,48,1920]{2,1,0:T(8,128)(2,1)S(1)} %get-tuple-element.258.refs_3_.refs_0_.refs_2_), channel_id=1, source_target_pairs={{0,1},{1,0},{2,3},{3,2},{4,5},{5,4},{6,7},{7,6},{8,9},{9,8},{10,11... | collective-permute-start | bytes 2211848 | tf_op jit(solution)/shard_map/ppermute | solution.py:984
  92.2 15.7 %collective-permute-start.26 = (bf16[4,48,1536]{2,1,0:T(8,128)(2,1)S(1)}, bf16[4,48,1536]{2,1,0:T(8,128)(2,1)S(1)}, u32[]{:S(2)}, u32[]{:S(2)}) collective-permute-start(bf16[4,48,1536]{2,1,0:T(8,128)(2,1)S(1)} %get-tuple-element.282.refs_2_.refs_3_), channel_id=1, source_target_pairs={{0,2},{2,0},{4,6},{6,4},{8,10},{10,8},{12,14},{14,12},{16,18},{18,... | collective-permute-start | bytes 1769480 | tf_op jit(solution)/shard_map/ppermute | solution.py:992
  93.0 14.9 %collective-permute-start.29 = (bf16[4,48,1536]{2,1,0:T(8,128)(2,1)S(1)}, bf16[4,48,1536]{2,1,0:T(8,128)(2,1)S(1)}, u32[]{:S(2)}, u32[]{:S(2)}) collective-permute-start(bf16[4,48,1536]{2,1,0:T(8,128)(2,1)S(1)} %get-tuple-element.282.refs_2_.refs_3_), channel_id=1, source_target_pairs={{0,1},{1,0},{2,3},{3,2},{4,5},{5,4},{6,7},{7,6},{8,9},{9,8},{10,11... | collective-permute-start | bytes 1769480 | tf_op jit(solution)/shard_map/ppermute | solution.py:984
  93.1 18.8 %collective-permute-start.25 = (bf16[4,48,1920]{2,1,0:T(8,128)(2,1)S(1)}, bf16[4,48,1920]{2,1,0:T(8,128)(2,1)S(1)}, u32[]{:S(2)}, u32[]{:S(2)}) collective-permute-start(bf16[4,48,1920]{2,1,0:T(8,128)(2,1)S(1)} %collective-permute-done.22.refs_4_.refs_1_.refs_3_), channel_id=1, source_target_pairs={{0,4},{2,6},{4,0},{6,2},{8,12},{10,14},{12,8},{14,10},{16,20},{18,... | collective-permute-start | bytes 2211848 | tf_op jit(solution)/shard_map/ppermute | solution.py:992
  93.6 18.3 %collective-permute-start.27 = (bf16[4,48,1920]{2,1,0:T(8,128)(2,1)S(1)}, bf16[4,48,1920]{2,1,0:T(8,128)(2,1)S(1)}, u32[]{:S(2)}, u32[]{:S(2)}) collective-permute-start(bf16[4,48,1920]{2,1,0:T(8,128)(2,1)S(1)} %collective-permute-done.22.refs_4_.refs_1_.refs_3_), channel_id=1, source_target_pairs={{0,1},{1,0},{2,3},{3,2},{4,5},{5,4},{6,7},{7,6},{8,9},{9,8},{10,11... | collective-permute-start | bytes 2211848 | tf_op jit(solution)/shard_map/ppermute | solution.py:984
  93.8 18.1 %collective-permute-start.28 = (bf16[4,48,1920]{2,1,0:T(8,128)(2,1)S(1)}, bf16[4,48,1920]{2,1,0:T(8,128)(2,1)S(1)}, u32[]{:S(2)}, u32[]{:S(2)}) collective-permute-start(bf16[4,48,1920]{2,1,0:T(8,128)(2,1)S(1)} %collective-permute-done.23.refs_5_.refs_2_.refs_4_), channel_id=1, source_target_pairs={{0,1},{1,0},{2,3},{3,2},{4,5},{5,4},{6,7},{7,6},{8,9},{9,8},{10,11... | collective-permute-start | bytes 2211848 | tf_op jit(solution)/shard_map/ppermute | solution.py:984
  112.0 15.7 %collective-permute-start.31 = (bf16[4,48,1536]{2,1,0:T(8,128)(2,1)S(1)}, bf16[4,48,1536]{2,1,0:T(8,128)(2,1)S(1)}, u32[]{:S(2)}, u32[]{:S(2)}) collective-permute-start(bf16[4,48,1536]{2,1,0:T(8,128)(2,1)S(1)} %get-tuple-element.282.refs_2_.refs_3_), channel_id=1, source_target_pairs={{0,4},{2,6},{4,0},{6,2},{8,12},{10,14},{12,8},{14,10},{16,20},{18,... | collective-permute-start | bytes 1769480 | tf_op jit(solution)/shard_map/ppermute | solution.py:992
  112.6 15.1 %collective-permute-start.32 = (bf16[4,48,1536]{2,1,0:T(8,128)(2,1)S(1)}, bf16[4,48,1536]{2,1,0:T(8,128)(2,1)S(1)}, u32[]{:S(2)}, u32[]{:S(2)}) collective-permute-start(bf16[4,48,1536]{2,1,0:T(8,128)(2,1)S(1)} %collective-permute-done.26.refs_3_.refs_4_), channel_id=1, source_target_pairs={{0,1},{1,0},{2,3},{3,2},{4,5},{5,4},{6,7},{7,6},{8,9},{9,8},{10,11... | collective-permute-start | bytes 1769480 | tf_op jit(solution)/shard_map/ppermute | solution.py:984
  127.8 15.6 %collective-permute-start.33 = (bf16[4,48,1536]{2,1,0:T(8,128)(2,1)S(1)}, bf16[4,48,1536]{2,1,0:T(8,128)(2,1)S(1)}, u32[]{:S(2)}, u32[]{:S(2)}) collective-permute-start(bf16[4,48,1536]{2,1,0:T(8,128)(2,1)S(1)} %collective-permute-done.31.refs_4_.refs_5_), channel_id=1, source_target_pairs={{0,2},{2,0},{4,6},{6,4},{8,10},{10,8},{12,14},{14,12},{16,18},{18,... | collective-permute-start | bytes 1769480 | tf_op jit(solution)/shard_map/ppermute | solution.py:992
  156.8 18.9 %collective-permute-start.36 = (bf16[4,4,48,1536]{3,2,1,0:T(8,128)(2,1)}, bf16[4,4,48,1536]{3,2,1,0:T(8,128)(2,1)S(1)}, u32[]{:S(2)}, u32[]{:S(2)}) collective-permute-start(bf16[4,4,48,1536]{3,2,1,0:T(8,128)(2,1)} %get-tuple-element.309), channel_id=1, source_target_pairs={{0,1},{1,0},{2,3},{3,2},{4,5},{5,4},{6,7},{7,6},{8,9},{9,8},{10,11... | collective-permute-start | bytes 7077896 | tf_op jit(solution)/shard_map/ppermute | solution.py:984
  176.3 15.5 %collective-permute-start.37 = (bf16[2,4,48,768]{3,2,1,0:T(8,128)(2,1)S(1)}, bf16[2,4,48,768]{3,2,1,0:T(8,128)(2,1)S(1)}, u32[]{:S(2)}, u32[]{:S(2)}) collective-permute-start(bf16[2,4,48,768]{3,2,1,0:T(8,128)(2,1)S(1)} %get-tuple-element.319), channel_id=1, source_target_pairs={{0,2},{2,0},{4,6},{6,4},{8,10},{10,8},{12,14},{14,12},{16,18},{18,... | collective-permute-start | bytes 1769480 | tf_op jit(solution)/shard_map/ppermute | solution.py:992
  177.1 15.1 %collective-permute-start.38 = (bf16[2,4,48,768]{3,2,1,0:T(8,128)(2,1)S(1)}, bf16[2,4,48,768]{3,2,1,0:T(8,128)(2,1)S(1)}, u32[]{:S(2)}, u32[]{:S(2)}) collective-permute-start(bf16[2,4,48,768]{3,2,1,0:T(8,128)(2,1)S(1)} %get-tuple-element.320), channel_id=1, source_target_pairs={{0,4},{2,6},{4,0},{6,2},{8,12},{10,14},{12,8},{14,10},{16,20},{18,... | collective-permute-start | bytes 1769480 | tf_op jit(solution)/shard_map/ppermute | solution.py:992
  204.5 23.4 %collective-permute-start.42 = (bf16[2,4,48,768]{3,2,1,0:T(8,128)(2,1)S(1)}, bf16[2,4,48,768]{3,2,1,0:T(8,128)(2,1)S(1)}, u32[]{:S(2)}, u32[]{:S(2)}) collective-permute-start(bf16[2,4,48,768]{3,2,1,0:T(8,128)(2,1)S(1)} %get-tuple-element.345), channel_id=1, source_target_pairs={{0,2},{2,0},{4,6},{6,4},{8,10},{10,8},{12,14},{14,12},{16,18},{18,... | collective-permute-start | bytes 1769480 | tf_op jit(solution)/shard_map/ppermute | solution.py:992
  205.2 22.6 %collective-permute-start.43 = (bf16[2,4,48,768]{3,2,1,0:T(8,128)(2,1)S(1)}, bf16[2,4,48,768]{3,2,1,0:T(8,128)(2,1)S(1)}, u32[]{:S(2)}, u32[]{:S(2)}) collective-permute-start(bf16[2,4,48,768]{3,2,1,0:T(8,128)(2,1)S(1)} %get-tuple-element.346), channel_id=1, source_target_pairs={{0,4},{2,6},{4,0},{6,2},{8,12},{10,14},{12,8},{14,10},{16,20},{18,... | collective-permute-start | bytes 1769480 | tf_op jit(solution)/shard_map/ppermute | solution.py:992
  229.1 20.9 %collective-permute-start.47 = (bf16[4,4,48,768]{3,2,1,0:T(8,128)(2,1)S(1)}, bf16[4,4,48,768]{3,2,1,0:T(8,128)(2,1)S(1)}, u32[]{:S(2)}, u32[]{:S(2)}) collective-permute-start(bf16[4,4,48,768]{3,2,1,0:T(8,128)(2,1)S(1)} %copy-done.30), channel_id=1, source_target_pairs={{0,1},{1,0},{2,3},{3,2},{4,5},{5,4},{6,7},{7,6},{8,9},{9,8},{10,11... | collective-permute-start | bytes 3538952 | tf_op jit(solution)/shard_map/ppermute | solution.py:984
  229.1 20.9 %collective-permute-start.44 = (bf16[4,48,768]{2,1,0:T(8,128)(2,1)S(1)}, bf16[4,48,768]{2,1,0:T(8,128)(2,1)S(1)}, u32[]{:S(2)}, u32[]{:S(2)}) collective-permute-start(bf16[4,48,768]{2,1,0:T(8,128)(2,1)S(1)} %fusion.2), channel_id=1, source_target_pairs={{0,4},{2,6},{4,0},{6,2},{8,12},{10,14},{12,8},{14,10},{16,20},{18,... | collective-permute-start | bytes 884744 | tf_op jit(solution)/shard_map/ppermute | solution.py:992
  230.2 19.8 %collective-permute-start.45 = (bf16[4,48,768]{2,1,0:T(8,128)(2,1)S(1)}, bf16[4,48,768]{2,1,0:T(8,128)(2,1)S(1)}, u32[]{:S(2)}, u32[]{:S(2)}) collective-permute-start(bf16[4,48,768]{2,1,0:T(8,128)(2,1)S(1)} %fusion.3), channel_id=1, source_target_pairs={{0,2},{2,0},{4,6},{6,4},{8,10},{10,8},{12,14},{14,12},{16,18},{18,... | collective-permute-start | bytes 884744 | tf_op jit(solution)/shard_map/ppermute | solution.py:992
  231.5 18.5 %collective-permute-start.46 = (bf16[512,768]{1,0:T(8,128)(2,1)S(1)}, bf16[512,768]{1,0:T(8,128)(2,1)S(1)}, u32[]{:S(2)}, u32[]{:S(2)}) collective-permute-start(bf16[512,768]{1,0:T(8,128)(2,1)S(1)} %get-tuple-element.361), channel_id=1, source_target_pairs={{0,1},{1,0},{2,3},{3,2},{4,5},{5,4},{6,7},{7,6},{8,9},{9,8},{10,11... | collective-permute-start | bytes 2359304 | tf_op jit(solution)/shard_map/ppermute | solution.py:984
  250.8 23.5 %collective-permute-start.49 = (bf16[4,48,768]{2,1,0:T(8,128)(2,1)S(1)}, bf16[4,48,768]{2,1,0:T(8,128)(2,1)S(1)}, u32[]{:S(2)}, u32[]{:S(2)}) collective-permute-start(bf16[4,48,768]{2,1,0:T(8,128)(2,1)S(1)} %get-tuple-element.379), channel_id=1, source_target_pairs={{0,2},{2,0},{4,6},{6,4},{8,10},{10,8},{12,14},{14,12},{16,18},{18,... | collective-permute-start | bytes 884744 | tf_op jit(solution)/shard_map/ppermute | solution.py:992
  251.6 22.7 %collective-permute-start.50 = (bf16[4,48,768]{2,1,0:T(8,128)(2,1)S(1)}, bf16[4,48,768]{2,1,0:T(8,128)(2,1)S(1)}, u32[]{:S(2)}, u32[]{:S(2)}) collective-permute-start(bf16[4,48,768]{2,1,0:T(8,128)(2,1)S(1)} %get-tuple-element.380), channel_id=1, source_target_pairs={{0,4},{2,6},{4,0},{6,2},{8,12},{10,14},{12,8},{14,10},{16,20},{18,... | collective-permute-start | bytes 884744 | tf_op jit(solution)/shard_map/ppermute | solution.py:992
  252.5 21.8 %collective-permute-start.51 = (bf16[4,48,768]{2,1,0:T(8,128)(2,1)S(1)}, bf16[4,48,768]{2,1,0:T(8,128)(2,1)S(1)}, u32[]{:S(2)}, u32[]{:S(2)}) collective-permute-start(bf16[4,48,768]{2,1,0:T(8,128)(2,1)S(1)} %get-tuple-element.381), channel_id=1, source_target_pairs={{0,6},{2,4},{4,2},{6,0},{8,14},{10,12},{12,10},{14,8},{16,22},{18,... | collective-permute-start | bytes 884744 | tf_op jit(solution)/shard_map/ppermute | solution.py:992
  254.3 19.9 %collective-permute-start.48 = (bf16[2,48,3072]{2,1,0:T(8,128)(2,1)S(1)}, bf16[2,48,3072]{2,1,0:T(8,128)(2,1)S(1)}, u32[]{:S(2)}, u32[]{:S(2)}) collective-permute-start(bf16[2,48,3072]{2,1,0:T(8,128)(2,1)S(1)} %get-tuple-element.378), channel_id=1, source_target_pairs={{0,8},{2,10},{4,12},{6,14},{8,0},{10,2},{12,4},{14,6},{16,24},{18,... | collective-permute-start | bytes 1769480 | tf_op jit(solution)/shard_map/ppermute | solution.py:992
  278.4 16.0 %collective-permute-start.54 = (bf16[48,3072]{1,0:T(8,128)(2,1)S(1)}, bf16[48,3072]{1,0:T(8,128)(2,1)S(1)}, u32[]{:S(2)}, u32[]{:S(2)}) collective-permute-start(bf16[48,3072]{1,0:T(8,128)(2,1)S(1)} %fusion.7), channel_id=1, source_target_pairs={{0,16},{2,18},{4,20},{6,22},{8,24},{10,26},{12,28},{14,30},{16,0},... | collective-permute-start | bytes 884744 | tf_op jit(solution)/shard_map/ppermute | solution.py:992
  282.0 14.7 %collective-permute-start.58 = (bf16[208,768]{1,0:T(8,128)(2,1)S(1)}, bf16[208,768]{1,0:T(8,128)(2,1)S(1)}, u32[]{:S(2)}, u32[]{:S(2)}) collective-permute-start(bf16[208,768]{1,0:T(8,128)(2,1)S(1)} %get-tuple-element.408), channel_id=1, source_target_pairs={{0,6},{2,4},{4,2},{6,0},{8,14},{10,12},{12,10},{14,8},{16,22},{18,... | collective-permute-start | bytes 958472 | tf_op jit(solution)/shard_map/ppermute | solution.py:992
  296.8 17.8 %collective-permute-start.59 = (f32[512,768]{1,0:T(8,128)S(1)}, f32[512,768]{1,0:T(8,128)S(1)}, u32[]{:S(2)}, u32[]{:S(2)}) collective-permute-start(f32[512,768]{1,0:T(8,128)S(1)} %get-tuple-element.410), channel_id=1, source_target_pairs={{0,1},{1,0},{2,3},{3,2},{4,5},{5,4},{6,7},{7,6},{8,9},{9,8},{10,11... | collective-permute-start | bytes 4718600 | tf_op jit(solution)/shard_map/ppermute | solution.py:984
  (90 other events, 777.3 us)
where the time goes:
time: 322 us; the launch traced here: 317 us
  Pallas kernels  191 us (59%)
  starting transfers between devices  48.7 us (15%)
  waiting for transfers between devices  48.5 us (15%)
  local copies, waits for them, and re-layouts  20.9 us (6%)
  other arithmetic  4.42 us (1%)
  between operations  3.88 us (1%)
    pallas_call x3, Pallas kernels, attend_back(): pl.pallas_call(functools.partial(attend_back_body, piece, out_piece, extr...  56.4 us
    pallas_call x4, Pallas kernels, feed_forward(): pl.pallas_call(functools.partial(feed_forward_body, piece, out_piece, fir...  54.3 us
    pallas_call x3, Pallas kernels, project_attend(): pl.pallas_call(functools.partial(project_attend_body, piece), in_specs=[s...  45.9 us
    ppermute x38, starting transfers between devices, hop(): return lax.ppermute(value, 'dp', [(i, i ^ mask) for i in range(count)])  45.2 us
    ppermute x38, waiting for transfers between devices, hop(): return lax.ppermute(value, 'dp', [(i, i ^ mask) for i in range(count)])  40.5 us
    unnamed x119, local copies, waits for them, and re-layouts  15.8 us
    pallas_call x1, Pallas kernels, out_back(): pl.pallas_call(functools.partial(out_back_body, piece, groups), grid=(len...  8.85 us
    ppermute x25, waiting for transfers between devices, swap(): return lax.ppermute(value, 'mp', [(0, 1), (1, 0)])  8.07 us
  transfers between devices with their start and end apart: 63, of which 19 were waited for; matrix products, arithmetic and copies ran while one was open for 2% of the time, Pallas kernels for 56%

commit v1 on v0

--- a/solution.py
+++ b/solution.py
@@ -141,12 +141,6 @@
     bias[1] = jnp.where((query >= key) & (seg_col[...] == seg_row[...]), 0.0, NEG)
 
 
-def fill_double(double, halves):
-    here = halves[0].shape[0]
-    for k in range(4):
-        double[k * here : (k + 1) * here, :] = halves[k % 2][...]
-
-
 def turned(doubles, start, r):
     coarse = pl.multiple_of(start // 16 * 16 + r * QB, 16)
     fine = start % 16
@@ -169,6 +163,7 @@
 
 def prepare_body(
     start,
+    core,
     own,
     other,
     cot_own,
@@ -176,16 +171,27 @@
     gain,
     offset,
     x_out,
+    normed_out,
+    normed_t_out,
+    cot_out,
+    cot_t_out,
+    double,
+    cot_double,
+    x,
     normed,
-    normed_t_out,
+    normed_t,
     cot,
     cot_t,
-    double,
-    x,
-    normed_t,
     sems,
 ):
-    fill_double(double, [own, other])
+    here = own.shape[1]
+    mine = core[0]
+    for buf, halves, sem in ((double, (own, other), 5), (cot_double, (cot_own, cot_other), 6)):
+        for k in range(4):
+            pltpu.make_async_copy(
+                halves[k % 2].at[mine], buf.at[pl.ds(k * here, here)], sems.at[sem]
+            ).start()
+    wait_bytes(double, sems.at[5])
 
     def step(r, carry):
         at = pl.ds(pl.multiple_of(r * QB, QB), QB)
@@ -200,48 +206,44 @@
     count = x.shape[0] // QB
     lax.fori_loop(0, count, step, 0)
     copies = [
-        pltpu.make_async_copy(x, x_out, sems.at[0]),
-        pltpu.make_async_copy(normed_t, normed_t_out, sems.at[1]),
+        pltpu.make_async_copy(normed, normed_out, sems.at[0]),
+        pltpu.make_async_copy(x, x_out, sems.at[1]),
+        pltpu.make_async_copy(normed_t, normed_t_out, sems.at[2]),
+        pltpu.make_async_copy(cot, cot_out, sems.at[3]),
+        pltpu.make_async_copy(cot_t, cot_t_out, sems.at[4]),
     ]
-    start_all(copies)
-    fill_double(double, [cot_own, cot_other])
+    start_all(copies[:3])
+    wait_bytes(cot_double, sems.at[6])
 
     def second(r, carry):
         at = pl.ds(pl.multiple_of(r * QB, QB), QB)
-        low = turned([double], start[0], r).astype(BF)
+        low = turned([cot_double], start[0], r).astype(BF)
         cot[at, :] = low
         cot_t[:, at] = low.T
         return carry
 
     lax.fori_loop(0, count, second, 0)
+    start_all(copies[3:])
     for copy in copies:
         copy.wait()
 
 
-def prepare(start, own, other, cot_own, cot_other, gain, offset):
-    here, depth = own.shape
+def prepare(start, core, own, other, cot_own, cot_other, gain, offset):
+    _, here, depth = own.shape
     shape, shape_t = (2 * here, depth), (depth, 2 * here)
+    shapes = [shape, shape, shape_t, shape, shape_t]
     return pl.pallas_call(
         prepare_body,
-        in_specs=[smem_spec()] + [vmem_spec()] * 6,
-        out_specs=[any_spec(), vmem_spec(), any_spec(), vmem_spec(), vmem_spec()],
-        out_shape=[
-            pltpu.HBM(shape, BF),
-            pltpu.VMEM(shape, BF),
-            pltpu.HBM(shape_t, BF),
-            pltpu.VMEM(shape, BF),
-            pltpu.VMEM(shape_t, BF),
-        ],
-        scratch_shapes=[
-            pltpu.VMEM((4 * here, depth), BF),
-            pltpu.VMEM(shape, BF),
-            pltpu.VMEM(shape_t, BF),
-            pltpu.SemaphoreType.DMA((2,)),
-        ],
-        compiler_params=params(20),
+        in_specs=[smem_spec()] * 2 + [any_spec()] * 4 + [vmem_spec()] * 2,
+        out_specs=[any_spec()] * 5,
+        out_shape=[pltpu.HBM(s, BF) for s in shapes],
+        scratch_shapes=[pltpu.VMEM((4 * here, depth), BF)] * 2
+        + [pltpu.VMEM(s, BF) for s in shapes]
+        + [pltpu.SemaphoreType.DMA((7,))],
+        compiler_params=params(28),
         cost_estimate=cost(4, 8),
         name="prepare",
-    )(start, own, other, cot_own, cot_other, gain, offset)
+    )(start, core, *in_hbm([own, other, cot_own, cot_other]), gain, offset)
 
 
 def turn_back_body(start, core, values, held, other, double, own, sem):
@@ -260,6 +262,26 @@
     copy = pltpu.make_async_copy(own, held.at[core[0]], sem)
     copy.start()
     copy.wait()
+
+
+def place_body(core, other, held, out, sem):
+    copy = pltpu.make_async_copy(other, out.at[1 - core[0]], sem)
+    copy.start()
+    copy.wait()
+
+
+def place(core, held, other):
+    return pl.pallas_call(
+        place_body,
+        in_specs=[smem_spec(), any_spec(), any_spec()],
+        out_specs=any_spec(),
+        out_shape=pltpu.HBM(held.shape, held.dtype),
+        input_output_aliases={2: 0},
+        scratch_shapes=[pltpu.SemaphoreType.DMA],
+        compiler_params=params(4),
+        cost_estimate=cost(0, 4),
+        name="place",
+    )(core, other, *in_hbm([held]))
 
 
 def turn_back(start, core, values):
@@ -313,12 +335,9 @@
     wait_bytes(weight, sem)
     length = normed.shape[0]
 
-    def project(r, carry):
-        at = pl.ds(pl.multiple_of(r * 512, 512), 512)
-        proj[at, :] = nn(normed[at, :], flat(weight[...])).astype(BF)
-        return carry
-
-    lax.fori_loop(0, length // 512, project, 0)
+    for c in range(3):
+        cols = slice(c * 256, c * 256 + 256)
+        proj[:, cols] = nn(normed[...], flat(weight[:, :, :, cols])).astype(BF)
     proj_copy = pltpu.make_async_copy(proj, proj_out, out_sem)
     proj_copy.start()
     for half in range(2):
@@ -387,7 +406,7 @@
         compiler_params=params(20),
         cost_estimate=cost(8, 8),
         name="project_attend",
-    )(me, *in_vmem([normed]), seg_col, seg_row, *in_hbm(slabs))
+    )(me, *in_hbm([normed]), seg_col, seg_row, *in_hbm(slabs))
 
 
 def join_heads(attended):
@@ -438,7 +457,9 @@
 def gelu_parts(values):
     size = jnp.abs(values)
     density = jnp.exp2(values * values * (-0.5 * LOG2E) + math.log2(1.0 / math.sqrt(2 * math.pi)))
-    t = 1.0 / (1.0 + 0.2316419 * size)
+    below = 1.0 + 0.2316419 * size
+    t = pl.reciprocal(below, approx=True)
+    t = t * (2.0 - below * t)
     poly = t * (
         0.319381530
         + t * (-0.356563782 + t * (1.781477937 + t * (-1.821255978 + t * 1.330274429)))
@@ -1082,11 +1103,6 @@
         [w_out.T, w_up, w_down.T],
     )[0]
 
-    def halves(values):
-        own = lax.dynamic_index_in_dim(values[:, 0], core, 0, keepdims=False)
-        away = lax.dynamic_index_in_dim(values[:, 0], 1 - core, 0, keepdims=False)
-        return own, swap(away)
-
     seg = lax.dynamic_index_in_dim(segment[:, 0], core, 0, keepdims=False)
     run = length * 3 // 4
     begin = jnp.argmax(seg[: length - run + 1] == seg[run - 1 :]).astype(jnp.int32)
@@ -1100,8 +1116,9 @@
     )
 
     flow = Flow(me)
-    token_halves = halves(tokens)
-    cot_halves = halves(cotangent)
+    core_place = core.astype(jnp.int32).reshape(1)
+    token_halves = [tokens[:, 0], swap(tokens[:, 0])]
+    cot_halves = [cotangent[:, 0], swap(cotangent[:, 0])]
     wide = 2 * part
     qkv_pieces = [Piece(rows, "slabs")] + [Piece(rows, "slabs", part * g) for g in range(groups - 1)]
     out_piece = Piece(rows, "slabs")
@@ -1126,13 +1143,14 @@
     def via(mask):
         return functools.partial(hop, mask=mask, count=dp_count)
 
-    def fetch_wide(widths, shard, near, away):
-        (both_ways,) = yield [(away, via(4))]
+    def fetch_wide(widths, shard, away):
+        near, both_ways = yield [(shard, via(4)), (away, via(4))]
         a0, c0 = arrange(rows, flow.me, [shard, near, away, both_ways], widths)
         a1, a2, b0 = yield [(a0, via(1)), (a0, via(2))] + swaps([a0])
         a3, c1, b1, b2, d0 = yield [(a1, via(2)), (c0, via(1))] + swaps([a1, a2, c0])
         slabs["a"] = [a0, a1, a2, a3, b0, b1, b2, swap(a3)]
-        c2, d1 = yield [(c0, via(2))] + swaps([c1])
+        (d1,) = yield swaps([c1])
+        (c2,) = yield [(c0, via(2))]
         c3, d2 = yield [(c2, via(1))] + swaps([c2])
         return [c0, c1, c2, c3, d0, d1, d2, swap(c3)]
 
@@ -1211,22 +1229,21 @@
         )
 
     if rows.split:
-        tied = tie(shards["q"], *token_halves, *cot_halves)
-        shard_q, token_halves, cot_halves = tied[0], tied[1:3], tied[3:]
+        shard_q = shards["q"]
         got = send_all(far_hops(rows, [shard_q] * (rows.far - 1)))
-        prepared = prepare(start, *token_halves, *cot_halves, gain1, bias1)
+        prepared = prepare(start, core_place, *token_halves, *cot_halves, gain1, bias1)
         tied = tie(*got, *prepared, shard_a)
         got, prepared, shard_a = tied[:3], tied[3:8], tied[8]
         near_q0, near_q1 = arrange(rows, me, [shard_q] + list(got), [part, wide])
         own = [near_q0] + [hop(near_q0, m, dp_count) for m in MASKS[1:]]
-        away_a = [hop(shard_a, m, dp_count) for m in (4, 8)]
+        away_a = hop(shard_a, 8, dp_count)
         slabs["q0"] = own + [swap(v) for v in own]
         flow.add(fetch_near, "q1", slabs, [near_q1])
         flow.add(
             functools.partial(fetch_wide, [part + wide * cut, wide * (subs - cut)]),
             "c",
             slabs,
-            [shard_a] + away_a,
+            [shard_a, away_a],
         )
         flow.step(own[3])
     else:
@@ -1237,7 +1254,7 @@
             ("c", shard_a[:, part + wide * cut :]),
         ):
             slabs[name] = whole(shard)
-        prepared = prepare(start, *token_halves, *cot_halves, gain1, bias1)
+        prepared = prepare(start, core_place, *token_halves, *cot_halves, gain1, bias1)
     x, normed, normed_t, cot, cot_t = prepared
     for g in range(groups):
         project(g)
@@ -1281,7 +1298,7 @@
     grad_middle, branch_t, sums2, grad_atts = out_back(
         out_piece, groups, flow.me, middle, grad_in, cot, gain2, slabs["a"]
     )
-    mixed, core_place, _ = flow.step(mixed, core.astype(jnp.int32).reshape(1), sums2)
+    mixed, core_place, _ = flow.step(mixed, core_place, sums2)
     mixed_held, mixed_other = turn_back(back, core_place, mixed)
     flow.add(exchange, "mixed", sums_of, [mixed_other])
     grad_projs = []
@@ -1363,12 +1380,9 @@
     feed_sum = jnp.concatenate(feed_sums, 1) if len(feed_sums) > 1 else feed_sums[0]
     feed_list = [feed_sum[:, wide * s : wide * (s + 1)] for s in range(subs)]
 
-    def place(values, other):
-        return lax.dynamic_update_index_in_dim(values, other, 1 - core, 0)[:, None]
-
     return (
-        place(mixed_held, sums_of["mixed"]),
-        place(tokens_held, swap(tokens_other)),
+        place(core_place, mixed_held, sums_of["mixed"])[:, None],
+        place(core_place, tokens_held, swap(tokens_other))[:, None],
         norm_sums[0],
         norm_sums[1],
         grad_qkv,

time: 322 us -> 320 us (level)
  Pallas kernels: 191 us -> 200 us
  local copies, waits for them, and re-layouts: 20.9 us -> 11.9 us
  waiting for transfers between devices: 48.5 us -> 41.7 us
  starting transfers between devices: 48.7 us -> 52.6 us
    unnamed x119 -> x97, local copies, waits for them, and re-layouts: 15.8 us -> 9.01 us
    ppermute x38, waiting for transfers between devices: 40.5 us -> 33.8 us  [hop(): return lax.ppermute(value, 'dp', [(i, i ^ mask) for i in range(count)])]
    pallas_call x1 -> x3, Pallas kernels: 4.93 us -> 11.1 us  [the longest x1 9.01 us: prepare(): pl.pallas_call(prepare_body, in_specs=[smem_spec()] * 2 + [any_spec()] *...]
    pallas_call x3, Pallas kernels: 45.9 us -> 49.7 us  [project_attend(): pl.pallas_call(functools.partial(project_attend_body, piece), in_specs=[s...]
    squeeze x2 -> x0, local copies, waits for them, and re-layouts: 3.45 us -> none  [halves(): away = lax.dynamic_index_in_dim(values[:, 0], 1 - core, 0, keepdims=False)]
  transfers between devices with their start and end apart: 63 -> 63, of which waited for: 19 -> 17; matrix products, arithmetic and copies ran while one was open for 2% -> 2% of each run, Pallas kernels for 56% -> 63%
where the time goes in v1:
time: 320 us; the launch traced here: 315 us
  Pallas kernels  200 us (62%)
  starting transfers between devices  52.6 us (16%)
  waiting for transfers between devices  41.7 us (13%)
  local copies, waits for them, and re-layouts  11.9 us (4%)
  other arithmetic  5.33 us (2%)
  between operations  3.85 us (1%)
    pallas_call x3, Pallas kernels, attend_back(): pl.pallas_call(functools.partial(attend_back_body, piece, out_piece, extr...  56.1 us
    pallas_call x4, Pallas kernels, feed_forward(): pl.pallas_call(functools.partial(feed_forward_body, piece, out_piece, fir...  55.4 us
    pallas_call x3, Pallas kernels, project_attend(): pl.pallas_call(functools.partial(project_attend_body, piece), in_specs=[s...  49.7 us
    ppermute x38, starting transfers between devices, hop(): return lax.ppermute(value, 'dp', [(i, i ^ mask) for i in range(count)])  48.4 us
    ppermute x38, waiting for transfers between devices, hop(): return lax.ppermute(value, 'dp', [(i, i ^ mask) for i in range(count)])  33.8 us
    pallas_call x1, Pallas kernels, out_back(): pl.pallas_call(functools.partial(out_back_body, piece, groups), grid=(len...  9.05 us
    pallas_call x1, Pallas kernels, prepare(): pl.pallas_call(prepare_body, in_specs=[smem_spec()] * 2 + [any_spec()] *...  9.01 us
    unnamed x97, local copies, waits for them, and re-layouts  9.01 us
  transfers between devices with their start and end apart: 63, of which 17 were waited for; matrix products, arithmetic and copies ran while one was open for 2% of the time, Pallas kernels for 63%

profile of v1, /device:TPU:0, one launch (start us, length us, event | category | flops | bytes accessed | tf_op | source)
XLA Modules:
  0.0 315.2 jit_solution(2765242399581825289)
XLA Ops:
  2.1 5.1 %collective-permute-start.2 = (bf16[48,1152]{1,0:T(8,128)(2,1)S(1)}, bf16[48,1152]{1,0:T(8,128)(2,1)S(1)}, u32[]{:S(2)}, u32[]{:S(2)}) collective-permute-start(bf16[48,1152]{1,0:T(8,128)(2,1)S(1)} %bitcast_dynamic-update-slice_fusion.refs_0_), channel_id=1, source_target_pairs={{0,24},{2,26},{4,28},{6,30},{8,16},{10,18},{12,20},{14,22},{16,8},... | collective-permute-start | bytes 331784 | tf_op jit(solution)/shard_map/ppermute | solution.py:1013
  15.1 9.0 %prepare.1 = (bf16[1024,768]{1,0:T(8,128)(2,1)}, bf16[1024,768]{1,0:T(8,128)(2,1)}, bf16[768,1024]{1,0:T(8,128)(2,1)}, bf16[1024,768]{1,0:T(8,128)(2,1)}, bf16[768,1024]{1,0:T(8,128)(2,1)}) custom-call(s32[1]{0:T(128)} %bitcast.1.start, s32[1]{0:T(128)} %bitcast.2.core, bf16[2,512,768]{2,1,0:T(8,128)(2,1)} %bitcast.70, bf16[2,512,768]{2,1,0:T(8,128)(2,1)} %copy-done.17, ...), custom_call_target="tpu_custom_call" | custom-call | flops 4000000000 | bytes 8000000 | tf_op jit(solution)/shard_map/prepare/pallas_call | solution.py:235
  24.2 1.7 collective-permute-start.8
  27.8 2.3 collective-permute-start.6
  30.6 1.8 collective-permute-done.7.refs_1_
  35.7 8.6 %collective-permute-done.6.refs_2_ = bf16[48,3456]{1,0:T(8,128)(2,1)S(1)} collective-permute-done((bf16[48,3456]{1,0:T(8,128)(2,1)S(1)}, bf16[48,3456]{1,0:T(8,128)(2,1)S(1)}, u32[]{:S(2)}, u32[]{:S(2)}) %collective-permute-start.6) | collective-permute-done | bytes 331808 | tf_op jit(solution)/shard_map/ppermute | solution.py:1013
  48.1 1.7 collective-permute-start.17
  49.8 12.2 %project_attend.3 = (bf16[1024,768]{1,0:T(8,128)(2,1)}, bf16[1024,256]{1,0:T(8,128)(2,1)}, f32[8,1024]{1,0:T(8,128)}) custom-call(s32[1]{0:T(128)} %bitcast.me, bf16[1024,768]{1,0:T(8,128)(2,1)} %get-tuple-element.233.normed, s32[256,1]{1,0:T(8,128)S(1)} %copy.37.seg_col, s32[1,256]{1,0:T(1,128)S(1)} %bitcast.58, bf16[4,48,384]{2,1,0:T(8,128)(2,1)} %copy-done.5, ...), custom_call_target="tpu_custom_call" | custom-call | flops 8000000000 | bytes 8000000 | tf_op jit(solution)/shard_map/project_attend/pallas_call | solution.py:387
  68.1 25.2 %project_attend.4 = (bf16[1024,768]{1,0:T(8,128)(2,1)}, bf16[1024,256]{1,0:T(8,128)(2,1)}, f32[8,1024]{1,0:T(8,128)}) custom-call(s32[1]{0:T(128)} %bitcast.me, bf16[1024,768]{1,0:T(8,128)(2,1)} %get-tuple-element.233.normed, s32[256,1]{1,0:T(8,128)S(1)} %copy.37.seg_col, s32[1,256]{1,0:T(1,128)S(1)} %bitcast.59, bf16[4,48,768]{2,1,0:T(8,128)(2,1)} %copy-done.2, ...), custom_call_target="tpu_custom_call" | custom-call | flops 8000000000 | bytes 8000000 | tf_op jit(solution)/shard_map/project_attend/pallas_call | solution.py:387
  95.2 12.2 %project_attend.5 = (bf16[1024,768]{1,0:T(8,128)(2,1)}, bf16[1024,256]{1,0:T(8,128)(2,1)}, f32[8,1024]{1,0:T(8,128)}) custom-call(s32[1]{0:T(128)} %bitcast.me, bf16[1024,768]{1,0:T(8,128)(2,1)} %get-tuple-element.233.normed, s32[256,1]{1,0:T(8,128)S(1)} %copy.37.seg_col, s32[1,256]{1,0:T(1,128)S(1)} %bitcast.60, bf16[4,48,768]{2,1,0:T(8,128)(2,1)} %copy-done.2, ...), custom_call_target="tpu_custom_call" | custom-call | flops 8000000000 | bytes 8000000 | tf_op jit(solution)/shard_map/project_attend/pallas_call | solution.py:387
  107.5 1.6 collective-permute-done.26.refs_3_.refs_4_
  109.2 3.9 %collective-permute-done.25.refs_6_.refs_3_.refs_5_ = bf16[4,48,1920]{2,1,0:T(8,128)(2,1)S(1)} collective-permute-done((bf16[4,48,1920]{2,1,0:T(8,128)(2,1)S(1)}, bf16[4,48,1920]{2,1,0:T(8,128)(2,1)S(1)}, u32[]{:S(2)}, u32[]{:S(2)}) %collective-permute-start.25) | collective-permute-done | bytes 737312 | tf_op jit(solution)/shard_map/ppermute | solution.py:1013
  113.7 1.7 collective-permute-done.30.refs_10_.refs_7_.refs_9_
  116.2 6.7 %out_norm.1 = (f32[1024,768]{1,0:T(8,128)}, bf16[1024,768]{1,0:T(8,128)(2,1)S(1)}, bf16[768,1024]{1,0:T(8,128)(2,1)S(1)}) custom-call(s32[1]{0:T(128)} %bitcast.me, bf16[1024,768]{1,0:T(8,128)(2,1)} %get-tuple-element.266.tokens.refs_9_, f32[1,768]{1,0:T(1,128)S(1)} %reshape.119.gain, f32[1,768]{1,0:T(1,128)S(1)} %reshape.120.offset, ...), custom_call_target="tpu_custom_call" | custom-call | flops 3000000000 | bytes 8000000 | tf_op jit(solution)/shard_map/out_norm/pallas_call | solution.py:438
  123.6 14.6 %feed_forward.4 = (f32[1024,768]{1,0:T(8,128)}, f32[1024,768]{1,0:T(8,128)}, bf16[4,4,48,1536]{3,2,1,0:T(8,128)(2,1)}, bf16[4,4,48,1536]{3,2,1,0:T(8,128)(2,1)}) custom-call(s32[1]{0:T(128)} %bitcast.me, bf16[1024,768]{1,0:T(8,128)(2,1)S(1)} %get-tuple-element.274.normed, bf16[768,1024]{1,0:T(8,128)(2,1)S(1)} %get-tuple-element.278.normed_t, ...), custom_call_target="tpu_custom_call" | custom-call | flops 11000000512 | bytes 20000000 | tf_op jit(solution)/shard_map/feed_forward/pallas_call | solution.py:562
  139.9 13.3 %feed_forward.5 = (f32[1024,768]{1,0:T(8,128)}, f32[1024,768]{1,0:T(8,128)}, bf16[4,4,48,1536]{3,2,1,0:T(8,128)(2,1)}, bf16[4,4,48,1536]{3,2,1,0:T(8,128)(2,1)}) custom-call(s32[1]{0:T(128)} %bitcast.me, bf16[1024,768]{1,0:T(8,128)(2,1)S(1)} %get-tuple-element.274.normed, ...), custom_call_target="tpu_custom_call", output_to_operand_aliasing={{2}: (15, {}), {3}: (16, {})} | custom-call | flops 11000000512 | bytes 20000000 | tf_op jit(solution)/shard_map/feed_forward/pallas_call | solution.py:562
  154.0 4.9 %collective-permute-done.35.refs_9_.refs_10_ = bf16[4,48,1536]{2,1,0:T(8,128)(2,1)S(1)} collective-permute-done((bf16[4,48,1536]{2,1,0:T(8,128)(2,1)S(1)}, bf16[4,48,1536]{2,1,0:T(8,128)(2,1)S(1)}, u32[]{:S(2)}, u32[]{:S(2)}) %collective-permute-start.35) | collective-permute-done | bytes 589856 | tf_op jit(solution)/shard_map/ppermute | solution.py:1005
  159.7 13.1 %feed_forward.6 = (f32[1024,768]{1,0:T(8,128)}, f32[1024,768]{1,0:T(8,128)}, bf16[4,4,48,1536]{3,2,1,0:T(8,128)(2,1)}, bf16[4,4,48,1536]{3,2,1,0:T(8,128)(2,1)}) custom-call(s32[1]{0:T(128)} %bitcast.me, bf16[1024,768]{1,0:T(8,128)(2,1)S(1)} %get-tuple-element.274.normed, bf16[768,1024]{1,0:T(8,128)(2,1)S(1)} %get-tuple-element.278.normed_t, ...), custom_call_target="tpu_custom_call" | custom-call | flops 11000000512 | bytes 20000000 | tf_op jit(solution)/shard_map/feed_forward/pallas_call | solution.py:562
  176.4 14.3 %feed_forward.7 = (bf16[1024,768]{1,0:T(8,128)(2,1)}, f32[1024,768]{1,0:T(8,128)}, bf16[4,4,48,1536]{3,2,1,0:T(8,128)(2,1)}, bf16[4,4,48,1536]{3,2,1,0:T(8,128)(2,1)}) custom-call(s32[1]{0:T(128)} %bitcast.me, bf16[1024,768]{1,0:T(8,128)(2,1)S(1)} %get-tuple-element.274.normed, ...), custom_call_target="tpu_custom_call", output_to_operand_aliasing={{2}: (16, {}), {3}: (17, {})} | custom-call | flops 11000000512 | bytes 20000000 | tf_op jit(solution)/shard_map/feed_forward/pallas_call | solution.py:562
  192.8 9.1 %out_back.1 = (f32[1024,768]{1,0:T(8,128)}, bf16[768,1024]{1,0:T(8,128)(2,1)S(1)}, f32[8,768]{1,0:T(8,128)S(1)}, bf16[1024,256]{1,0:T(8,128)(2,1)}, bf16[1024,25...) custom-call(s32[1]{0:T(128)} %bitcast.me, f32[1024,768]{1,0:T(8,128)} %get-tuple-element.309.refs_2_.middle, ...), custom_call_target="tpu_custom_call" | custom-call | flops 4000000000 | bytes 16000000 | tf_op jit(solution)/shard_map/out_back/pallas_call | solution.py:621
  204.9 19.3 %attend_back.3 = (f32[1024,768]{1,0:T(8,128)}, bf16[4,4,48,768]{3,2,1,0:T(8,128)(2,1)}, bf16[4,4,48,768]{3,2,1,0:T(8,128)(2,1)}) custom-call(s32[1]{0:T(128)} %bitcast.me, bf16[768,1024]{1,0:T(8,128)(2,1)} %get-tuple-element.332.normed_t_in, bf16[1024,768]{1,0:T(8,128)(2,1)} %get-tuple-element.333.proj, ...), custom_call_target="tpu_custom_call" | custom-call | flops 12000000000 | bytes 8000000 | tf_op jit(solution)/shard_map/attend_back/pallas_call | solution.py:821
  224.2 2.1 turn_back.1
  229.4 18.5 %attend_back.4 = (f32[1024,768]{1,0:T(8,128)}, bf16[4,4,48,768]{3,2,1,0:T(8,128)(2,1)}, bf16[4,4,48,768]{3,2,1,0:T(8,128)(2,1)}) custom-call(s32[1]{0:T(128)} %bitcast.me, bf16[768,1024]{1,0:T(8,128)(2,1)} %get-tuple-element.332.normed_t_in, bf16[1024,768]{1,0:T(8,128)(2,1)} %get-tuple-element.349.proj, ...), custom_call_target="tpu_custom_call" | custom-call | flops 12000000000 | bytes 8000000 | tf_op jit(solution)/shard_map/attend_back/pallas_call | solution.py:821
  253.5 18.3 %attend_back.5 = (f32[1024,768]{1,0:T(8,128)}, bf16[4,4,48,768]{3,2,1,0:T(8,128)(2,1)}, bf16[4,4,48,768]{3,2,1,0:T(8,128)(2,1)}, f32[8,768]{1,0:T(8,128)S(1)}) custom-call(s32[1]{0:T(128)} %bitcast.me, bf16[768,1024]{1,0:T(8,128)(2,1)} %get-tuple-element.332.normed_t_in, ...), custom_call_target="tpu_custom_call", output_to_operand_aliasing={{1}: (18, {}), {2}: (19, {})} | custom-call | flops 12000000000 | bytes 8000000 | tf_op jit(solution)/shard_map/attend_back/pallas_call | solution.py:821
  276.2 2.9 collective-permute-start.54
  282.6 7.8 %norm_back.1 = (f32[2,512,768]{2,1,0:T(8,128)}, f32[512,768]{1,0:T(8,128)S(1)}) custom-call(s32[1]{0:T(128)S(6)} %select_n.27.start, s32[1]{0:T(128)} %bitcast.2.core, bf16[1024,768]{1,0:T(8,128)(2,1)} %get-tuple-element.266.tokens.refs_9_, f32[1024,768]{1,0:T(8,128)} %get-tuple-element.394.grad_normed, f32[1024,768]{1,0:T(8,128)} %get-tuple-element.395.grad_middle, ...), custom_call_target="tpu_custom_call" | custom-call | flops 4000000000 | bytes 16000000 | tf_op jit(solution)/shard_map/norm_back/pallas_call | solution.py:869
  290.4 2.2 collective-permute-done.54
  292.6 3.4 %collective-permute-done.57.m2 = bf16[208,768]{1,0:T(8,128)(2,1)S(1)} collective-permute-done((bf16[208,768]{1,0:T(8,128)(2,1)S(1)}, bf16[208,768]{1,0:T(8,128)(2,1)S(1)}, u32[]{:S(2)}, u32[]{:S(2)}) %collective-permute-start.57) | collective-permute-done | bytes 319520 | tf_op jit(solution)/shard_map/ppermute | solution.py:1013
  296.8 1.7 collective-permute-start.60
  300.0 3.6 %collective-permute-done.62 = bf16[48,768]{1,0:T(8,128)(2,1)S(1)} collective-permute-done((bf16[48,768]{1,0:T(8,128)(2,1)S(1)}, bf16[48,768]{1,0:T(8,128)(2,1)S(1)}, u32[]{:S(2)}, u32[]{:S(2)}) %collective-permute-start.62) | collective-permute-done | bytes 73760 | tf_op jit(solution)/shard_map/ppermute | solution.py:1013
  305.0 2.4 collective-permute-start.61
  308.0 4.5 %collective-permute-done.61.away = bf16[64,768]{1,0:T(8,128)(2,1)S(1)} collective-permute-done((bf16[64,768]{1,0:T(8,128)(2,1)S(1)}, bf16[64,768]{1,0:T(8,128)(2,1)S(1)}, u32[]{:S(2)}, u32[]{:S(2)}) %collective-permute-start.61) | collective-permute-done | bytes 98336 | tf_op jit(solution)/shard_map/ppermute | solution.py:1013
  (245 shorter events, 61.6 us)
Async XLA Ops:
  2.1 22.0 %collective-permute-start.2 = (bf16[48,1152]{1,0:T(8,128)(2,1)S(1)}, bf16[48,1152]{1,0:T(8,128)(2,1)S(1)}, u32[]{:S(2)}, u32[]{:S(2)}) collective-permute-start(bf16[48,1152]{1,0:T(8,128)(2,1)S(1)} %bitcast_dynamic-update-slice_fusion.refs_0_), channel_id=1, source_target_pairs={{0,24},{2,26},{4,28},{6,30},{8,16},{10,18},{12,20},{14,22},{16,8},... | collective-permute-start | bytes 331784 | tf_op jit(solution)/shard_map/ppermute | solution.py:1013
  7.2 16.9 %collective-permute-start.1 = (bf16[48,1152]{1,0:T(8,128)(2,1)S(1)}, bf16[48,1152]{1,0:T(8,128)(2,1)S(1)}, u32[]{:S(2)}, u32[]{:S(2)}) collective-permute-start(bf16[48,1152]{1,0:T(8,128)(2,1)S(1)} %bitcast_dynamic-update-slice_fusion.refs_0_), channel_id=1, source_target_pairs={{0,16},{2,18},{4,20},{6,22},{8,24},{10,26},{12,28},{14,30},{16,0},... | collective-permute-start | bytes 331784 | tf_op jit(solution)/shard_map/ppermute | solution.py:1013
  7.2 17.0 %collective-permute-start = (bf16[48,1152]{1,0:T(8,128)(2,1)S(1)}, bf16[48,1152]{1,0:T(8,128)(2,1)S(1)}, u32[]{:S(2)}, u32[]{:S(2)}) collective-permute-start(bf16[48,1152]{1,0:T(8,128)(2,1)S(1)} %bitcast_dynamic-update-slice_fusion.refs_0_), channel_id=1, source_target_pairs={{0,8},{2,10},{4,12},{6,14},{8,0},{10,2},{12,4},{14,6},{16,24},{18,... | collective-permute-start | bytes 331784 | tf_op jit(solution)/shard_map/ppermute | solution.py:1013
  27.8 16.4 %collective-permute-start.6 = (bf16[48,3456]{1,0:T(8,128)(2,1)S(1)}, bf16[48,3456]{1,0:T(8,128)(2,1)S(1)}, u32[]{:S(2)}, u32[]{:S(2)}) collective-permute-start(bf16[48,3456]{1,0:T(8,128)(2,1)S(1)} %pack.1.refs_0_), channel_id=1, source_target_pairs={{0,16},{2,18},{4,20},{6,22},{8,24},{10,26},{12,28},{14,30},{16,0},... | collective-permute-start | bytes 995336 | tf_op jit(solution)/shard_map/ppermute | solution.py:1013
  30.1 15.6 %collective-permute-start.9 = (bf16[4,48,384]{2,1,0:T(8,128)(2,1)S(1)}, bf16[4,48,384]{2,1,0:T(8,128)(2,1)S(1)}, u32[]{:S(2)}, u32[]{:S(2)}) collective-permute-start(bf16[4,48,384]{2,1,0:T(8,128)(2,1)S(1)} %get-tuple-element.225.refs_0_), channel_id=1, source_target_pairs={{0,1},{1,0},{2,3},{3,2},{4,5},{5,4},{6,7},{7,6},{8,9},{9,8},{10,11... | collective-permute-start | bytes 442376 | tf_op jit(solution)/shard_map/ppermute | solution.py:1005
  30.1 17.1 %collective-permute-start.11 = (bf16[4,48,384]{2,1,0:T(8,128)(2,1)S(1)}, bf16[4,48,384]{2,1,0:T(8,128)(2,1)S(1)}, u32[]{:S(2)}, u32[]{:S(2)}) collective-permute-start(bf16[4,48,384]{2,1,0:T(8,128)(2,1)S(1)} %collective-permute-done.8.refs_2_), channel_id=1, source_target_pairs={{0,1},{1,0},{2,3},{3,2},{4,5},{5,4},{6,7},{7,6},{8,9},{9,8},{10,11... | collective-permute-start | bytes 442376 | tf_op jit(solution)/shard_map/ppermute | solution.py:1005
  44.2 17.8 %collective-permute-start.13 = (bf16[4,48,768]{2,1,0:T(8,128)(2,1)S(1)}, bf16[4,48,768]{2,1,0:T(8,128)(2,1)S(1)}, u32[]{:S(2)}, u32[]{:S(2)}) collective-permute-start(bf16[4,48,768]{2,1,0:T(8,128)(2,1)S(1)} %get-tuple-element.237.refs_0_), channel_id=1, source_target_pairs={{0,2},{2,0},{4,6},{6,4},{8,10},{10,8},{12,14},{14,12},{16,18},{18,... | collective-permute-start | bytes 884744 | tf_op jit(solution)/shard_map/ppermute | solution.py:1013
  45.7 16.5 %collective-permute-start.14 = (bf16[4,48,768]{2,1,0:T(8,128)(2,1)S(1)}, bf16[4,48,768]{2,1,0:T(8,128)(2,1)S(1)}, u32[]{:S(2)}, u32[]{:S(2)}) collective-permute-start(bf16[4,48,768]{2,1,0:T(8,128)(2,1)S(1)} %get-tuple-element.237.refs_0_), channel_id=1, source_target_pairs={{0,4},{2,6},{4,0},{6,2},{8,12},{10,14},{12,8},{14,10},{16,20},{18,... | collective-permute-start | bytes 884744 | tf_op jit(solution)/shard_map/ppermute | solution.py:1013
  63.5 29.9 %collective-permute-start.22 = (bf16[4,48,1920]{2,1,0:T(8,128)(2,1)S(1)}, bf16[4,48,1920]{2,1,0:T(8,128)(2,1)S(1)}, u32[]{:S(2)}, u32[]{:S(2)}) collective-permute-start(bf16[4,48,1920]{2,1,0:T(8,128)(2,1)S(1)} %get-tuple-element.251.refs_3_.refs_0_.refs_2_), channel_id=1, source_target_pairs={{0,2},{2,0},{4,6},{6,4},{8,10},{10,8},{12,14},{14,12},{16,18},{18,... | collective-permute-start | bytes 2211848 | tf_op jit(solution)/shard_map/ppermute | solution.py:1013
  65.0 28.4 %collective-permute-start.23 = (bf16[4,48,1920]{2,1,0:T(8,128)(2,1)S(1)}, bf16[4,48,1920]{2,1,0:T(8,128)(2,1)S(1)}, u32[]{:S(2)}, u32[]{:S(2)}) collective-permute-start(bf16[4,48,1920]{2,1,0:T(8,128)(2,1)S(1)} %get-tuple-element.251.refs_3_.refs_0_.refs_2_), channel_id=1, source_target_pairs={{0,4},{2,6},{4,0},{6,2},{8,12},{10,14},{12,8},{14,10},{16,20},{18,... | collective-permute-start | bytes 2211848 | tf_op jit(solution)/shard_map/ppermute | solution.py:1013
  66.6 26.9 %collective-permute-start.24 = (bf16[4,48,1920]{2,1,0:T(8,128)(2,1)S(1)}, bf16[4,48,1920]{2,1,0:T(8,128)(2,1)S(1)}, u32[]{:S(2)}, u32[]{:S(2)}) collective-permute-start(bf16[4,48,1920]{2,1,0:T(8,128)(2,1)S(1)} %get-tuple-element.251.refs_3_.refs_0_.refs_2_), channel_id=1, source_target_pairs={{0,1},{1,0},{2,3},{3,2},{4,5},{5,4},{6,7},{7,6},{8,9},{9,8},{10,11... | collective-permute-start | bytes 2211848 | tf_op jit(solution)/shard_map/ppermute | solution.py:1005
  93.5 15.7 %collective-permute-start.26 = (bf16[4,48,1536]{2,1,0:T(8,128)(2,1)S(1)}, bf16[4,48,1536]{2,1,0:T(8,128)(2,1)S(1)}, u32[]{:S(2)}, u32[]{:S(2)}) collective-permute-start(bf16[4,48,1536]{2,1,0:T(8,128)(2,1)S(1)} %get-tuple-element.282.refs_2_.refs_3_), channel_id=1, source_target_pairs={{0,2},{2,0},{4,6},{6,4},{8,10},{10,8},{12,14},{14,12},{16,18},{18,... | collective-permute-start | bytes 1769480 | tf_op jit(solution)/shard_map/ppermute | solution.py:1013
  94.2 18.8 %collective-permute-start.25 = (bf16[4,48,1920]{2,1,0:T(8,128)(2,1)S(1)}, bf16[4,48,1920]{2,1,0:T(8,128)(2,1)S(1)}, u32[]{:S(2)}, u32[]{:S(2)}) collective-permute-start(bf16[4,48,1920]{2,1,0:T(8,128)(2,1)S(1)} %collective-permute-done.22.refs_4_.refs_1_.refs_3_), channel_id=1, source_target_pairs={{0,4},{2,6},{4,0},{6,2},{8,12},{10,14},{12,8},{14,10},{16,20},{18,... | collective-permute-start | bytes 2211848 | tf_op jit(solution)/shard_map/ppermute | solution.py:1013
  94.7 18.3 %collective-permute-start.27 = (bf16[4,48,1920]{2,1,0:T(8,128)(2,1)S(1)}, bf16[4,48,1920]{2,1,0:T(8,128)(2,1)S(1)}, u32[]{:S(2)}, u32[]{:S(2)}) collective-permute-start(bf16[4,48,1920]{2,1,0:T(8,128)(2,1)S(1)} %collective-permute-done.22.refs_4_.refs_1_.refs_3_), channel_id=1, source_target_pairs={{0,1},{1,0},{2,3},{3,2},{4,5},{5,4},{6,7},{7,6},{8,9},{9,8},{10,11... | collective-permute-start | bytes 2211848 | tf_op jit(solution)/shard_map/ppermute | solution.py:1005
  94.9 18.2 %collective-permute-start.28 = (bf16[4,48,1920]{2,1,0:T(8,128)(2,1)S(1)}, bf16[4,48,1920]{2,1,0:T(8,128)(2,1)S(1)}, u32[]{:S(2)}, u32[]{:S(2)}) collective-permute-start(bf16[4,48,1920]{2,1,0:T(8,128)(2,1)S(1)} %collective-permute-done.23.refs_5_.refs_2_.refs_4_), channel_id=1, source_target_pairs={{0,1},{1,0},{2,3},{3,2},{4,5},{5,4},{6,7},{7,6},{8,9},{9,8},{10,11... | collective-permute-start | bytes 2211848 | tf_op jit(solution)/shard_map/ppermute | solution.py:1005
  123.0 15.4 %collective-permute-start.32 = (bf16[4,48,1536]{2,1,0:T(8,128)(2,1)S(1)}, bf16[4,48,1536]{2,1,0:T(8,128)(2,1)S(1)}, u32[]{:S(2)}, u32[]{:S(2)}) collective-permute-start(bf16[4,48,1536]{2,1,0:T(8,128)(2,1)S(1)} %get-tuple-element.282.refs_2_.refs_3_), channel_id=1, source_target_pairs={{0,4},{2,6},{4,0},{6,2},{8,12},{10,14},{12,8},{14,10},{16,20},{18,... | collective-permute-start | bytes 1769480 | tf_op jit(solution)/shard_map/ppermute | solution.py:1013
  153.4 19.4 %collective-permute-start.36 = (bf16[4,4,48,1536]{3,2,1,0:T(8,128)(2,1)}, bf16[4,4,48,1536]{3,2,1,0:T(8,128)(2,1)S(1)}, u32[]{:S(2)}, u32[]{:S(2)}) collective-permute-start(bf16[4,4,48,1536]{3,2,1,0:T(8,128)(2,1)} %get-tuple-element.303), channel_id=1, source_target_pairs={{0,1},{1,0},{2,3},{3,2},{4,5},{5,4},{6,7},{7,6},{8,9},{9,8},{10,11... | collective-permute-start | bytes 7077896 | tf_op jit(solution)/shard_map/ppermute | solution.py:1005
  173.7 17.0 %collective-permute-start.37 = (bf16[2,4,48,768]{3,2,1,0:T(8,128)(2,1)S(1)}, bf16[2,4,48,768]{3,2,1,0:T(8,128)(2,1)S(1)}, u32[]{:S(2)}, u32[]{:S(2)}) collective-permute-start(bf16[2,4,48,768]{3,2,1,0:T(8,128)(2,1)S(1)} %get-tuple-element.313), channel_id=1, source_target_pairs={{0,2},{2,0},{4,6},{6,4},{8,10},{10,8},{12,14},{14,12},{16,18},{18,... | collective-permute-start | bytes 1769480 | tf_op jit(solution)/shard_map/ppermute | solution.py:1013
  174.9 15.8 %collective-permute-start.38 = (bf16[2,4,48,768]{3,2,1,0:T(8,128)(2,1)S(1)}, bf16[2,4,48,768]{3,2,1,0:T(8,128)(2,1)S(1)}, u32[]{:S(2)}, u32[]{:S(2)}) collective-permute-start(bf16[2,4,48,768]{3,2,1,0:T(8,128)(2,1)S(1)} %get-tuple-element.314), channel_id=1, source_target_pairs={{0,4},{2,6},{4,0},{6,2},{8,12},{10,14},{12,8},{14,10},{16,20},{18,... | collective-permute-start | bytes 1769480 | tf_op jit(solution)/shard_map/ppermute | solution.py:1013
  202.6 23.8 %collective-permute-start.42 = (bf16[2,4,48,768]{3,2,1,0:T(8,128)(2,1)S(1)}, bf16[2,4,48,768]{3,2,1,0:T(8,128)(2,1)S(1)}, u32[]{:S(2)}, u32[]{:S(2)}) collective-permute-start(bf16[2,4,48,768]{3,2,1,0:T(8,128)(2,1)S(1)} %get-tuple-element.337), channel_id=1, source_target_pairs={{0,2},{2,0},{4,6},{6,4},{8,10},{10,8},{12,14},{14,12},{16,18},{18,... | collective-permute-start | bytes 1769480 | tf_op jit(solution)/shard_map/ppermute | solution.py:1013
  203.8 22.5 %collective-permute-start.43 = (bf16[2,4,48,768]{3,2,1,0:T(8,128)(2,1)S(1)}, bf16[2,4,48,768]{3,2,1,0:T(8,128)(2,1)S(1)}, u32[]{:S(2)}, u32[]{:S(2)}) collective-permute-start(bf16[2,4,48,768]{3,2,1,0:T(8,128)(2,1)S(1)} %get-tuple-element.338), channel_id=1, source_target_pairs={{0,4},{2,6},{4,0},{6,2},{8,12},{10,14},{12,8},{14,10},{16,20},{18,... | collective-permute-start | bytes 1769480 | tf_op jit(solution)/shard_map/ppermute | solution.py:1013
  227.6 20.3 %collective-permute-start.47 = (bf16[4,4,48,768]{3,2,1,0:T(8,128)(2,1)S(1)}, bf16[4,4,48,768]{3,2,1,0:T(8,128)(2,1)S(1)}, u32[]{:S(2)}, u32[]{:S(2)}) collective-permute-start(bf16[4,4,48,768]{3,2,1,0:T(8,128)(2,1)S(1)} %copy-done.18), channel_id=1, source_target_pairs={{0,1},{1,0},{2,3},{3,2},{4,5},{5,4},{6,7},{7,6},{8,9},{9,8},{10,11... | collective-permute-start | bytes 3538952 | tf_op jit(solution)/shard_map/ppermute | solution.py:1005
  227.6 20.3 %collective-permute-start.44 = (bf16[4,48,768]{2,1,0:T(8,128)(2,1)S(1)}, bf16[4,48,768]{2,1,0:T(8,128)(2,1)S(1)}, u32[]{:S(2)}, u32[]{:S(2)}) collective-permute-start(bf16[4,48,768]{2,1,0:T(8,128)(2,1)S(1)} %fusion.2), channel_id=1, source_target_pairs={{0,4},{2,6},{4,0},{6,2},{8,12},{10,14},{12,8},{14,10},{16,20},{18,... | collective-permute-start | bytes 884744 | tf_op jit(solution)/shard_map/ppermute | solution.py:1013
  228.6 19.4 %collective-permute-start.45 = (bf16[4,48,768]{2,1,0:T(8,128)(2,1)S(1)}, bf16[4,48,768]{2,1,0:T(8,128)(2,1)S(1)}, u32[]{:S(2)}, u32[]{:S(2)}) collective-permute-start(bf16[4,48,768]{2,1,0:T(8,128)(2,1)S(1)} %fusion.3), channel_id=1, source_target_pairs={{0,2},{2,0},{4,6},{6,4},{8,10},{10,8},{12,14},{14,12},{16,18},{18,... | collective-permute-start | bytes 884744 | tf_op jit(solution)/shard_map/ppermute | solution.py:1013
  229.4 18.6 %collective-permute-start.46 = (bf16[512,768]{1,0:T(8,128)(2,1)S(1)}, bf16[512,768]{1,0:T(8,128)(2,1)S(1)}, u32[]{:S(2)}, u32[]{:S(2)}) collective-permute-start(bf16[512,768]{1,0:T(8,128)(2,1)S(1)} %get-tuple-element.354), channel_id=1, source_target_pairs={{0,1},{1,0},{2,3},{3,2},{4,5},{5,4},{6,7},{7,6},{8,9},{9,8},{10,11... | collective-permute-start | bytes 2359304 | tf_op jit(solution)/shard_map/ppermute | solution.py:1005
  248.7 23.2 %collective-permute-start.49 = (bf16[4,48,768]{2,1,0:T(8,128)(2,1)S(1)}, bf16[4,48,768]{2,1,0:T(8,128)(2,1)S(1)}, u32[]{:S(2)}, u32[]{:S(2)}) collective-permute-start(bf16[4,48,768]{2,1,0:T(8,128)(2,1)S(1)} %get-tuple-element.373), channel_id=1, source_target_pairs={{0,2},{2,0},{4,6},{6,4},{8,10},{10,8},{12,14},{14,12},{16,18},{18,... | collective-permute-start | bytes 884744 | tf_op jit(solution)/shard_map/ppermute | solution.py:1013
  250.0 21.9 %collective-permute-start.50 = (bf16[4,48,768]{2,1,0:T(8,128)(2,1)S(1)}, bf16[4,48,768]{2,1,0:T(8,128)(2,1)S(1)}, u32[]{:S(2)}, u32[]{:S(2)}) collective-permute-start(bf16[4,48,768]{2,1,0:T(8,128)(2,1)S(1)} %get-tuple-element.374), channel_id=1, source_target_pairs={{0,4},{2,6},{4,0},{6,2},{8,12},{10,14},{12,8},{14,10},{16,20},{18,... | collective-permute-start | bytes 884744 | tf_op jit(solution)/shard_map/ppermute | solution.py:1013
  251.1 20.8 %collective-permute-start.51 = (bf16[4,48,768]{2,1,0:T(8,128)(2,1)S(1)}, bf16[4,48,768]{2,1,0:T(8,128)(2,1)S(1)}, u32[]{:S(2)}, u32[]{:S(2)}) collective-permute-start(bf16[4,48,768]{2,1,0:T(8,128)(2,1)S(1)} %get-tuple-element.375), channel_id=1, source_target_pairs={{0,6},{2,4},{4,2},{6,0},{8,14},{10,12},{12,10},{14,8},{16,22},{18,... | collective-permute-start | bytes 884744 | tf_op jit(solution)/shard_map/ppermute | solution.py:1013
  252.3 19.7 %collective-permute-start.48 = (bf16[2,48,3072]{2,1,0:T(8,128)(2,1)S(1)}, bf16[2,48,3072]{2,1,0:T(8,128)(2,1)S(1)}, u32[]{:S(2)}, u32[]{:S(2)}) collective-permute-start(bf16[2,48,3072]{2,1,0:T(8,128)(2,1)S(1)} %get-tuple-element.372), channel_id=1, source_target_pairs={{0,8},{2,10},{4,12},{6,14},{8,0},{10,2},{12,4},{14,6},{16,24},{18,... | collective-permute-start | bytes 1769480 | tf_op jit(solution)/shard_map/ppermute | solution.py:1013
  276.2 16.4 %collective-permute-start.54 = (bf16[48,3072]{1,0:T(8,128)(2,1)S(1)}, bf16[48,3072]{1,0:T(8,128)(2,1)S(1)}, u32[]{:S(2)}, u32[]{:S(2)}) collective-permute-start(bf16[48,3072]{1,0:T(8,128)(2,1)S(1)} %fusion.7), channel_id=1, source_target_pairs={{0,16},{2,18},{4,20},{6,22},{8,24},{10,26},{12,28},{14,30},{16,0},... | collective-permute-start | bytes 884744 | tf_op jit(solution)/shard_map/ppermute | solution.py:1013
  280.3 15.7 %collective-permute-start.57 = (bf16[208,768]{1,0:T(8,128)(2,1)S(1)}, bf16[208,768]{1,0:T(8,128)(2,1)S(1)}, u32[]{:S(2)}, u32[]{:S(2)}) collective-permute-start(bf16[208,768]{1,0:T(8,128)(2,1)S(1)} %get-tuple-element.401), channel_id=1, source_target_pairs={{0,4},{2,6},{4,0},{6,2},{8,12},{10,14},{12,8},{14,10},{16,20},{18,... | collective-permute-start | bytes 958472 | tf_op jit(solution)/shard_map/ppermute | solution.py:1013
  296.1 17.8 %collective-permute-start.59 = (f32[512,768]{1,0:T(8,128)S(1)}, f32[512,768]{1,0:T(8,128)S(1)}, u32[]{:S(2)}, u32[]{:S(2)}) collective-permute-start(f32[512,768]{1,0:T(8,128)S(1)} %get-tuple-element.403), channel_id=1, source_target_pairs={{0,1},{1,0},{2,3},{3,2},{4,5},{5,4},{6,7},{7,6},{8,9},{9,8},{10,11... | collective-permute-start | bytes 4718600 | tf_op jit(solution)/shard_map/ppermute | solution.py:1005
  (78 other events, 770.5 us)

commit v2 on v1

--- a/solution.py
+++ b/solution.py
@@ -161,37 +161,16 @@
     return centered * root, root
 
 
-def prepare_body(
-    start,
-    core,
-    own,
-    other,
-    cot_own,
-    cot_other,
-    gain,
-    offset,
-    x_out,
-    normed_out,
-    normed_t_out,
-    cot_out,
-    cot_t_out,
-    double,
-    cot_double,
-    x,
-    normed,
-    normed_t,
-    cot,
-    cot_t,
-    sems,
-):
+def start_double(double, core, own, other, sem):
     here = own.shape[1]
-    mine = core[0]
-    for buf, halves, sem in ((double, (own, other), 5), (cot_double, (cot_own, cot_other), 6)):
-        for k in range(4):
-            pltpu.make_async_copy(
-                halves[k % 2].at[mine], buf.at[pl.ds(k * here, here)], sems.at[sem]
-            ).start()
-    wait_bytes(double, sems.at[5])
+    halves = (own, other)
+    for k in range(4):
+        pltpu.make_async_copy(halves[k % 2].at[core], double.at[pl.ds(k * here, here)], sem).start()
+
+
+def prepare_body(start, core, own, other, gain, offset, x_out, normed_out, normed_t_out, double, x, normed, normed_t, sems):
+    start_double(double, core[0], own, other, sems.at[3])
+    wait_bytes(double, sems.at[3])
 
     def step(r, carry):
         at = pl.ds(pl.multiple_of(r * QB, QB), QB)
@@ -203,47 +182,71 @@
         normed_t[:, at] = low.T
         return carry
 
-    count = x.shape[0] // QB
-    lax.fori_loop(0, count, step, 0)
+    lax.fori_loop(0, x.shape[0] // QB, step, 0)
     copies = [
         pltpu.make_async_copy(normed, normed_out, sems.at[0]),
         pltpu.make_async_copy(x, x_out, sems.at[1]),
         pltpu.make_async_copy(normed_t, normed_t_out, sems.at[2]),
-        pltpu.make_async_copy(cot, cot_out, sems.at[3]),
-        pltpu.make_async_copy(cot_t, cot_t_out, sems.at[4]),
     ]
-    start_all(copies[:3])
-    wait_bytes(cot_double, sems.at[6])
-
-    def second(r, carry):
+    start_all(copies)
+    for copy in copies:
+        copy.wait()
+
+
+def prepare(start, core, own, other, gain, offset):
+    _, here, depth = own.shape
+    shape, shape_t = (2 * here, depth), (depth, 2 * here)
+    shapes = [shape, shape, shape_t]
+    return pl.pallas_call(
+        prepare_body,
+        in_specs=[smem_spec()] * 2 + [any_spec()] * 2 + [vmem_spec()] * 2,
+        out_specs=[any_spec()] * 3,
+        out_shape=[pltpu.HBM(s, BF) for s in shapes],
+        scratch_shapes=[pltpu.VMEM((4 * here, depth), BF)]
+        + [pltpu.VMEM(s, BF) for s in shapes]
+        + [pltpu.SemaphoreType.DMA((4,))],
+        compiler_params=params(20),
+        cost_estimate=cost(4, 8),
+        name="prepare",
+    )(start, core, *in_hbm([own, other]), gain, offset)
+
+
+def turn_body(start, core, own, other, cot_out, cot_t_out, double, cot, cot_t, sems):
+    start_double(double, core[0], own, other, sems.at[2])
+    wait_bytes(double, sems.at[2])
+
+    def step(r, carry):
         at = pl.ds(pl.multiple_of(r * QB, QB), QB)
-        low = turned([cot_double], start[0], r).astype(BF)
+        low = turned([double], start[0], r).astype(BF)
         cot[at, :] = low
         cot_t[:, at] = low.T
         return carry
 
-    lax.fori_loop(0, count, second, 0)
-    start_all(copies[3:])
+    lax.fori_loop(0, cot.shape[0] // QB, step, 0)
+    copies = [
+        pltpu.make_async_copy(cot, cot_out, sems.at[0]),
+        pltpu.make_async_copy(cot_t, cot_t_out, sems.at[1]),
+    ]
+    start_all(copies)
     for copy in copies:
         copy.wait()
 
 
-def prepare(start, core, own, other, cot_own, cot_other, gain, offset):
+def turn(start, core, own, other):
     _, here, depth = own.shape
-    shape, shape_t = (2 * here, depth), (depth, 2 * here)
-    shapes = [shape, shape, shape_t, shape, shape_t]
+    shapes = [(2 * here, depth), (depth, 2 * here)]
     return pl.pallas_call(
-        prepare_body,
-        in_specs=[smem_spec()] * 2 + [any_spec()] * 4 + [vmem_spec()] * 2,
-        out_specs=[any_spec()] * 5,
+        turn_body,
+        in_specs=[smem_spec()] * 2 + [any_spec()] * 2,
+        out_specs=[any_spec()] * 2,
         out_shape=[pltpu.HBM(s, BF) for s in shapes],
-        scratch_shapes=[pltpu.VMEM((4 * here, depth), BF)] * 2
+        scratch_shapes=[pltpu.VMEM((4 * here, depth), BF)]
         + [pltpu.VMEM(s, BF) for s in shapes]
-        + [pltpu.SemaphoreType.DMA((7,))],
-        compiler_params=params(28),
+        + [pltpu.SemaphoreType.DMA((3,))],
+        compiler_params=params(16),
         cost_estimate=cost(4, 8),
-        name="prepare",
-    )(start, core, *in_hbm([own, other, cot_own, cot_other]), gain, offset)
+        name="turn",
+    )(start, core, *in_hbm([own, other]))
 
 
 def turn_back_body(start, core, values, held, other, double, own, sem):
@@ -325,15 +328,19 @@
     )(me, *pieces)
 
 
-def project_attend_body(piece, me, normed, seg_col, seg_row, *refs):
+def project_attend_body(piece, me, normed_in, seg_col, seg_row, *refs):
     slabs = refs[: piece.count]
-    proj_out, att, lse, weight, proj, bias, keys_m, values_t, att_t, sem, out_sem = refs[piece.count :]
+    proj_out, att, lse, weight, proj, normed, bias, keys_m, values_t, att_t, sem, out_sem = refs[
+        piece.count :
+    ]
+    normed_copy = pltpu.make_async_copy(normed_in, normed, out_sem)
+    normed_copy.start()
     moves = [(half, 0, 384, weight.at[:, :, :, pl.ds(384 * half, 384)]) for half in range(2)]
     start_all(piece_copies(piece, me[0], slabs, moves, sem, False))
     fill_bias(bias, seg_col, seg_row)
     values_t[...] = jnp.ones_like(values_t)
+    normed_copy.wait()
     wait_bytes(weight, sem)
-    length = normed.shape[0]
 
     for c in range(3):
         cols = slice(c * 256, c * 256 + 256)
@@ -386,7 +393,7 @@
     rows = piece.rows
     return pl.pallas_call(
         functools.partial(project_attend_body, piece),
-        in_specs=[smem_spec()] + [vmem_spec()] * 3 + [any_spec()] * len(slabs),
+        in_specs=[smem_spec(), any_spec()] + [vmem_spec()] * 2 + [any_spec()] * len(slabs),
         out_specs=[any_spec()] + [vmem_spec()] * 2,
         out_shape=[
             pltpu.HBM((length, 768), BF),
@@ -396,6 +403,7 @@
         scratch_shapes=[
             pltpu.VMEM(rows.shape + (768,), BF),
             pltpu.VMEM((length, 768), BF),
+            pltpu.VMEM((length, depth), BF),
             pltpu.VMEM((2, QB, QB), F32),
             pltpu.VMEM((4, length, 128), BF),
             pltpu.VMEM((8, HD + 16, length), BF),
@@ -469,15 +477,33 @@
     return values * below, below + values * density
 
 
-def feed_forward_body(piece, out_piece, first, final, aliased, me, normed, normed_t, cot, cot_t, *refs):
+def norm_pull(grad, hat, root, gain):
+    scaled = grad * gain
+    first = jnp.mean(scaled, axis=-1, keepdims=True)
+    second = jnp.mean(scaled * hat, axis=-1, keepdims=True)
+    return root * (scaled - first - hat * second)
+
+
+def feed_forward_body(
+    piece, out_piece, first, last_piece, groups, aliased, me, normed, normed_t, cot, cot_t, *refs
+):
     refs = list(refs)
+    final = last_piece is not None
     held = [] if first else [refs.pop(0), refs.pop(0)]
-    middle = refs.pop(0) if final else None
+    if final:
+        middle, gain = refs.pop(0), refs.pop(0)
+        out_slabs, refs = refs[: last_piece.count], refs[last_piece.count :]
     slabs, refs = refs[: piece.count], refs[piece.count + aliased :]
-    mixed, grad_in = refs[:2]
-    outs, refs = refs[2:4], refs[4:]
+    outs, refs = refs[:2], refs[2:]
+    mixed = refs.pop(0)
+    if final:
+        grad_middle_out, branch_t, sums = refs[:3]
+        grad_att, refs = refs[3 : 3 + groups], refs[3 + groups :]
+    else:
+        grad_in = refs.pop(0)
     weight, staged, act, grad_hidden, mixed_acc, grad_acc, sems = refs[:7]
-    mixed_low, middle_here = refs[7:] if final else (None, None)
+    if final:
+        mixed_low, middle_here, out_weight, grad_middle = refs[7:]
     length, depth = normed.shape
     moves = []
     for half in range(2):
@@ -494,6 +520,12 @@
     if final:
         held_copies.append(pltpu.make_async_copy(middle, middle_here, sems.at[4]))
     start_all(held_copies)
+    if final:
+        width = depth // 2
+        views = [
+            (half, 0, width, out_weight.at[:, :, :, pl.ds(width * half, width)]) for half in range(2)
+        ]
+        start_all(piece_copies(last_piece, me[0], out_slabs, views, sems.at[5], False))
     wait_bytes(weight, sems.at[0])
     chunks = [slice(c * 256, c * 256 + 256) for c in range(3)]
 
@@ -522,11 +554,37 @@
         else:
             mixed_acc[:, cols] = mixed_part
         grad_acc[:, cols] = grad_part
-    out_copies = [
-        pltpu.make_async_copy(mixed_low if final else mixed_acc, mixed, sems.at[1]),
-        pltpu.make_async_copy(grad_acc, grad_in, sems.at[2]),
-    ]
-    start_all(out_copies)
+    if final:
+        out_copies = [pltpu.make_async_copy(mixed_low, mixed, sems.at[1])]
+        start_all(out_copies)
+        wait_bytes(out_weight, sems.at[5])
+        sums[...] = jnp.zeros_like(sums)
+
+        def back_step(r, carry):
+            at = pl.ds(pl.multiple_of(r * QB, QB), QB)
+            hat, root = norm_parts(middle_here[at, :])
+            grad = grad_acc[at, :]
+            value = cot[at, :].astype(F32) + norm_pull(grad, hat, root, gain[...])
+            grad_middle[at, :] = value
+            low = value.astype(BF)
+            branch_t[:, at] = low.T
+            sums[0:1, :] += jnp.sum(grad * hat, axis=0, keepdims=True)
+            sums[1:2, :] += jnp.sum(grad, axis=0, keepdims=True)
+            back = nn(low, flat(out_weight[...])).astype(BF)
+            for g in range(groups):
+                grad_att[g][at, 0:128] = back[:, g * 128 : g * 128 + 128]
+                grad_att[g][at, 128:256] = back[:, width + g * 128 : width + g * 128 + 128]
+            return carry
+
+        lax.fori_loop(0, length // QB, back_step, 0)
+        out_copies.append(pltpu.make_async_copy(grad_middle, grad_middle_out, sems.at[2]))
+        out_copies[-1].start()
+    else:
+        out_copies = [
+            pltpu.make_async_copy(mixed_acc, mixed, sems.at[1]),
+            pltpu.make_async_copy(grad_acc, grad_in, sems.at[2]),
+        ]
+        start_all(out_copies)
     for c in range(3):
         cols = slice(c * 256, c * 256 + 256)
         up = nn(normed_t[...], grad_hidden[:, cols]).astype(BF)
@@ -539,15 +597,14 @@
     wait_bytes(staged, sems.at[3])
 
 
-def feed_forward(piece, out_piece, me, normed, normed_t, cot, cot_t, held, middle, slabs, onto):
+def feed_forward(
+    piece, out_piece, me, normed, normed_t, cot, cot_t, held, slabs, onto, last=None
+):
     length, depth = normed.shape
     rows = piece.rows
-    first, final = held is None, middle is not None
+    first, final = held is None, last is not None
     ins = [me] + in_vmem([normed, normed_t, cot, cot_t]) + ([] if first else in_hbm(held))
     specs = [smem_spec()] + [vmem_spec()] * 4 + [any_spec()] * (0 if first else 2)
-    if final:
-        ins += in_hbm([middle])
-        specs.append(any_spec())
     scratch = [
         pltpu.VMEM(rows.shape + (1536,), BF),
         pltpu.VMEM(rows.shape + (1536,), BF),
@@ -555,82 +612,41 @@
         pltpu.VMEM((length, 768), BF),
         pltpu.VMEM((length, depth), F32),
         pltpu.VMEM((length, depth), F32),
-        pltpu.SemaphoreType.DMA((5,)),
+        pltpu.SemaphoreType.DMA((6,)),
     ]
+    last_piece, groups = None, 0
+    outs = [pltpu.HBM(out_piece.shape, BF)] * 2 + [pltpu.HBM((length, depth), BF if final else F32)]
+    out_specs = [any_spec()] * 3
     if final:
-        scratch += [pltpu.VMEM((length, depth), BF), pltpu.VMEM((length, depth), F32)]
+        last_piece, last_slabs, middle, gain, groups = last
+        ins += in_hbm([middle]) + [gain] + in_hbm(last_slabs)
+        specs += [any_spec(), vmem_spec()] + [any_spec()] * len(last_slabs)
+        scratch += [
+            pltpu.VMEM((length, depth), BF),
+            pltpu.VMEM((length, depth), F32),
+            pltpu.VMEM(rows.shape + (depth,), BF),
+            pltpu.VMEM((length, depth), F32),
+        ]
+        outs += [pltpu.HBM((length, depth), F32), pltpu.VMEM((depth, length), BF), SDS((8, depth), F32)]
+        outs += [pltpu.HBM((length, 256), BF)] * groups
+        out_specs += [any_spec()] + [vmem_spec()] * (2 + groups)
+    else:
+        outs.append(pltpu.HBM((length, depth), F32))
+        out_specs.append(any_spec())
     got = pl.pallas_call(
-        functools.partial(feed_forward_body, piece, out_piece, first, final, len(onto)),
+        functools.partial(
+            feed_forward_body, piece, out_piece, first, last_piece, groups, len(onto)
+        ),
         in_specs=specs + [any_spec()] * (piece.count + len(onto)),
-        out_specs=[any_spec()] * 4,
-        out_shape=[pltpu.HBM((length, depth), BF if final else F32), pltpu.HBM((length, depth), F32)]
-        + [pltpu.HBM(out_piece.shape, BF)] * 2,
-        input_output_aliases={len(ins) + piece.count + k: 2 + k for k in range(len(onto))},
+        out_specs=out_specs,
+        out_shape=outs,
+        input_output_aliases={len(ins) + piece.count + k: k for k in range(len(onto))},
         scratch_shapes=scratch,
-        compiler_params=params(40),
-        cost_estimate=cost(11, 20),
+        compiler_params=params(48 if final else 32),
+        cost_estimate=cost(14 if final else 11, 20),
         name="feed_forward",
     )(*ins, *in_hbm(slabs), *in_hbm(onto))
-    return got[0], got[1], got[2:]
-
-
-def norm_pull(grad, hat, root, gain):
-    scaled = grad * gain
-    first = jnp.mean(scaled, axis=-1, keepdims=True)
-    second = jnp.mean(scaled * hat, axis=-1, keepdims=True)
-    return root * (scaled - first - hat * second)
-
-
-def add_sums(sums, grad, hat):
-    @pl.when(pl.program_id(0) == 0)
-    def _():
-        sums[...] = jnp.zeros_like(sums)
-
-    sums[0:1, :] += jnp.sum(grad * hat, axis=0, keepdims=True)
-    sums[1:2, :] += jnp.sum(grad, axis=0, keepdims=True)
-
-
-def out_back_body(piece, groups, me, middle, grad_in, cot, gain, *refs):
-    slabs, refs = refs[: piece.count], refs[piece.count :]
-    grad_middle, branch_t, sums = refs[:3]
-    grad_att = refs[3 : 3 + groups]
-    weight, sem = refs[3 + groups :]
-    width = weight.shape[3] // 2
-
-    @pl.when(pl.program_id(0) == 0)
-    def _():
-        moves = [(half, 0, width, weight.at[:, :, :, pl.ds(width * half, width)]) for half in range(2)]
-        start_all(piece_copies(piece, me[0], slabs, moves, sem, False))
-        wait_bytes(weight, sem)
-
-    hat, root = norm_parts(middle[...])
-    grad = grad_in[...]
-    value = cot[...].astype(F32) + norm_pull(grad, hat, root, gain[...])
-    grad_middle[...] = value
-    low = value.astype(BF)
-    branch_t[...] = low.T
-    add_sums(sums, grad, hat)
-    back = nn(low, flat(weight[...])).astype(BF)
-    for g in range(groups):
-        grad_att[g][:, 0:128] = back[:, g * 128 : g * 128 + 128]
-        grad_att[g][:, 128:256] = back[:, width + g * 128 : width + g * 128 + 128]
-
-
-def out_back(piece, groups, me, middle, grad_in, cot, gain, slabs):
-    length, depth = middle.shape
-    got = pl.pallas_call(
-        functools.partial(out_back_body, piece, groups),
-        grid=(length // 512,),
-        in_specs=[smem_spec()] + [row_spec(depth)] * 3 + [whole_spec((1, depth))] + [any_spec()] * len(slabs),
-        out_specs=[row_spec(depth), column_spec(depth), whole_spec((8, depth))] + [row_spec(256)] * groups,
-        out_shape=[pltpu.HBM((length, depth), F32), pltpu.VMEM((depth, length), BF), SDS((8, depth), F32)]
-        + [pltpu.HBM((length, 256), BF)] * groups,
-        scratch_shapes=[pltpu.VMEM(piece.rows.shape + (depth,), BF), pltpu.SemaphoreType.DMA],
-        compiler_params=params(28),
-        cost_estimate=cost(4, 16),
-        name="out_back",
-    )(me, *in_hbm([middle, grad_in]), *in_vmem([cot]), gain, *in_hbm(slabs))
-    return got[0], got[1], got[2], got[3:]
+    return got[:2], got[2:]
 
 
 def attend_back_body(piece, out_piece, extra, aliased, final, me, normed_t_in, proj, att, grad_att, lse, seg_col, seg_row, *refs):
@@ -1143,15 +1159,18 @@
     def via(mask):
         return functools.partial(hop, mask=mask, count=dp_count)
 
-    def fetch_wide(widths, shard, away):
+    def fetch_wide(shard, away):
         near, both_ways = yield [(shard, via(4)), (away, via(4))]
-        a0, c0 = arrange(rows, flow.me, [shard, near, away, both_ways], widths)
-        a1, a2, b0 = yield [(a0, via(1)), (a0, via(2))] + swaps([a0])
-        a3, c1, b1, b2, d0 = yield [(a1, via(2)), (c0, via(1))] + swaps([a1, a2, c0])
+        (a0,) = arrange(rows, flow.me, [shard, near, away, both_ways], [shard.shape[1]])
+        a1, a2, b0, away = yield [(a0, via(1)), (a0, via(2))] + swaps([a0]) + [(shard_c, via(8))]
+        a3, b1, b2, near, both_ways = yield (
+            [(a1, via(2))] + swaps([a1, a2]) + [(shard_c, via(4)), (away, via(4))]
+        )
         slabs["a"] = [a0, a1, a2, a3, b0, b1, b2, swap(a3)]
-        (d1,) = yield swaps([c1])
-        (c2,) = yield [(c0, via(2))]
-        c3, d2 = yield [(c2, via(1))] + swaps([c2])
+        (c0,) = arrange(rows, flow.me, [shard_c, near, away, both_ways], [shard_c.shape[1]])
+        (d0,) = yield swaps([c0])
+        c1, c2 = yield [(c0, via(1)), (c0, via(2))]
+        c3, d1, d2 = yield [(c2, via(1))] + swaps([c1, c2])
         return [c0, c1, c2, c3, d0, d1, d2, swap(c3)]
 
     def whole(shard):
@@ -1231,20 +1250,21 @@
     if rows.split:
         shard_q = shards["q"]
         got = send_all(far_hops(rows, [shard_q] * (rows.far - 1)))
-        prepared = prepare(start, core_place, *token_halves, *cot_halves, gain1, bias1)
+        prepared = prepare(start, core_place, *token_halves, gain1, bias1)
         tied = tie(*got, *prepared, shard_a)
-        got, prepared, shard_a = tied[:3], tied[3:8], tied[8]
+        got, prepared, shard_a = tied[:3], tied[3:6], tied[6]
         near_q0, near_q1 = arrange(rows, me, [shard_q] + list(got), [part, wide])
         own = [near_q0] + [hop(near_q0, m, dp_count) for m in MASKS[1:]]
+        first_cols = part + wide * cut
+        shard_c, shard_a = shard_a[:, first_cols:], shard_a[:, :first_cols]
         away_a = hop(shard_a, 8, dp_count)
-        slabs["q0"] = own + [swap(v) for v in own]
+        start_cot, _ = tie(start, near_q0)
+        turned_cot = turn(start_cot, core_place, *cot_halves)
+        tied = tie(*own, *turned_cot)
+        own, turned_cot = tied[:4], tied[4:]
+        slabs["q0"] = list(own) + [swap(v) for v in own]
         flow.add(fetch_near, "q1", slabs, [near_q1])
-        flow.add(
-            functools.partial(fetch_wide, [part + wide * cut, wide * (subs - cut)]),
-            "c",
-            slabs,
-            [shard_a, away_a],
-        )
+        flow.add(fetch_wide, "c", slabs, [shard_a, away_a])
         flow.step(own[3])
     else:
         for name, shard in (
@@ -1254,8 +1274,10 @@
             ("c", shard_a[:, part + wide * cut :]),
         ):
             slabs[name] = whole(shard)
-        prepared = prepare(start, core_place, *token_halves, *cot_halves, gain1, bias1)
-    x, normed, normed_t, cot, cot_t = prepared
+        prepared = prepare(start, core_place, *token_halves, gain1, bias1)
+        turned_cot = turn(start, core_place, *cot_halves)
+    x, normed, normed_t = prepared
+    cot, cot_t = turned_cot
     for g in range(groups):
         project(g)
         flow.step(forward[g][2])
@@ -1270,7 +1292,8 @@
     onto = []
     feed_names = ["a"] * cut + ["c"] * (subs - cut)
     for s in range(subs):
-        mixed, grad_in, grads = feed_forward(
+        final = s == subs - 1
+        grads, held = feed_forward(
             feed_pieces[s],
             feed_outs[s],
             flow.me,
@@ -1279,11 +1302,10 @@
             cot,
             cot_t,
             held,
-            middle if s == subs - 1 else None,
             slabs[feed_names[s]],
             onto,
+            (out_piece, slabs["a"], middle, gain2, groups) if final else None,
         )
-        held = (mixed, grad_in)
         onto = grads
         if s % cut == cut - 1:
             k = s // cut
@@ -1294,10 +1316,9 @@
             else:
                 sums_of[k] = plain(*grads)
             onto = []
-        flow.step(grad_in)
-    grad_middle, branch_t, sums2, grad_atts = out_back(
-        out_piece, groups, flow.me, middle, grad_in, cot, gain2, slabs["a"]
-    )
+        if not final:
+            flow.step(held[1])
+    mixed, grad_middle, branch_t, sums2, *grad_atts = held
     mixed, core_place, _ = flow.step(mixed, core_place, sums2)
     mixed_held, mixed_other = turn_back(back, core_place, mixed)
     flow.add(exchange, "mixed", sums_of, [mixed_other])

time: 320 us -> 311 us (0.972)
  waiting for transfers between devices: 41.7 us -> 33.4 us
  Pallas kernels: 200 us -> 195 us
    ppermute x38 -> x41, waiting for transfers between devices: 33.8 us -> 25.9 us  [hop(): return lax.ppermute(value, 'dp', [(i, i ^ mask) for i in range(count)])]
    pallas_call x4, Pallas kernels: 55.4 us -> 59.7 us  [feed_forward(): pl.pallas_call(functools.partial(feed_forward_body, piece, out_piece, fir...]
    pallas_call x1, Pallas kernels: 9.05 us -> 5.34 us  [turn(): pl.pallas_call(turn_body, in_specs=[smem_spec()] * 2 + [any_spec()] * 2,...]
    pallas_call x3, Pallas kernels: 49.7 us -> 46.5 us  [project_attend(): pl.pallas_call(functools.partial(project_attend_body, piece), in_specs=[s...]
    ppermute x38 -> x41, starting transfers between devices: 48.4 us -> 50.2 us  [hop(): return lax.ppermute(value, 'dp', [(i, i ^ mask) for i in range(count)])]
    unnamed x97 -> x99, local copies, waits for them, and re-layouts: 9.01 us -> 9.92 us
  transfers between devices with their start and end apart: 63 -> 66, of which waited for: 17 -> 11; matrix products, arithmetic and copies ran while one was open for 2% -> 2% of each run, Pallas kernels for 63% -> 63%
where the time goes in v2:
time: 311 us; the launch traced here: 306 us
  Pallas kernels  195 us (63%)
  starting transfers between devices  54.9 us (18%)
  waiting for transfers between devices  33.4 us (11%)
  local copies, waits for them, and re-layouts  13.5 us (4%)
  other arithmetic  5.17 us (2%)
  between operations  3.89 us (1%)
    pallas_call x4, Pallas kernels, feed_forward(): pl.pallas_call(functools.partial(feed_forward_body, piece, out_piece, fir...  59.7 us
    pallas_call x3, Pallas kernels, attend_back(): pl.pallas_call(functools.partial(attend_back_body, piece, out_piece, extr...  56.3 us
    ppermute x41, starting transfers between devices, hop(): return lax.ppermute(value, 'dp', [(i, i ^ mask) for i in range(count)])  50.2 us
    pallas_call x3, Pallas kernels, project_attend(): pl.pallas_call(functools.partial(project_attend_body, piece), in_specs=[s...  46.5 us
    ppermute x41, waiting for transfers between devices, hop(): return lax.ppermute(value, 'dp', [(i, i ^ mask) for i in range(count)])  25.9 us
    unnamed x99, local copies, waits for them, and re-layouts  9.92 us
    pallas_call x1, Pallas kernels, norm_back(): pl.pallas_call(norm_back_body, grid=(length // QB,), in_specs=[smem_spec(...  7.76 us
    ppermute x25, waiting for transfers between devices, swap(): return lax.ppermute(value, 'mp', [(0, 1), (1, 0)])  7.46 us
  transfers between devices with their start and end apart: 66, of which 11 were waited for; matrix products, arithmetic and copies ran while one was open for 2% of the time, Pallas kernels for 63%

profile of v2, /device:TPU:0, one launch (start us, length us, event | category | flops | bytes accessed | tf_op | source)
XLA Modules:
  0.0 306.2 jit_solution(12241513463930550474)
XLA Ops:
  2.1 5.1 %collective-permute-start.2 = (bf16[48,1152]{1,0:T(8,128)(2,1)S(1)}, bf16[48,1152]{1,0:T(8,128)(2,1)S(1)}, u32[]{:S(2)}, u32[]{:S(2)}) collective-permute-start(bf16[48,1152]{1,0:T(8,128)(2,1)S(1)} %bitcast_dynamic-update-slice_fusion.refs_0_), channel_id=1, source_target_pairs={{0,24},{2,26},{4,28},{6,30},{8,16},{10,18},{12,20},{14,22},{16,8},... | collective-permute-start | bytes 331784 | tf_op jit(solution)/shard_map/ppermute | solution.py:1029
  14.0 6.8 %prepare.1 = (bf16[1024,768]{1,0:T(8,128)(2,1)}, bf16[1024,768]{1,0:T(8,128)(2,1)}, bf16[768,1024]{1,0:T(8,128)(2,1)}) custom-call(s32[1]{0:T(128)} %bitcast.1.start, s32[1]{0:T(128)} %bitcast.2.core, bf16[2,512,768]{2,1,0:T(8,128)(2,1)} %bitcast.70, bf16[2,512,768]{2,1,0:T(8,128)(2,1)} %collective-permute-done.3.other, f32[1,768]{1,0:T(1,128)S(1)} %reshape.115.gain, ...), custom_call_target="tpu_custom_call" | custom-call | flops 4000000000 | bytes 8000000 | tf_op jit(solution)/shard_map/prepare/pallas_call | solution.py:200
  20.9 2.7 collective-permute-start.6
  24.5 2.4 collective-permute-start.8
  28.0 5.3 %turn.1 = (bf16[1024,768]{1,0:T(8,128)(2,1)}, bf16[768,1024]{1,0:T(8,128)(2,1)}) custom-call(s32[1]{0:T(128)} %bitcast.1.start, s32[1]{0:T(128)} %bitcast.2.core, bf16[2,512,768]{2,1,0:T(8,128)(2,1)} %bitcast.72, bf16[2,512,768]{2,1,0:T(8,128)(2,1)} %copy-done.18), custom_call_target="tpu_custom_call" | custom-call | flops 4000000000 | bytes 8000000 | tf_op jit(solution)/shard_map/turn/pallas_call | solution.py:238
  36.0 2.1 collective-permute-start.16
  39.7 1.6 collective-permute-start.14
  42.0 11.2 %project_attend.3 = (bf16[1024,768]{1,0:T(8,128)(2,1)}, bf16[1024,256]{1,0:T(8,128)(2,1)}, f32[8,1024]{1,0:T(8,128)}) custom-call(s32[1]{0:T(128)} %bitcast.me, bf16[1024,768]{1,0:T(8,128)(2,1)} %get-tuple-element.241.normed_in, s32[256,1]{1,0:T(8,128)S(1)} %copy.37.seg_col, s32[1,256]{1,0:T(1,128)S(1)} %bitcast.58, bf16[4,48,384]{2,1,0:T(8,128)(2,1)} %copy-done.6, ...), custom_call_target="tpu_custom_call" | custom-call | flops 8000000000 | bytes 8000000 | tf_op jit(solution)/shard_map/project_attend/pallas_call | solution.py:394
  59.6 24.2 %project_attend.4 = (bf16[1024,768]{1,0:T(8,128)(2,1)}, bf16[1024,256]{1,0:T(8,128)(2,1)}, f32[8,1024]{1,0:T(8,128)}) custom-call(s32[1]{0:T(128)} %bitcast.me, bf16[1024,768]{1,0:T(8,128)(2,1)} %get-tuple-element.241.normed_in, s32[256,1]{1,0:T(8,128)S(1)} %copy.37.seg_col, s32[1,256]{1,0:T(1,128)S(1)} %bitcast.59, bf16[4,48,768]{2,1,0:T(8,128)(2,1)} %copy-done.3, ...), custom_call_target="tpu_custom_call" | custom-call | flops 8000000000 | bytes 8000000 | tf_op jit(solution)/shard_map/project_attend/pallas_call | solution.py:394
  83.8 1.6 collective-permute-start.29
  87.1 11.2 %project_attend.5 = (bf16[1024,768]{1,0:T(8,128)(2,1)}, bf16[1024,256]{1,0:T(8,128)(2,1)}, f32[8,1024]{1,0:T(8,128)}) custom-call(s32[1]{0:T(128)} %bitcast.me, bf16[1024,768]{1,0:T(8,128)(2,1)} %get-tuple-element.241.normed_in, s32[256,1]{1,0:T(8,128)S(1)} %copy.37.seg_col, s32[1,256]{1,0:T(1,128)S(1)} %bitcast.60, bf16[4,48,768]{2,1,0:T(8,128)(2,1)} %copy-done.3, ...), custom_call_target="tpu_custom_call" | custom-call | flops 8000000000 | bytes 8000000 | tf_op jit(solution)/shard_map/project_attend/pallas_call | solution.py:394
  98.4 5.2 %collective-permute-done.26.refs_6_.refs_3_.refs_5_.refs_7_ = bf16[4,48,1920]{2,1,0:T(8,128)(2,1)S(1)} collective-permute-done((bf16[4,48,1920]{2,1,0:T(8,128)(2,1)S(1)}, bf16[4,48,1920]{2,1,0:T(8,128)(2,1)S(1)}, u32[]{:S(2)}, u32[]{:S(2)}) %collective-permute-start.26) | collective-permute-done | bytes 737312 | tf_op jit(solution)/shard_map/ppermute | solution.py:1029
  106.8 6.7 %out_norm.1 = (f32[1024,768]{1,0:T(8,128)}, bf16[1024,768]{1,0:T(8,128)(2,1)S(1)}, bf16[768,1024]{1,0:T(8,128)(2,1)S(1)}) custom-call(s32[1]{0:T(128)} %bitcast.me, bf16[1024,768]{1,0:T(8,128)(2,1)} %get-tuple-element.278.tokens.refs_9_, f32[1,768]{1,0:T(1,128)S(1)} %reshape.119.gain.refs_3_, f32[1,768]{1,0:T(1,128)S(1)} %reshape.120.offset, ...), custom_call_target="tpu_custom_call" | custom-call | flops 3000000000 | bytes 8000000 | tf_op jit(solution)/shard_map/out_norm/pallas_call | solution.py:446
  115.4 14.5 %feed_forward.4 = (bf16[4,4,48,1536]{3,2,1,0:T(8,128)(2,1)}, bf16[4,4,48,1536]{3,2,1,0:T(8,128)(2,1)}, f32[1024,768]{1,0:T(8,128)}, f32[1024,768]{1,0:T(8,128)}) custom-call(s32[1]{0:T(128)} %bitcast.me, bf16[1024,768]{1,0:T(8,128)(2,1)S(1)} %get-tuple-element.286.normed, bf16[768,1024]{1,0:T(8,128)(2,1)S(1)} %get-tuple-element.290.normed_t, ...), custom_call_target="tpu_custom_call" | custom-call | flops 11000000512 | bytes 20000000 | tf_op jit(solution)/shard_map/feed_forward/pallas_call | solution.py:636
  131.5 13.2 %feed_forward.5 = (bf16[4,4,48,1536]{3,2,1,0:T(8,128)(2,1)}, bf16[4,4,48,1536]{3,2,1,0:T(8,128)(2,1)}, f32[1024,768]{1,0:T(8,128)}, f32[1024,768]{1,0:T(8,128)}) custom-call(s32[1]{0:T(128)} %bitcast.me, bf16[1024,768]{1,0:T(8,128)(2,1)S(1)} %get-tuple-element.286.normed, ...), custom_call_target="tpu_custom_call", output_to_operand_aliasing={{0}: (15, {}), {1}: (16, {})} | custom-call | flops 11000000512 | bytes 20000000 | tf_op jit(solution)/shard_map/feed_forward/pallas_call | solution.py:636
  145.4 4.5 %collective-permute-done.38.refs_9_.refs_19_ = bf16[4,48,1536]{2,1,0:T(8,128)(2,1)S(1)} collective-permute-done((bf16[4,48,1536]{2,1,0:T(8,128)(2,1)S(1)}, bf16[4,48,1536]{2,1,0:T(8,128)(2,1)S(1)}, u32[]{:S(2)}, u32[]{:S(2)}) %collective-permute-start.38) | collective-permute-done | bytes 589856 | tf_op jit(solution)/shard_map/ppermute | solution.py:1021
  150.7 13.1 %feed_forward.6 = (bf16[4,4,48,1536]{3,2,1,0:T(8,128)(2,1)}, bf16[4,4,48,1536]{3,2,1,0:T(8,128)(2,1)}, f32[1024,768]{1,0:T(8,128)}, f32[1024,768]{1,0:T(8,128)}) custom-call(s32[1]{0:T(128)} %bitcast.me, bf16[1024,768]{1,0:T(8,128)(2,1)S(1)} %get-tuple-element.286.normed, bf16[768,1024]{1,0:T(8,128)(2,1)S(1)} %get-tuple-element.290.normed_t, ...), custom_call_target="tpu_custom_call" | custom-call | flops 11000000512 | bytes 20000000 | tf_op jit(solution)/shard_map/feed_forward/pallas_call | solution.py:636
  167.3 18.9 %feed_forward.7 = (bf16[4,4,48,1536]{3,2,1,0:T(8,128)(2,1)}, bf16[4,4,48,1536]{3,2,1,0:T(8,128)(2,1)}, bf16[1024,768]{1,0:T(8,128)(2,1)}, f32[1024,768]{1,0:T(8,...) custom-call(s32[1]{0:T(128)} %bitcast.me, ...), custom_call_target="tpu_custom_call", output_to_operand_aliasing={{0}: (25, {}), {1}: (26, {})} | custom-call | flops 14000000000 | bytes 20000000 | tf_op jit(solution)/shard_map/feed_forward/pallas_call | solution.py:636
  188.1 19.5 %attend_back.3 = (f32[1024,768]{1,0:T(8,128)}, bf16[4,4,48,768]{3,2,1,0:T(8,128)(2,1)}, bf16[4,4,48,768]{3,2,1,0:T(8,128)(2,1)}) custom-call(s32[1]{0:T(128)} %bitcast.me, bf16[768,1024]{1,0:T(8,128)(2,1)} %get-tuple-element.339.normed_t_in, bf16[1024,768]{1,0:T(8,128)(2,1)} %get-tuple-element.340.proj, ...), custom_call_target="tpu_custom_call" | custom-call | flops 12000000000 | bytes 8000000 | tf_op jit(solution)/shard_map/attend_back/pallas_call | solution.py:837
  207.6 2.1 turn_back.1
  214.3 18.5 %attend_back.4 = (f32[1024,768]{1,0:T(8,128)}, bf16[4,4,48,768]{3,2,1,0:T(8,128)(2,1)}, bf16[4,4,48,768]{3,2,1,0:T(8,128)(2,1)}) custom-call(s32[1]{0:T(128)} %bitcast.me, bf16[768,1024]{1,0:T(8,128)(2,1)} %get-tuple-element.339.normed_t_in, bf16[1024,768]{1,0:T(8,128)(2,1)} %get-tuple-element.357.proj, ...), custom_call_target="tpu_custom_call" | custom-call | flops 12000000000 | bytes 8000000 | tf_op jit(solution)/shard_map/attend_back/pallas_call | solution.py:837
  235.9 1.5 collective-permute-start.52
  238.4 18.3 %attend_back.5 = (f32[1024,768]{1,0:T(8,128)}, bf16[4,4,48,768]{3,2,1,0:T(8,128)(2,1)}, bf16[4,4,48,768]{3,2,1,0:T(8,128)(2,1)}, f32[8,768]{1,0:T(8,128)S(1)}) custom-call(s32[1]{0:T(128)} %bitcast.me, bf16[768,1024]{1,0:T(8,128)(2,1)} %get-tuple-element.339.normed_t_in, ...), custom_call_target="tpu_custom_call", output_to_operand_aliasing={{1}: (18, {}), {2}: (19, {})} | custom-call | flops 12000000000 | bytes 8000000 | tf_op jit(solution)/shard_map/attend_back/pallas_call | solution.py:837
  260.2 1.5 collective-permute-start.56
  263.4 1.5 collective-permute-start.59
  265.8 7.8 %norm_back.1 = (f32[2,512,768]{2,1,0:T(8,128)}, f32[512,768]{1,0:T(8,128)S(1)}) custom-call(s32[1]{0:T(128)S(6)} %select_n.27.start, s32[1]{0:T(128)} %bitcast.2.core, bf16[1024,768]{1,0:T(8,128)(2,1)} %get-tuple-element.278.tokens.refs_9_, f32[1024,768]{1,0:T(8,128)} %get-tuple-element.403.grad_normed, f32[1024,768]{1,0:T(8,128)} %get-tuple-element.404.grad_middle, ...), custom_call_target="tpu_custom_call" | custom-call | flops 4000000000 | bytes 16000000 | tf_op jit(solution)/shard_map/norm_back/pallas_call | solution.py:885
  273.6 5.2 %collective-permute-done.57 = bf16[2,48,768]{2,1,0:T(8,128)(2,1)S(1)} collective-permute-done((bf16[2,48,768]{2,1,0:T(8,128)(2,1)S(1)}, bf16[2,48,768]{2,1,0:T(8,128)(2,1)S(1)}, u32[]{:S(2)}, u32[]{:S(2)}) %collective-permute-start.57) | collective-permute-done | bytes 147488 | tf_op jit(solution)/shard_map/ppermute | solution.py:1029
  279.3 2.6 collective-permute-start.64
  282.0 1.7 collective-permute-start.62
  284.9 7.0 %collective-permute-done.62.near = bf16[112,768]{1,0:T(8,128)(2,1)S(1)} collective-permute-done((bf16[112,768]{1,0:T(8,128)(2,1)S(1)}, bf16[112,768]{1,0:T(8,128)(2,1)S(1)}, u32[]{:S(2)}, u32[]{:S(2)}) %collective-permute-start.62) | collective-permute-done | bytes 172064 | tf_op jit(solution)/shard_map/ppermute | solution.py:1029
  291.9 2.5 collective-permute-start.63
  294.3 6.4 %collective-permute-done.65 = bf16[48,768]{1,0:T(8,128)(2,1)S(1)} collective-permute-done((bf16[48,768]{1,0:T(8,128)(2,1)S(1)}, bf16[48,768]{1,0:T(8,128)(2,1)S(1)}, u32[]{:S(2)}, u32[]{:S(2)}) %collective-permute-start.65) | collective-permute-done | bytes 73760 | tf_op jit(solution)/shard_map/ppermute | solution.py:1029
  (256 shorter events, 55.9 us)
Async XLA Ops:
  1.2 25.7 %collective-permute-start.7 = (bf16[2,512,768]{2,1,0:T(8,128)(2,1)}, bf16[2,512,768]{2,1,0:T(8,128)(2,1)S(1)}, u32[]{:S(2)}, u32[]{:S(2)}) collective-permute-start(bf16[2,512,768]{2,1,0:T(8,128)(2,1)} %bitcast.71), channel_id=1, source_target_pairs={{0,1},{1,0},{2,3},{3,2},{4,5},{5,4},{6,7},{7,6},{8,9},{9,8},{10,11... | collective-permute-start | bytes 4718600 | tf_op jit(solution)/shard_map/ppermute | solution.py:1021
  2.1 18.7 %collective-permute-start.2 = (bf16[48,1152]{1,0:T(8,128)(2,1)S(1)}, bf16[48,1152]{1,0:T(8,128)(2,1)S(1)}, u32[]{:S(2)}, u32[]{:S(2)}) collective-permute-start(bf16[48,1152]{1,0:T(8,128)(2,1)S(1)} %bitcast_dynamic-update-slice_fusion.refs_0_), channel_id=1, source_target_pairs={{0,24},{2,26},{4,28},{6,30},{8,16},{10,18},{12,20},{14,22},{16,8},... | collective-permute-start | bytes 331784 | tf_op jit(solution)/shard_map/ppermute | solution.py:1029
  36.0 17.1 %collective-permute-start.16 = (bf16[48,1920]{1,0:T(8,128)(2,1)S(1)}, bf16[48,1920]{1,0:T(8,128)(2,1)S(1)}, u32[]{:S(2)}, u32[]{:S(2)}) collective-permute-start(bf16[48,1920]{1,0:T(8,128)(2,1)S(1)} %slice.205.refs_0_), channel_id=1, source_target_pairs={{0,8},{2,10},{4,12},{6,14},{8,0},{10,2},{12,4},{14,6},{16,24},{18,... | collective-permute-start | bytes 552968 | tf_op jit(solution)/shard_map/ppermute | solution.py:1029
  55.4 28.4 %collective-permute-start.25 = (bf16[48,1536]{1,0:T(8,128)(2,1)S(1)}, bf16[48,1536]{1,0:T(8,128)(2,1)S(1)}, u32[]{:S(2)}, u32[]{:S(2)}) collective-permute-start(bf16[48,1536]{1,0:T(8,128)(2,1)S(1)} %slice.206.refs_0_), channel_id=1, source_target_pairs={{0,16},{2,18},{4,20},{6,22},{8,24},{10,26},{12,28},{14,30},{16,0},... | collective-permute-start | bytes 442376 | tf_op jit(solution)/shard_map/ppermute | solution.py:1029
  55.8 28.0 %collective-permute-start.22 = (bf16[4,48,1920]{2,1,0:T(8,128)(2,1)S(1)}, bf16[4,48,1920]{2,1,0:T(8,128)(2,1)S(1)}, u32[]{:S(2)}, u32[]{:S(2)}) collective-permute-start(bf16[4,48,1920]{2,1,0:T(8,128)(2,1)S(1)} %arrange.4.refs_3_.refs_0_.refs_2_.refs_4_), channel_id=1, source_target_pairs={{0,2},{2,0},{4,6},{6,4},{8,10},{10,8},{12,14},{14,12},{16,18},{18,... | collective-permute-start | bytes 2211848 | tf_op jit(solution)/shard_map/ppermute | solution.py:1029
  56.8 27.0 %collective-permute-start.23 = (bf16[4,48,1920]{2,1,0:T(8,128)(2,1)S(1)}, bf16[4,48,1920]{2,1,0:T(8,128)(2,1)S(1)}, u32[]{:S(2)}, u32[]{:S(2)}) collective-permute-start(bf16[4,48,1920]{2,1,0:T(8,128)(2,1)S(1)} %arrange.4.refs_3_.refs_0_.refs_2_.refs_4_), channel_id=1, source_target_pairs={{0,4},{2,6},{4,0},{6,2},{8,12},{10,14},{12,8},{14,10},{16,20},{18,... | collective-permute-start | bytes 2211848 | tf_op jit(solution)/shard_map/ppermute | solution.py:1029
  58.1 25.7 %collective-permute-start.24 = (bf16[4,48,1920]{2,1,0:T(8,128)(2,1)S(1)}, bf16[4,48,1920]{2,1,0:T(8,128)(2,1)S(1)}, u32[]{:S(2)}, u32[]{:S(2)}) collective-permute-start(bf16[4,48,1920]{2,1,0:T(8,128)(2,1)S(1)} %arrange.4.refs_3_.refs_0_.refs_2_.refs_4_), channel_id=1, source_target_pairs={{0,1},{1,0},{2,3},{3,2},{4,5},{5,4},{6,7},{7,6},{8,9},{9,8},{10,11... | collective-permute-start | bytes 2211848 | tf_op jit(solution)/shard_map/ppermute | solution.py:1021
  85.9 17.6 %collective-permute-start.26 = (bf16[4,48,1920]{2,1,0:T(8,128)(2,1)S(1)}, bf16[4,48,1920]{2,1,0:T(8,128)(2,1)S(1)}, u32[]{:S(2)}, u32[]{:S(2)}) collective-permute-start(bf16[4,48,1920]{2,1,0:T(8,128)(2,1)S(1)} %collective-permute-done.22.refs_4_.refs_1_.refs_3_.refs_5_), channel_id=1, source_target_pairs={{0,4},{2,6},{4,0},{6,2},{8,12},{10,14},{12,8},{14,10},{16,20},{18,... | collective-permute-start | bytes 2211848 | tf_op jit(solution)/shard_map/ppermute | solution.py:1029
  86.6 16.9 %collective-permute-start.27 = (bf16[4,48,1920]{2,1,0:T(8,128)(2,1)S(1)}, bf16[4,48,1920]{2,1,0:T(8,128)(2,1)S(1)}, u32[]{:S(2)}, u32[]{:S(2)}) collective-permute-start(bf16[4,48,1920]{2,1,0:T(8,128)(2,1)S(1)} %collective-permute-done.22.refs_4_.refs_1_.refs_3_.refs_5_), channel_id=1, source_target_pairs={{0,1},{1,0},{2,3},{3,2},{4,5},{5,4},{6,7},{7,6},{8,9},{9,8},{10,11... | collective-permute-start | bytes 2211848 | tf_op jit(solution)/shard_map/ppermute | solution.py:1021
  86.6 16.9 %collective-permute-start.28 = (bf16[4,48,1920]{2,1,0:T(8,128)(2,1)S(1)}, bf16[4,48,1920]{2,1,0:T(8,128)(2,1)S(1)}, u32[]{:S(2)}, u32[]{:S(2)}) collective-permute-start(bf16[4,48,1920]{2,1,0:T(8,128)(2,1)S(1)} %collective-permute-done.23.refs_5_.refs_2_.refs_4_.refs_6_), channel_id=1, source_target_pairs={{0,1},{1,0},{2,3},{3,2},{4,5},{5,4},{6,7},{7,6},{8,9},{9,8},{10,11... | collective-permute-start | bytes 2211848 | tf_op jit(solution)/shard_map/ppermute | solution.py:1021
  113.5 16.3 %collective-permute-start.33 = (bf16[4,48,1536]{2,1,0:T(8,128)(2,1)S(1)}, bf16[4,48,1536]{2,1,0:T(8,128)(2,1)S(1)}, u32[]{:S(2)}, u32[]{:S(2)}) collective-permute-start(bf16[4,48,1536]{2,1,0:T(8,128)(2,1)S(1)} %arrange.5.refs_2_.refs_12_), channel_id=1, source_target_pairs={{0,2},{2,0},{4,6},{6,4},{8,10},{10,8},{12,14},{14,12},{16,18},{18,... | collective-permute-start | bytes 1769480 | tf_op jit(solution)/shard_map/ppermute | solution.py:1029
  144.8 19.0 %collective-permute-start.39 = (bf16[4,4,48,1536]{3,2,1,0:T(8,128)(2,1)}, bf16[4,4,48,1536]{3,2,1,0:T(8,128)(2,1)S(1)}, u32[]{:S(2)}, u32[]{:S(2)}) collective-permute-start(bf16[4,4,48,1536]{3,2,1,0:T(8,128)(2,1)} %get-tuple-element.318), channel_id=1, source_target_pairs={{0,1},{1,0},{2,3},{3,2},{4,5},{5,4},{6,7},{7,6},{8,9},{9,8},{10,11... | collective-permute-start | bytes 7077896 | tf_op jit(solution)/shard_map/ppermute | solution.py:1021
  164.7 21.6 %collective-permute-start.40 = (bf16[2,4,48,768]{3,2,1,0:T(8,128)(2,1)S(1)}, bf16[2,4,48,768]{3,2,1,0:T(8,128)(2,1)S(1)}, u32[]{:S(2)}, u32[]{:S(2)}) collective-permute-start(bf16[2,4,48,768]{3,2,1,0:T(8,128)(2,1)S(1)} %get-tuple-element.329), channel_id=1, source_target_pairs={{0,2},{2,0},{4,6},{6,4},{8,10},{10,8},{12,14},{14,12},{16,18},{18,... | collective-permute-start | bytes 1769480 | tf_op jit(solution)/shard_map/ppermute | solution.py:1029
  165.8 20.5 %collective-permute-start.41 = (bf16[2,4,48,768]{3,2,1,0:T(8,128)(2,1)S(1)}, bf16[2,4,48,768]{3,2,1,0:T(8,128)(2,1)S(1)}, u32[]{:S(2)}, u32[]{:S(2)}) collective-permute-start(bf16[2,4,48,768]{3,2,1,0:T(8,128)(2,1)S(1)} %get-tuple-element.330), channel_id=1, source_target_pairs={{0,4},{2,6},{4,0},{6,2},{8,12},{10,14},{12,8},{14,10},{16,20},{18,... | collective-permute-start | bytes 1769480 | tf_op jit(solution)/shard_map/ppermute | solution.py:1029
  186.4 23.3 %collective-permute-start.44 = (bf16[4,4,48,1536]{3,2,1,0:T(8,128)(2,1)}, bf16[4,4,48,1536]{3,2,1,0:T(8,128)(2,1)S(1)}, u32[]{:S(2)}, u32[]{:S(2)}) collective-permute-start(bf16[4,4,48,1536]{3,2,1,0:T(8,128)(2,1)} %get-tuple-element.346), channel_id=1, source_target_pairs={{0,1},{1,0},{2,3},{3,2},{4,5},{5,4},{6,7},{7,6},{8,9},{9,8},{10,11... | collective-permute-start | bytes 7077896 | tf_op jit(solution)/shard_map/ppermute | solution.py:1021
  186.5 23.2 %collective-permute-start.42 = (bf16[4,48,768]{2,1,0:T(8,128)(2,1)S(1)}, bf16[4,48,768]{2,1,0:T(8,128)(2,1)S(1)}, u32[]{:S(2)}, u32[]{:S(2)}) collective-permute-start(bf16[4,48,768]{2,1,0:T(8,128)(2,1)S(1)} %get-tuple-element.344), channel_id=1, source_target_pairs={{0,4},{2,6},{4,0},{6,2},{8,12},{10,14},{12,8},{14,10},{16,20},{18,... | collective-permute-start | bytes 884744 | tf_op jit(solution)/shard_map/ppermute | solution.py:1029
  187.1 22.6 %collective-permute-start.43 = (bf16[4,48,768]{2,1,0:T(8,128)(2,1)S(1)}, bf16[4,48,768]{2,1,0:T(8,128)(2,1)S(1)}, u32[]{:S(2)}, u32[]{:S(2)}) collective-permute-start(bf16[4,48,768]{2,1,0:T(8,128)(2,1)S(1)} %get-tuple-element.345), channel_id=1, source_target_pairs={{0,2},{2,0},{4,6},{6,4},{8,10},{10,8},{12,14},{14,12},{16,18},{18,... | collective-permute-start | bytes 884744 | tf_op jit(solution)/shard_map/ppermute | solution.py:1029
  211.0 21.9 %collective-permute-start.48 = (bf16[4,4,48,768]{3,2,1,0:T(8,128)(2,1)S(1)}, bf16[4,4,48,768]{3,2,1,0:T(8,128)(2,1)S(1)}, u32[]{:S(2)}, u32[]{:S(2)}) collective-permute-start(bf16[4,4,48,768]{3,2,1,0:T(8,128)(2,1)S(1)} %copy-done.19), channel_id=1, source_target_pairs={{0,1},{1,0},{2,3},{3,2},{4,5},{5,4},{6,7},{7,6},{8,9},{9,8},{10,11... | collective-permute-start | bytes 3538952 | tf_op jit(solution)/shard_map/ppermute | solution.py:1021
  211.8 21.1 %collective-permute-start.45 = (bf16[2,4,48,768]{3,2,1,0:T(8,128)(2,1)S(1)}, bf16[2,4,48,768]{3,2,1,0:T(8,128)(2,1)S(1)}, u32[]{:S(2)}, u32[]{:S(2)}) collective-permute-start(bf16[2,4,48,768]{3,2,1,0:T(8,128)(2,1)S(1)} %get-tuple-element.360), channel_id=1, source_target_pairs={{0,2},{2,0},{4,6},{6,4},{8,10},{10,8},{12,14},{14,12},{16,18},{18,... | collective-permute-start | bytes 1769480 | tf_op jit(solution)/shard_map/ppermute | solution.py:1029
  212.8 20.1 %collective-permute-start.46 = (bf16[2,4,48,768]{3,2,1,0:T(8,128)(2,1)S(1)}, bf16[2,4,48,768]{3,2,1,0:T(8,128)(2,1)S(1)}, u32[]{:S(2)}, u32[]{:S(2)}) collective-permute-start(bf16[2,4,48,768]{3,2,1,0:T(8,128)(2,1)S(1)} %get-tuple-element.361), channel_id=1, source_target_pairs={{0,4},{2,6},{4,0},{6,2},{8,12},{10,14},{12,8},{14,10},{16,20},{18,... | collective-permute-start | bytes 1769480 | tf_op jit(solution)/shard_map/ppermute | solution.py:1029
  214.3 18.6 %collective-permute-start.47 = (bf16[512,768]{1,0:T(8,128)(2,1)S(1)}, bf16[512,768]{1,0:T(8,128)(2,1)S(1)}, u32[]{:S(2)}, u32[]{:S(2)}) collective-permute-start(bf16[512,768]{1,0:T(8,128)(2,1)S(1)} %get-tuple-element.362), channel_id=1, source_target_pairs={{0,1},{1,0},{2,3},{3,2},{4,5},{5,4},{6,7},{7,6},{8,9},{9,8},{10,11... | collective-permute-start | bytes 2359304 | tf_op jit(solution)/shard_map/ppermute | solution.py:1021
  233.3 23.4 %collective-permute-start.49 = (bf16[4,48,768]{2,1,0:T(8,128)(2,1)S(1)}, bf16[4,48,768]{2,1,0:T(8,128)(2,1)S(1)}, u32[]{:S(2)}, u32[]{:S(2)}) collective-permute-start(bf16[4,48,768]{2,1,0:T(8,128)(2,1)S(1)} %fusion.2), channel_id=1, source_target_pairs={{0,4},{2,6},{4,0},{6,2},{8,12},{10,14},{12,8},{14,10},{16,20},{18,... | collective-permute-start | bytes 884744 | tf_op jit(solution)/shard_map/ppermute | solution.py:1029
  233.9 22.9 %collective-permute-start.50 = (bf16[4,48,768]{2,1,0:T(8,128)(2,1)S(1)}, bf16[4,48,768]{2,1,0:T(8,128)(2,1)S(1)}, u32[]{:S(2)}, u32[]{:S(2)}) collective-permute-start(bf16[4,48,768]{2,1,0:T(8,128)(2,1)S(1)} %fusion.3), channel_id=1, source_target_pairs={{0,2},{2,0},{4,6},{6,4},{8,10},{10,8},{12,14},{14,12},{16,18},{18,... | collective-permute-start | bytes 884744 | tf_op jit(solution)/shard_map/ppermute | solution.py:1029
  234.9 21.9 %collective-permute-start.51 = (bf16[4,48,768]{2,1,0:T(8,128)(2,1)S(1)}, bf16[4,48,768]{2,1,0:T(8,128)(2,1)S(1)}, u32[]{:S(2)}, u32[]{:S(2)}) collective-permute-start(bf16[4,48,768]{2,1,0:T(8,128)(2,1)S(1)} %get-tuple-element.379), channel_id=1, source_target_pairs={{0,2},{2,0},{4,6},{6,4},{8,10},{10,8},{12,14},{14,12},{16,18},{18,... | collective-permute-start | bytes 884744 | tf_op jit(solution)/shard_map/ppermute | solution.py:1029
  235.9 20.9 %collective-permute-start.52 = (bf16[4,48,768]{2,1,0:T(8,128)(2,1)S(1)}, bf16[4,48,768]{2,1,0:T(8,128)(2,1)S(1)}, u32[]{:S(2)}, u32[]{:S(2)}) collective-permute-start(bf16[4,48,768]{2,1,0:T(8,128)(2,1)S(1)} %get-tuple-element.380), channel_id=1, source_target_pairs={{0,4},{2,6},{4,0},{6,2},{8,12},{10,14},{12,8},{14,10},{16,20},{18,... | collective-permute-start | bytes 884744 | tf_op jit(solution)/shard_map/ppermute | solution.py:1029
  237.4 19.4 %collective-permute-start.53 = (bf16[4,48,768]{2,1,0:T(8,128)(2,1)S(1)}, bf16[4,48,768]{2,1,0:T(8,128)(2,1)S(1)}, u32[]{:S(2)}, u32[]{:S(2)}) collective-permute-start(bf16[4,48,768]{2,1,0:T(8,128)(2,1)S(1)} %get-tuple-element.381), channel_id=1, source_target_pairs={{0,6},{2,4},{4,2},{6,0},{8,14},{10,12},{12,10},{14,8},{16,22},{18,... | collective-permute-start | bytes 884744 | tf_op jit(solution)/shard_map/ppermute | solution.py:1029
  260.2 18.9 %collective-permute-start.56 = (bf16[2,48,3072]{2,1,0:T(8,128)(2,1)S(1)}, bf16[2,48,3072]{2,1,0:T(8,128)(2,1)S(1)}, u32[]{:S(2)}, u32[]{:S(2)}) collective-permute-start(bf16[2,48,3072]{2,1,0:T(8,128)(2,1)S(1)} %get-tuple-element.407), channel_id=1, source_target_pairs={{0,8},{2,10},{4,12},{6,14},{8,0},{10,2},{12,4},{14,6},{16,24},{18,... | collective-permute-start | bytes 1769480 | tf_op jit(solution)/shard_map/ppermute | solution.py:1029
  261.8 17.1 %collective-permute-start.57 = (bf16[2,48,768]{2,1,0:T(8,128)(2,1)S(1)}, bf16[2,48,768]{2,1,0:T(8,128)(2,1)S(1)}, u32[]{:S(2)}, u32[]{:S(2)}) collective-permute-start(bf16[2,48,768]{2,1,0:T(8,128)(2,1)S(1)} %get-tuple-element.408), channel_id=1, source_target_pairs={{0,8},{2,10},{4,12},{6,14},{8,0},{10,2},{12,4},{14,6},{16,24},{18,... | collective-permute-start | bytes 442376 | tf_op jit(solution)/shard_map/ppermute | solution.py:1029
  262.3 16.5 %collective-permute-start.58 = (bf16[208,768]{1,0:T(8,128)(2,1)S(1)}, bf16[208,768]{1,0:T(8,128)(2,1)S(1)}, u32[]{:S(2)}, u32[]{:S(2)}) collective-permute-start(bf16[208,768]{1,0:T(8,128)(2,1)S(1)} %get-tuple-element.409), channel_id=1, source_target_pairs={{0,2},{2,0},{4,6},{6,4},{8,10},{10,8},{12,14},{14,12},{16,18},{18,... | collective-permute-start | bytes 958472 | tf_op jit(solution)/shard_map/ppermute | solution.py:1029
  279.3 21.5 %collective-permute-start.64 = (bf16[48,3072]{1,0:T(8,128)(2,1)S(1)}, bf16[48,3072]{1,0:T(8,128)(2,1)S(1)}, u32[]{:S(2)}, u32[]{:S(2)}) collective-permute-start(bf16[48,3072]{1,0:T(8,128)(2,1)S(1)} %fusion.8), channel_id=1, source_target_pairs={{0,16},{2,18},{4,20},{6,22},{8,24},{10,26},{12,28},{14,30},{16,0},... | collective-permute-start | bytes 884744 | tf_op jit(solution)/shard_map/ppermute | solution.py:1029
  284.6 16.2 %collective-permute-start.65 = (bf16[48,768]{1,0:T(8,128)(2,1)S(1)}, bf16[48,768]{1,0:T(8,128)(2,1)S(1)}, u32[]{:S(2)}, u32[]{:S(2)}) collective-permute-start(bf16[48,768]{1,0:T(8,128)(2,1)S(1)} %fusion.9), channel_id=1, source_target_pairs={{0,16},{2,18},{4,20},{6,22},{8,24},{10,26},{12,28},{14,30},{16,0},... | collective-permute-start | bytes 221192 | tf_op jit(solution)/shard_map/ppermute | solution.py:1029
  284.9 19.9 %collective-permute-start.61 = (f32[512,768]{1,0:T(8,128)S(1)}, f32[512,768]{1,0:T(8,128)S(1)}, u32[]{:S(2)}, u32[]{:S(2)}) collective-permute-start(f32[512,768]{1,0:T(8,128)S(1)} %get-tuple-element.412), channel_id=1, source_target_pairs={{0,1},{1,0},{2,3},{3,2},{4,5},{5,4},{6,7},{7,6},{8,9},{9,8},{10,11... | collective-permute-start | bytes 4718600 | tf_op jit(solution)/shard_map/ppermute | solution.py:1021
  (82 other events, 663.8 us)

commit v3 on v2

--- a/solution.py
+++ b/solution.py
@@ -561,7 +561,7 @@
         sums[...] = jnp.zeros_like(sums)
 
         def back_step(r, carry):
-            at = pl.ds(pl.multiple_of(r * QB, QB), QB)
+            at = pl.ds(pl.multiple_of(r * 512, 512), 512)
             hat, root = norm_parts(middle_here[at, :])
             grad = grad_acc[at, :]
             value = cot[at, :].astype(F32) + norm_pull(grad, hat, root, gain[...])
@@ -576,7 +576,7 @@
                 grad_att[g][at, 128:256] = back[:, width + g * 128 : width + g * 128 + 128]
             return carry
 
-        lax.fori_loop(0, length // QB, back_step, 0)
+        lax.fori_loop(0, length // 512, back_step, 0)
         out_copies.append(pltpu.make_async_copy(grad_middle, grad_middle_out, sems.at[2]))
         out_copies[-1].start()
     else:
@@ -1063,7 +1063,7 @@
     def add(self, transfer, name, results, seeds=()):
         self.active.append([transfer, list(seeds), name, results])
 
-    def step(self, *pivots):
+    def step(self, *pivots, gate=None):
         values = [v for item in self.active for v in item[1]]
         tied = list(tie(self.me, *pivots, *values))
         self.me = tied.pop(0)
@@ -1082,8 +1082,11 @@
                 requests.append(asked)
             except StopIteration as stop:
                 results[name] = stop.value
-        tied = list(tie(self.me, *(operand for asked in requests for operand, _ in asked)))
-        self.me = tied.pop(0)
+        gates = gate() if gate else []
+        operands = [operand for asked in requests for operand, _ in asked]
+        tied = list(tie(self.me, *gates, *operands))
+        self.me = tied[0]
+        tied = tied[1 + len(gates) :]
         for item, asked in zip(self.active, requests):
             item[1] = [send(operand) for (_, send), operand in zip(asked, tied)]
             tied = tied[len(asked) :]
@@ -1142,7 +1145,7 @@
     feed_pieces += [Piece(rows, "slabs", wide * s) for s in range(subs - cut)]
     turns = [(0, 2, 1, 3), MASKS]
     feed_outs = [
-        Piece(rows, "stack", wide * (s % cut), wide * cut, turns[s % cut]) for s in range(subs)
+        Piece(rows, "stack", 0, wide, turns[s % 2]) for s in range(subs)
     ]
     qkv_outs = [Piece(rows, "stack", part, wide)]
     qkv_outs += [Piece(rows, "stack", part * g, part * (groups - 1)) for g in range(groups - 1)]
@@ -1177,17 +1180,15 @@
         own = gather_whole(shard)
         return [own, swap(own)]
 
-    def halve(own, other):
-        (other,) = yield swaps([other])
-        middle_col = own.shape[-1] // 2
-        keep, send = [], []
-        for cols in (slice(0, middle_col), slice(middle_col, None)):
-            keep.append(low_sum([own[:2, ..., cols], other[:2, ..., cols]]).astype(BF))
-            send.append(low_sum([own[2:, ..., cols], other[2:, ..., cols]]).astype(BF))
-        near = yield [(v, via(m)) for v, m in zip(send, (1, 2))]
-        send = [low_sum([k[1], n[1]]).astype(BF) for k, n in zip(keep, near)]
-        away = yield [(v, via(m)) for v, m in zip(send, (2, 1))]
-        return [list(group) for group in zip(keep, near, away)]
+    def halve(first, hurry, own, other):
+        if hurry:
+            other = swap(other)
+        else:
+            (other,) = yield swaps([other])
+        keep, send = (low_sum([own[k : k + 2], other[k : k + 2]]).astype(BF) for k in (0, 2))
+        (near,) = yield [(send, via(first))]
+        (away,) = yield [(low_sum([keep[1], near[1]]).astype(BF), via(3 - first))]
+        return [keep, near, away]
 
     def direct(mine):
         got = yield hops_of(mine, (1, 2, 3))
@@ -1202,9 +1203,9 @@
         (away,) = yield [(low_sum([keep[1], near[1]]).astype(BF), via(8))]
         return low_sum([keep[0], near[0], away])
 
-    def reduce_all(own, other):
-        groups_here = yield from halve(own, other)
-        return (yield from reduce_far(sums_of["early"] + groups_here))
+    def reduce_all(first, own, other):
+        group = yield from halve(first, True, own, other)
+        return (yield from reduce_far([sums_of[s] for s in range(subs - 1)] + [group]))
 
     def reduce_last(own, other, sums):
         other, sums_away = swap(other), swap(sums)
@@ -1303,20 +1304,19 @@
             cot_t,
             held,
             slabs[feed_names[s]],
-            onto,
+            [],
             (out_piece, slabs["a"], middle, gain2, groups) if final else None,
         )
-        onto = grads
-        if s % cut == cut - 1:
-            k = s // cut
-            if rows.split and k == 0:
-                flow.add(halve, "early", sums_of, grads)
-            elif rows.split:
-                flow.add(reduce_all, "feed", sums_of, grads)
-            else:
-                sums_of[k] = plain(*grads)
-            onto = []
-        if not final:
+        first = 1 + s % 2
+        if not rows.split:
+            sums_of[s] = plain(*grads)
+        elif final:
+            flow.add(functools.partial(reduce_all, first), "feed", sums_of, grads)
+        else:
+            flow.add(functools.partial(halve, first, False), s, sums_of, grads)
+        if s == 1 and rows.split:
+            flow.step(held[1], gate=lambda: slabs["c"][-1:])
+        elif not final:
             flow.step(held[1])
     mixed, grad_middle, branch_t, sums2, *grad_atts = held
     mixed, core_place, _ = flow.step(mixed, core_place, sums2)
@@ -1396,7 +1396,7 @@
         parts = [early[:, part:], last[:, :part], last[:, part:]]
         grad_qkv = jnp.concatenate([r.reshape(-1, 3, 128) for r in parts], 2)
         grad_out = early[:, :part].T
-        feed_sums = [sums_of[0], sums_of[1]]
+        feed_sums = [sums_of[s] for s in range(subs)]
         norm_sums = jnp.sum(lax.all_gather(sums + swap(sums), "dp", axis=0), 0)
     feed_sum = jnp.concatenate(feed_sums, 1) if len(feed_sums) > 1 else feed_sums[0]
     feed_list = [feed_sum[:, wide * s : wide * (s + 1)] for s in range(subs)]

time: 311 us -> 307 us (0.987)
  waiting for transfers between devices: 33.4 us -> 27.1 us
    ppermute x25 -> x27, waiting for transfers between devices: 7.46 us -> 3.17 us  [swap(): return lax.ppermute(value, 'mp', [(0, 1), (1, 0)])]
    unnamed x99 -> x107, local copies, waits for them, and re-layouts: 9.92 us -> 12.7 us
  transfers between devices with their start and end apart: 66 -> 68, of which waited for: 11 -> 16; matrix products, arithmetic and copies ran while one was open for 2% -> 3% of each run, Pallas kernels for 63% -> 64%
where the time goes in v3:
time: 307 us; the launch traced here: 302 us
  Pallas kernels  195 us (64%)
  starting transfers between devices  55.1 us (18%)
  waiting for transfers between devices  27.1 us (9%)
  local copies, waits for them, and re-layouts  16.3 us (5%)
  other arithmetic  4.91 us (2%)
  between operations  3.88 us (1%)
    pallas_call x4, Pallas kernels, feed_forward(): pl.pallas_call(functools.partial(feed_forward_body, piece, out_piece, fir...  59.5 us
    pallas_call x3, Pallas kernels, attend_back(): pl.pallas_call(functools.partial(attend_back_body, piece, out_piece, extr...  55.9 us
    ppermute x41, starting transfers between devices, hop(): return lax.ppermute(value, 'dp', [(i, i ^ mask) for i in range(count)])  50.4 us
    pallas_call x3, Pallas kernels, project_attend(): pl.pallas_call(functools.partial(project_attend_body, piece), in_specs=[s...  46.5 us
    ppermute x41, waiting for transfers between devices, hop(): return lax.ppermute(value, 'dp', [(i, i ^ mask) for i in range(count)])  23.9 us
    unnamed x107, local copies, waits for them, and re-layouts  12.7 us
    pallas_call x1, Pallas kernels, norm_back(): pl.pallas_call(norm_back_body, grid=(length // QB,), in_specs=[smem_spec(...  7.75 us
    pallas_call x1, Pallas kernels, prepare(): pl.pallas_call(prepare_body, in_specs=[smem_spec()] * 2 + [any_spec()] *...  6.76 us
  transfers between devices with their start and end apart: 68, of which 16 were waited for; matrix products, arithmetic and copies ran while one was open for 3% of the time, Pallas kernels for 64%

profile of v3, /device:TPU:0, one launch (start us, length us, event | category | flops | bytes accessed | tf_op | source)
XLA Modules:
  0.0 301.9 jit_solution(5386525783789716952)
XLA Ops:
  2.1 5.1 %collective-permute-start.2 = (bf16[48,1152]{1,0:T(8,128)(2,1)S(1)}, bf16[48,1152]{1,0:T(8,128)(2,1)S(1)}, u32[]{:S(2)}, u32[]{:S(2)}) collective-permute-start(bf16[48,1152]{1,0:T(8,128)(2,1)S(1)} %bitcast_dynamic-update-slice_fusion.refs_0_), channel_id=1, source_target_pairs={{0,24},{2,26},{4,28},{6,30},{8,16},{10,18},{12,20},{14,22},{16,8},... | collective-permute-start | bytes 331784 | tf_op jit(solution)/shard_map/ppermute | solution.py:1029
  14.0 6.8 %prepare.1 = (bf16[1024,768]{1,0:T(8,128)(2,1)}, bf16[1024,768]{1,0:T(8,128)(2,1)}, bf16[768,1024]{1,0:T(8,128)(2,1)}) custom-call(s32[1]{0:T(128)} %bitcast.1.start, s32[1]{0:T(128)} %bitcast.2.core, bf16[2,512,768]{2,1,0:T(8,128)(2,1)} %bitcast.70, bf16[2,512,768]{2,1,0:T(8,128)(2,1)} %collective-permute-done.3.other, f32[1,768]{1,0:T(1,128)S(1)} %reshape.115.gain, ...), custom_call_target="tpu_custom_call" | custom-call | flops 4000000000 | bytes 8000000 | tf_op jit(solution)/shard_map/prepare/pallas_call | solution.py:200
  20.8 2.7 collective-permute-start.6
  24.4 2.3 collective-permute-start.8
  27.9 5.4 %turn.1 = (bf16[1024,768]{1,0:T(8,128)(2,1)}, bf16[768,1024]{1,0:T(8,128)(2,1)}) custom-call(s32[1]{0:T(128)} %bitcast.1.start, s32[1]{0:T(128)} %bitcast.2.core, bf16[2,512,768]{2,1,0:T(8,128)(2,1)} %bitcast.72, bf16[2,512,768]{2,1,0:T(8,128)(2,1)} %copy-done.20), custom_call_target="tpu_custom_call" | custom-call | flops 4000000000 | bytes 8000000 | tf_op jit(solution)/shard_map/turn/pallas_call | solution.py:238
  36.0 2.1 collective-permute-start.16
  38.2 1.5 collective-permute-start.13
  39.8 1.5 collective-permute-start.14
  41.9 11.2 %project_attend.3 = (bf16[1024,768]{1,0:T(8,128)(2,1)}, bf16[1024,256]{1,0:T(8,128)(2,1)}, f32[8,1024]{1,0:T(8,128)}) custom-call(s32[1]{0:T(128)} %bitcast.me, bf16[1024,768]{1,0:T(8,128)(2,1)} %get-tuple-element.247.normed_in, s32[256,1]{1,0:T(8,128)S(1)} %copy.33.seg_col, s32[1,256]{1,0:T(1,128)S(1)} %bitcast.58, bf16[4,48,384]{2,1,0:T(8,128)(2,1)} %copy-done.6, ...), custom_call_target="tpu_custom_call" | custom-call | flops 8000000000 | bytes 8000000 | tf_op jit(solution)/shard_map/project_attend/pallas_call | solution.py:394
  59.5 24.2 %project_attend.4 = (bf16[1024,768]{1,0:T(8,128)(2,1)}, bf16[1024,256]{1,0:T(8,128)(2,1)}, f32[8,1024]{1,0:T(8,128)}) custom-call(s32[1]{0:T(128)} %bitcast.me, bf16[1024,768]{1,0:T(8,128)(2,1)} %get-tuple-element.247.normed_in, s32[256,1]{1,0:T(8,128)S(1)} %copy.33.seg_col, s32[1,256]{1,0:T(1,128)S(1)} %bitcast.59, bf16[4,48,768]{2,1,0:T(8,128)(2,1)} %copy-done.3, ...), custom_call_target="tpu_custom_call" | custom-call | flops 8000000000 | bytes 8000000 | tf_op jit(solution)/shard_map/project_attend/pallas_call | solution.py:394
  83.8 1.6 collective-permute-start.29
  87.3 11.2 %project_attend.5 = (bf16[1024,768]{1,0:T(8,128)(2,1)}, bf16[1024,256]{1,0:T(8,128)(2,1)}, f32[8,1024]{1,0:T(8,128)}) custom-call(s32[1]{0:T(128)} %bitcast.me, bf16[1024,768]{1,0:T(8,128)(2,1)} %get-tuple-element.247.normed_in, s32[256,1]{1,0:T(8,128)S(1)} %copy.33.seg_col, s32[1,256]{1,0:T(1,128)S(1)} %bitcast.60, bf16[4,48,768]{2,1,0:T(8,128)(2,1)} %copy-done.3, ...), custom_call_target="tpu_custom_call" | custom-call | flops 8000000000 | bytes 8000000 | tf_op jit(solution)/shard_map/project_attend/pallas_call | solution.py:394
  98.5 5.1 %collective-permute-done.26.refs_6_.refs_3_.refs_5_.refs_7_ = bf16[4,48,1920]{2,1,0:T(8,128)(2,1)S(1)} collective-permute-done((bf16[4,48,1920]{2,1,0:T(8,128)(2,1)S(1)}, bf16[4,48,1920]{2,1,0:T(8,128)(2,1)S(1)}, u32[]{:S(2)}, u32[]{:S(2)}) %collective-permute-start.26) | collective-permute-done | bytes 737312 | tf_op jit(solution)/shard_map/ppermute | solution.py:1029
  106.8 6.7 %out_norm.1 = (f32[1024,768]{1,0:T(8,128)}, bf16[1024,768]{1,0:T(8,128)(2,1)S(1)}, bf16[768,1024]{1,0:T(8,128)(2,1)S(1)}) custom-call(s32[1]{0:T(128)} %bitcast.me, bf16[1024,768]{1,0:T(8,128)(2,1)} %get-tuple-element.284.tokens.refs_9_, f32[1,768]{1,0:T(1,128)S(1)} %reshape.119.gain.refs_3_, f32[1,768]{1,0:T(1,128)S(1)} %reshape.120.offset, ...), custom_call_target="tpu_custom_call" | custom-call | flops 3000000000 | bytes 8000000 | tf_op jit(solution)/shard_map/out_norm/pallas_call | solution.py:446
  115.3 14.4 %feed_forward.4 = (bf16[4,4,48,768]{3,2,1,0:T(8,128)(2,1)}, bf16[4,4,48,768]{3,2,1,0:T(8,128)(2,1)}, f32[1024,768]{1,0:T(8,128)}, f32[1024,768]{1,0:T(8,128)}) custom-call(s32[1]{0:T(128)} %bitcast.me, bf16[1024,768]{1,0:T(8,128)(2,1)S(1)} %get-tuple-element.292.normed, bf16[768,1024]{1,0:T(8,128)(2,1)S(1)} %get-tuple-element.296.normed_t, ...), custom_call_target="tpu_custom_call" | custom-call | flops 11000000512 | bytes 20000000 | tf_op jit(solution)/shard_map/feed_forward/pallas_call | solution.py:636
  131.6 13.4 %feed_forward.5 = (bf16[4,4,48,768]{3,2,1,0:T(8,128)(2,1)}, bf16[4,4,48,768]{3,2,1,0:T(8,128)(2,1)}, f32[1024,768]{1,0:T(8,128)}, f32[1024,768]{1,0:T(8,128)}) custom-call(s32[1]{0:T(128)} %bitcast.me, bf16[1024,768]{1,0:T(8,128)(2,1)S(1)} %get-tuple-element.292.normed, bf16[768,1024]{1,0:T(8,128)(2,1)S(1)} %get-tuple-element.296.normed_t, ...), custom_call_target="tpu_custom_call" | custom-call | flops 11000000512 | bytes 20000000 | tf_op jit(solution)/shard_map/feed_forward/pallas_call | solution.py:636
  149.0 13.0 %feed_forward.6 = (bf16[4,4,48,768]{3,2,1,0:T(8,128)(2,1)}, bf16[4,4,48,768]{3,2,1,0:T(8,128)(2,1)}, f32[1024,768]{1,0:T(8,128)}, f32[1024,768]{1,0:T(8,128)}) custom-call(s32[1]{0:T(128)} %bitcast.me, bf16[1024,768]{1,0:T(8,128)(2,1)S(1)} %get-tuple-element.292.normed, bf16[768,1024]{1,0:T(8,128)(2,1)S(1)} %get-tuple-element.296.normed_t, ...), custom_call_target="tpu_custom_call" | custom-call | flops 11000000512 | bytes 20000000 | tf_op jit(solution)/shard_map/feed_forward/pallas_call | solution.py:636
  163.9 1.6 collective-permute-start.42
  166.0 18.7 %feed_forward.7 = (bf16[4,4,48,768]{3,2,1,0:T(8,128)(2,1)}, bf16[4,4,48,768]{3,2,1,0:T(8,128)(2,1)}, bf16[1024,768]{1,0:T(8,128)(2,1)}, f32[1024,768]{1,0:T(8,12...) custom-call(s32[1]{0:T(128)} %bitcast.me, ...), custom_call_target="tpu_custom_call" | custom-call | flops 14000000000 | bytes 20000000 | tf_op jit(solution)/shard_map/feed_forward/pallas_call | solution.py:636
  186.7 2.1 turn_back.1
  194.0 19.2 %attend_back.3 = (f32[1024,768]{1,0:T(8,128)}, bf16[4,4,48,768]{3,2,1,0:T(8,128)(2,1)}, bf16[4,4,48,768]{3,2,1,0:T(8,128)(2,1)}) custom-call(s32[1]{0:T(128)} %bitcast.me, bf16[768,1024]{1,0:T(8,128)(2,1)} %get-tuple-element.355.normed_t_in, bf16[1024,768]{1,0:T(8,128)(2,1)} %get-tuple-element.356.proj, ...), custom_call_target="tpu_custom_call" | custom-call | flops 12000000000 | bytes 8000000 | tf_op jit(solution)/shard_map/attend_back/pallas_call | solution.py:837
  216.9 18.5 %attend_back.4 = (f32[1024,768]{1,0:T(8,128)}, bf16[4,4,48,768]{3,2,1,0:T(8,128)(2,1)}, bf16[4,4,48,768]{3,2,1,0:T(8,128)(2,1)}) custom-call(s32[1]{0:T(128)} %bitcast.me, bf16[768,1024]{1,0:T(8,128)(2,1)} %get-tuple-element.355.normed_t_in, bf16[1024,768]{1,0:T(8,128)(2,1)} %get-tuple-element.373.proj, ...), custom_call_target="tpu_custom_call" | custom-call | flops 12000000000 | bytes 8000000 | tf_op jit(solution)/shard_map/attend_back/pallas_call | solution.py:837
  237.1 1.5 collective-permute-start.55
  241.0 18.3 %attend_back.5 = (f32[1024,768]{1,0:T(8,128)}, bf16[4,4,48,768]{3,2,1,0:T(8,128)(2,1)}, bf16[4,4,48,768]{3,2,1,0:T(8,128)(2,1)}, f32[8,768]{1,0:T(8,128)S(1)}) custom-call(s32[1]{0:T(128)} %bitcast.me, bf16[768,1024]{1,0:T(8,128)(2,1)} %get-tuple-element.355.normed_t_in, ...), custom_call_target="tpu_custom_call", output_to_operand_aliasing={{1}: (18, {}), {2}: (19, {})} | custom-call | flops 12000000000 | bytes 8000000 | tf_op jit(solution)/shard_map/attend_back/pallas_call | solution.py:837
  263.6 2.5 collective-permute-start.59
  269.5 7.8 %norm_back.1 = (f32[2,512,768]{2,1,0:T(8,128)}, f32[512,768]{1,0:T(8,128)S(1)}) custom-call(s32[1]{0:T(128)S(6)} %select_n.27.start, s32[1]{0:T(128)} %bitcast.2.core, bf16[1024,768]{1,0:T(8,128)(2,1)} %get-tuple-element.284.tokens.refs_9_, f32[1024,768]{1,0:T(8,128)} %get-tuple-element.418.grad_normed, f32[1024,768]{1,0:T(8,128)} %get-tuple-element.419.grad_middle, ...), custom_call_target="tpu_custom_call" | custom-call | flops 4000000000 | bytes 16000000 | tf_op jit(solution)/shard_map/norm_back/pallas_call | solution.py:885
  277.3 2.3 collective-permute-done.59
  279.6 2.0 collective-permute-done.62.m2
  283.5 1.6 collective-permute-start.65
  286.5 3.6 %collective-permute-done.67 = bf16[48,768]{1,0:T(8,128)(2,1)S(1)} collective-permute-done((bf16[48,768]{1,0:T(8,128)(2,1)S(1)}, bf16[48,768]{1,0:T(8,128)(2,1)S(1)}, u32[]{:S(2)}, u32[]{:S(2)}) %collective-permute-start.67) | collective-permute-done | bytes 73760 | tf_op jit(solution)/shard_map/ppermute | solution.py:1029
  291.6 2.3 collective-permute-start.66
  294.6 4.6 %collective-permute-done.66.away = bf16[64,768]{1,0:T(8,128)(2,1)S(1)} collective-permute-done((bf16[64,768]{1,0:T(8,128)(2,1)S(1)}, bf16[64,768]{1,0:T(8,128)(2,1)S(1)}, u32[]{:S(2)}, u32[]{:S(2)}) %collective-permute-start.66) | collective-permute-done | bytes 98336 | tf_op jit(solution)/shard_map/ppermute | solution.py:1029
  (270 shorter events, 63.6 us)
Async XLA Ops:
  1.2 25.6 %collective-permute-start.7 = (bf16[2,512,768]{2,1,0:T(8,128)(2,1)}, bf16[2,512,768]{2,1,0:T(8,128)(2,1)S(1)}, u32[]{:S(2)}, u32[]{:S(2)}) collective-permute-start(bf16[2,512,768]{2,1,0:T(8,128)(2,1)} %bitcast.71), channel_id=1, source_target_pairs={{0,1},{1,0},{2,3},{3,2},{4,5},{5,4},{6,7},{7,6},{8,9},{9,8},{10,11... | collective-permute-start | bytes 4718600 | tf_op jit(solution)/shard_map/ppermute | solution.py:1021
  2.1 18.6 %collective-permute-start.2 = (bf16[48,1152]{1,0:T(8,128)(2,1)S(1)}, bf16[48,1152]{1,0:T(8,128)(2,1)S(1)}, u32[]{:S(2)}, u32[]{:S(2)}) collective-permute-start(bf16[48,1152]{1,0:T(8,128)(2,1)S(1)} %bitcast_dynamic-update-slice_fusion.refs_0_), channel_id=1, source_target_pairs={{0,24},{2,26},{4,28},{6,30},{8,16},{10,18},{12,20},{14,22},{16,8},... | collective-permute-start | bytes 331784 | tf_op jit(solution)/shard_map/ppermute | solution.py:1029
  36.0 17.1 %collective-permute-start.16 = (bf16[48,1920]{1,0:T(8,128)(2,1)S(1)}, bf16[48,1920]{1,0:T(8,128)(2,1)S(1)}, u32[]{:S(2)}, u32[]{:S(2)}) collective-permute-start(bf16[48,1920]{1,0:T(8,128)(2,1)S(1)} %slice.205.refs_0_), channel_id=1, source_target_pairs={{0,8},{2,10},{4,12},{6,14},{8,0},{10,2},{12,4},{14,6},{16,24},{18,... | collective-permute-start | bytes 552968 | tf_op jit(solution)/shard_map/ppermute | solution.py:1029
  38.1 15.1 %collective-permute-start.17 = (bf16[48,1920]{1,0:T(8,128)(2,1)S(1)}, bf16[48,1920]{1,0:T(8,128)(2,1)S(1)}, u32[]{:S(2)}, u32[]{:S(2)}) collective-permute-start(bf16[48,1920]{1,0:T(8,128)(2,1)S(1)} %collective-permute-done.8.refs_2_), channel_id=1, source_target_pairs={{0,8},{2,10},{4,12},{6,14},{8,0},{10,2},{12,4},{14,6},{16,24},{18,... | collective-permute-start | bytes 552968 | tf_op jit(solution)/shard_map/ppermute | solution.py:1029
  55.4 28.4 %collective-permute-start.25 = (bf16[48,1536]{1,0:T(8,128)(2,1)S(1)}, bf16[48,1536]{1,0:T(8,128)(2,1)S(1)}, u32[]{:S(2)}, u32[]{:S(2)}) collective-permute-start(bf16[48,1536]{1,0:T(8,128)(2,1)S(1)} %slice.206.refs_0_), channel_id=1, source_target_pairs={{0,16},{2,18},{4,20},{6,22},{8,24},{10,26},{12,28},{14,30},{16,0},... | collective-permute-start | bytes 442376 | tf_op jit(solution)/shard_map/ppermute | solution.py:1029
  55.8 27.9 %collective-permute-start.22 = (bf16[4,48,1920]{2,1,0:T(8,128)(2,1)S(1)}, bf16[4,48,1920]{2,1,0:T(8,128)(2,1)S(1)}, u32[]{:S(2)}, u32[]{:S(2)}) collective-permute-start(bf16[4,48,1920]{2,1,0:T(8,128)(2,1)S(1)} %arrange.4.refs_3_.refs_0_.refs_2_.refs_4_), channel_id=1, source_target_pairs={{0,2},{2,0},{4,6},{6,4},{8,10},{10,8},{12,14},{14,12},{16,18},{18,... | collective-permute-start | bytes 2211848 | tf_op jit(solution)/shard_map/ppermute | solution.py:1029
  56.9 26.8 %collective-permute-start.23 = (bf16[4,48,1920]{2,1,0:T(8,128)(2,1)S(1)}, bf16[4,48,1920]{2,1,0:T(8,128)(2,1)S(1)}, u32[]{:S(2)}, u32[]{:S(2)}) collective-permute-start(bf16[4,48,1920]{2,1,0:T(8,128)(2,1)S(1)} %arrange.4.refs_3_.refs_0_.refs_2_.refs_4_), channel_id=1, source_target_pairs={{0,4},{2,6},{4,0},{6,2},{8,12},{10,14},{12,8},{14,10},{16,20},{18,... | collective-permute-start | bytes 2211848 | tf_op jit(solution)/shard_map/ppermute | solution.py:1029
  58.1 25.7 %collective-permute-start.24 = (bf16[4,48,1920]{2,1,0:T(8,128)(2,1)S(1)}, bf16[4,48,1920]{2,1,0:T(8,128)(2,1)S(1)}, u32[]{:S(2)}, u32[]{:S(2)}) collective-permute-start(bf16[4,48,1920]{2,1,0:T(8,128)(2,1)S(1)} %arrange.4.refs_3_.refs_0_.refs_2_.refs_4_), channel_id=1, source_target_pairs={{0,1},{1,0},{2,3},{3,2},{4,5},{5,4},{6,7},{7,6},{8,9},{9,8},{10,11... | collective-permute-start | bytes 2211848 | tf_op jit(solution)/shard_map/ppermute | solution.py:1021
  85.9 17.7 %collective-permute-start.26 = (bf16[4,48,1920]{2,1,0:T(8,128)(2,1)S(1)}, bf16[4,48,1920]{2,1,0:T(8,128)(2,1)S(1)}, u32[]{:S(2)}, u32[]{:S(2)}) collective-permute-start(bf16[4,48,1920]{2,1,0:T(8,128)(2,1)S(1)} %collective-permute-done.22.refs_4_.refs_1_.refs_3_.refs_5_), channel_id=1, source_target_pairs={{0,4},{2,6},{4,0},{6,2},{8,12},{10,14},{12,8},{14,10},{16,20},{18,... | collective-permute-start | bytes 2211848 | tf_op jit(solution)/shard_map/ppermute | solution.py:1029
  86.7 16.8 %collective-permute-start.27 = (bf16[4,48,1920]{2,1,0:T(8,128)(2,1)S(1)}, bf16[4,48,1920]{2,1,0:T(8,128)(2,1)S(1)}, u32[]{:S(2)}, u32[]{:S(2)}) collective-permute-start(bf16[4,48,1920]{2,1,0:T(8,128)(2,1)S(1)} %collective-permute-done.22.refs_4_.refs_1_.refs_3_.refs_5_), channel_id=1, source_target_pairs={{0,1},{1,0},{2,3},{3,2},{4,5},{5,4},{6,7},{7,6},{8,9},{9,8},{10,11... | collective-permute-start | bytes 2211848 | tf_op jit(solution)/shard_map/ppermute | solution.py:1021
  86.8 16.8 %collective-permute-start.28 = (bf16[4,48,1920]{2,1,0:T(8,128)(2,1)S(1)}, bf16[4,48,1920]{2,1,0:T(8,128)(2,1)S(1)}, u32[]{:S(2)}, u32[]{:S(2)}) collective-permute-start(bf16[4,48,1920]{2,1,0:T(8,128)(2,1)S(1)} %collective-permute-done.23.refs_5_.refs_2_.refs_4_.refs_6_), channel_id=1, source_target_pairs={{0,1},{1,0},{2,3},{3,2},{4,5},{5,4},{6,7},{7,6},{8,9},{9,8},{10,11... | collective-permute-start | bytes 2211848 | tf_op jit(solution)/shard_map/ppermute | solution.py:1021
  113.5 16.2 %collective-permute-start.33 = (bf16[4,48,1536]{2,1,0:T(8,128)(2,1)S(1)}, bf16[4,48,1536]{2,1,0:T(8,128)(2,1)S(1)}, u32[]{:S(2)}, u32[]{:S(2)}) collective-permute-start(bf16[4,48,1536]{2,1,0:T(8,128)(2,1)S(1)} %arrange.5.refs_2_.refs_12_), channel_id=1, source_target_pairs={{0,2},{2,0},{4,6},{6,4},{8,10},{10,8},{12,14},{14,12},{16,18},{18,... | collective-permute-start | bytes 1769480 | tf_op jit(solution)/shard_map/ppermute | solution.py:1029
  129.9 15.8 %collective-permute-start.38 = (bf16[4,4,48,768]{3,2,1,0:T(8,128)(2,1)}, bf16[4,4,48,768]{3,2,1,0:T(8,128)(2,1)S(1)}, u32[]{:S(2)}, u32[]{:S(2)}) collective-permute-start(bf16[4,4,48,768]{3,2,1,0:T(8,128)(2,1)} %get-tuple-element.314), channel_id=1, source_target_pairs={{0,1},{1,0},{2,3},{3,2},{4,5},{5,4},{6,7},{7,6},{8,9},{9,8},{10,11... | collective-permute-start | bytes 3538952 | tf_op jit(solution)/shard_map/ppermute | solution.py:1021
  129.9 15.7 %collective-permute-start.35 = (bf16[4,48,1536]{2,1,0:T(8,128)(2,1)S(1)}, bf16[4,48,1536]{2,1,0:T(8,128)(2,1)S(1)}, u32[]{:S(2)}, u32[]{:S(2)}) collective-permute-start(bf16[4,48,1536]{2,1,0:T(8,128)(2,1)S(1)} %collective-permute-done.34.refs_4_.refs_14_), channel_id=1, source_target_pairs={{0,2},{2,0},{4,6},{6,4},{8,10},{10,8},{12,14},{14,12},{16,18},{18,... | collective-permute-start | bytes 1769480 | tf_op jit(solution)/shard_map/ppermute | solution.py:1029
  147.8 15.7 %collective-permute-start.41 = (bf16[4,4,48,768]{3,2,1,0:T(8,128)(2,1)S(1)}, bf16[4,4,48,768]{3,2,1,0:T(8,128)(2,1)S(1)}, u32[]{:S(2)}, u32[]{:S(2)}) collective-permute-start(bf16[4,4,48,768]{3,2,1,0:T(8,128)(2,1)S(1)} %copy-done.23), channel_id=1, source_target_pairs={{0,1},{1,0},{2,3},{3,2},{4,5},{5,4},{6,7},{7,6},{8,9},{9,8},{10,11... | collective-permute-start | bytes 3538952 | tf_op jit(solution)/shard_map/ppermute | solution.py:1021
  147.9 15.6 %collective-permute-start.40 = (bf16[2,4,48,768]{3,2,1,0:T(8,128)(2,1)S(1)}, bf16[2,4,48,768]{3,2,1,0:T(8,128)(2,1)S(1)}, u32[]{:S(2)}, u32[]{:S(2)}) collective-permute-start(bf16[2,4,48,768]{3,2,1,0:T(8,128)(2,1)S(1)} %get-tuple-element.328), channel_id=1, source_target_pairs={{0,2},{2,0},{4,6},{6,4},{8,10},{10,8},{12,14},{14,12},{16,18},{18,... | collective-permute-start | bytes 1769480 | tf_op jit(solution)/shard_map/ppermute | solution.py:1029
  163.9 20.8 %collective-permute-start.42 = (bf16[4,48,768]{2,1,0:T(8,128)(2,1)S(1)}, bf16[4,48,768]{2,1,0:T(8,128)(2,1)S(1)}, u32[]{:S(2)}, u32[]{:S(2)}) collective-permute-start(bf16[4,48,768]{2,1,0:T(8,128)(2,1)S(1)} %fusion), channel_id=1, source_target_pairs={{0,4},{2,6},{4,0},{6,2},{8,12},{10,14},{12,8},{14,10},{16,20},{18,... | collective-permute-start | bytes 884744 | tf_op jit(solution)/shard_map/ppermute | solution.py:1029
  165.4 19.6 %collective-permute-start.43 = (bf16[2,4,48,768]{3,2,1,0:T(8,128)(2,1)S(1)}, bf16[2,4,48,768]{3,2,1,0:T(8,128)(2,1)S(1)}, u32[]{:S(2)}, u32[]{:S(2)}) collective-permute-start(bf16[2,4,48,768]{3,2,1,0:T(8,128)(2,1)S(1)} %get-tuple-element.343), channel_id=1, source_target_pairs={{0,4},{2,6},{4,0},{6,2},{8,12},{10,14},{12,8},{14,10},{16,20},{18,... | collective-permute-start | bytes 1769480 | tf_op jit(solution)/shard_map/ppermute | solution.py:1029
  166.0 19.1 %collective-permute-start.44 = (bf16[4,4,48,768]{3,2,1,0:T(8,128)(2,1)S(1)}, bf16[4,4,48,768]{3,2,1,0:T(8,128)(2,1)S(1)}, u32[]{:S(2)}, u32[]{:S(2)}) collective-permute-start(bf16[4,4,48,768]{3,2,1,0:T(8,128)(2,1)S(1)} %copy-done.21), channel_id=1, source_target_pairs={{0,1},{1,0},{2,3},{3,2},{4,5},{5,4},{6,7},{7,6},{8,9},{9,8},{10,11... | collective-permute-start | bytes 3538952 | tf_op jit(solution)/shard_map/ppermute | solution.py:1021
  190.5 22.8 %collective-permute-start.46 = (bf16[4,48,768]{2,1,0:T(8,128)(2,1)S(1)}, bf16[4,48,768]{2,1,0:T(8,128)(2,1)S(1)}, u32[]{:S(2)}, u32[]{:S(2)}) collective-permute-start(bf16[4,48,768]{2,1,0:T(8,128)(2,1)S(1)} %fusion.1), channel_id=1, source_target_pairs={{0,2},{2,0},{4,6},{6,4},{8,10},{10,8},{12,14},{14,12},{16,18},{18,... | collective-permute-start | bytes 884744 | tf_op jit(solution)/shard_map/ppermute | solution.py:1029
  191.6 21.6 %collective-permute-start.47 = (bf16[2,4,48,768]{3,2,1,0:T(8,128)(2,1)S(1)}, bf16[2,4,48,768]{3,2,1,0:T(8,128)(2,1)S(1)}, u32[]{:S(2)}, u32[]{:S(2)}) collective-permute-start(bf16[2,4,48,768]{3,2,1,0:T(8,128)(2,1)S(1)} %get-tuple-element.361), channel_id=1, source_target_pairs={{0,2},{2,0},{4,6},{6,4},{8,10},{10,8},{12,14},{14,12},{16,18},{18,... | collective-permute-start | bytes 1769480 | tf_op jit(solution)/shard_map/ppermute | solution.py:1029
  192.6 20.7 %collective-permute-start.48 = (bf16[2,4,48,768]{3,2,1,0:T(8,128)(2,1)S(1)}, bf16[2,4,48,768]{3,2,1,0:T(8,128)(2,1)S(1)}, u32[]{:S(2)}, u32[]{:S(2)}) collective-permute-start(bf16[2,4,48,768]{3,2,1,0:T(8,128)(2,1)S(1)} %get-tuple-element.362), channel_id=1, source_target_pairs={{0,4},{2,6},{4,0},{6,2},{8,12},{10,14},{12,8},{14,10},{16,20},{18,... | collective-permute-start | bytes 1769480 | tf_op jit(solution)/shard_map/ppermute | solution.py:1029
  214.5 20.9 %collective-permute-start.52 = (bf16[4,4,48,768]{3,2,1,0:T(8,128)(2,1)S(1)}, bf16[4,4,48,768]{3,2,1,0:T(8,128)(2,1)S(1)}, u32[]{:S(2)}, u32[]{:S(2)}) collective-permute-start(bf16[4,4,48,768]{3,2,1,0:T(8,128)(2,1)S(1)} %copy-done.22), channel_id=1, source_target_pairs={{0,1},{1,0},{2,3},{3,2},{4,5},{5,4},{6,7},{7,6},{8,9},{9,8},{10,11... | collective-permute-start | bytes 3538952 | tf_op jit(solution)/shard_map/ppermute | solution.py:1021
  215.2 20.1 %collective-permute-start.49 = (bf16[4,48,768]{2,1,0:T(8,128)(2,1)S(1)}, bf16[4,48,768]{2,1,0:T(8,128)(2,1)S(1)}, u32[]{:S(2)}, u32[]{:S(2)}) collective-permute-start(bf16[4,48,768]{2,1,0:T(8,128)(2,1)S(1)} %get-tuple-element.376), channel_id=1, source_target_pairs={{0,4},{2,6},{4,0},{6,2},{8,12},{10,14},{12,8},{14,10},{16,20},{18,... | collective-permute-start | bytes 884744 | tf_op jit(solution)/shard_map/ppermute | solution.py:1029
  215.7 19.6 %collective-permute-start.50 = (bf16[4,48,768]{2,1,0:T(8,128)(2,1)S(1)}, bf16[4,48,768]{2,1,0:T(8,128)(2,1)S(1)}, u32[]{:S(2)}, u32[]{:S(2)}) collective-permute-start(bf16[4,48,768]{2,1,0:T(8,128)(2,1)S(1)} %get-tuple-element.377), channel_id=1, source_target_pairs={{0,2},{2,0},{4,6},{6,4},{8,10},{10,8},{12,14},{14,12},{16,18},{18,... | collective-permute-start | bytes 884744 | tf_op jit(solution)/shard_map/ppermute | solution.py:1029
  216.8 18.5 %collective-permute-start.51 = (bf16[512,768]{1,0:T(8,128)(2,1)S(1)}, bf16[512,768]{1,0:T(8,128)(2,1)S(1)}, u32[]{:S(2)}, u32[]{:S(2)}) collective-permute-start(bf16[512,768]{1,0:T(8,128)(2,1)S(1)} %get-tuple-element.378), channel_id=1, source_target_pairs={{0,1},{1,0},{2,3},{3,2},{4,5},{5,4},{6,7},{7,6},{8,9},{9,8},{10,11... | collective-permute-start | bytes 2359304 | tf_op jit(solution)/shard_map/ppermute | solution.py:1021
  236.1 23.3 %collective-permute-start.54 = (bf16[4,48,768]{2,1,0:T(8,128)(2,1)S(1)}, bf16[4,48,768]{2,1,0:T(8,128)(2,1)S(1)}, u32[]{:S(2)}, u32[]{:S(2)}) collective-permute-start(bf16[4,48,768]{2,1,0:T(8,128)(2,1)S(1)} %get-tuple-element.397), channel_id=1, source_target_pairs={{0,2},{2,0},{4,6},{6,4},{8,10},{10,8},{12,14},{14,12},{16,18},{18,... | collective-permute-start | bytes 884744 | tf_op jit(solution)/shard_map/ppermute | solution.py:1029
  237.1 22.3 %collective-permute-start.55 = (bf16[4,48,768]{2,1,0:T(8,128)(2,1)S(1)}, bf16[4,48,768]{2,1,0:T(8,128)(2,1)S(1)}, u32[]{:S(2)}, u32[]{:S(2)}) collective-permute-start(bf16[4,48,768]{2,1,0:T(8,128)(2,1)S(1)} %get-tuple-element.398), channel_id=1, source_target_pairs={{0,4},{2,6},{4,0},{6,2},{8,12},{10,14},{12,8},{14,10},{16,20},{18,... | collective-permute-start | bytes 884744 | tf_op jit(solution)/shard_map/ppermute | solution.py:1029
  238.6 20.8 %collective-permute-start.56 = (bf16[4,48,768]{2,1,0:T(8,128)(2,1)S(1)}, bf16[4,48,768]{2,1,0:T(8,128)(2,1)S(1)}, u32[]{:S(2)}, u32[]{:S(2)}) collective-permute-start(bf16[4,48,768]{2,1,0:T(8,128)(2,1)S(1)} %get-tuple-element.399), channel_id=1, source_target_pairs={{0,6},{2,4},{4,2},{6,0},{8,14},{10,12},{12,10},{14,8},{16,22},{18,... | collective-permute-start | bytes 884744 | tf_op jit(solution)/shard_map/ppermute | solution.py:1029
  239.7 19.8 %collective-permute-start.53 = (bf16[2,48,3072]{2,1,0:T(8,128)(2,1)S(1)}, bf16[2,48,3072]{2,1,0:T(8,128)(2,1)S(1)}, u32[]{:S(2)}, u32[]{:S(2)}) collective-permute-start(bf16[2,48,3072]{2,1,0:T(8,128)(2,1)S(1)} %get-tuple-element.396), channel_id=1, source_target_pairs={{0,8},{2,10},{4,12},{6,14},{8,0},{10,2},{12,4},{14,6},{16,24},{18,... | collective-permute-start | bytes 1769480 | tf_op jit(solution)/shard_map/ppermute | solution.py:1029
  263.6 16.0 %collective-permute-start.59 = (bf16[48,3072]{1,0:T(8,128)(2,1)S(1)}, bf16[48,3072]{1,0:T(8,128)(2,1)S(1)}, u32[]{:S(2)}, u32[]{:S(2)}) collective-permute-start(bf16[48,3072]{1,0:T(8,128)(2,1)S(1)} %fusion.7), channel_id=1, source_target_pairs={{0,16},{2,18},{4,20},{6,22},{8,24},{10,26},{12,28},{14,30},{16,0},... | collective-permute-start | bytes 884744 | tf_op jit(solution)/shard_map/ppermute | solution.py:1029
  282.7 17.9 %collective-permute-start.64 = (f32[512,768]{1,0:T(8,128)S(1)}, f32[512,768]{1,0:T(8,128)S(1)}, u32[]{:S(2)}, u32[]{:S(2)}) collective-permute-start(f32[512,768]{1,0:T(8,128)S(1)} %get-tuple-element.427), channel_id=1, source_target_pairs={{0,1},{1,0},{2,3},{3,2},{4,5},{5,4},{6,7},{7,6},{8,9},{9,8},{10,11... | collective-permute-start | bytes 4718600 | tf_op jit(solution)/shard_map/ppermute | solution.py:1021
  (88 other events, 658.6 us)
